TPU v7x, 256 devices: a whole 4x4x8 slice. The times are simulated.
256 devices in a mesh: replica: 32 (over x, z), shard: 8 (over y, core).
Axes of the slice: x: 4, y: 4, z: 8, core: 2. Of those that a mesh axis runs over, the one named last changes fastest.
Arguments:
- local_params: bfloat16 [32, 2048, 8192], P('replica', 'shard'), may hold values from -6 to 6
- shared_base: bfloat16 [2048, 8192], P('shard'), may hold values from -6 to 6
- momentum: float32 [2048, 8192], P('shard', 'replica'), may hold values from -6 to 6
Outputs:
- new_fragment: bfloat16 [2048, 8192], P('shard')
- new_momentum: float32 [2048, 8192], P('shard', 'replica')
All inputs are finite; a program needn't handle non-finite values.
Results may differ from a plain program's by a relative error of at most 0.009.
Values may be sent and summed in bfloat16 or wider, within the bound.
No kernel may reach another device: no remote copies, remote signals or barrier semaphores. Data moves between devices by JAX's collectives and lax.ppermute only.
A program may use at most 128 MiB of HBM per device.

v0:
```python
import jax
import jax.numpy as jnp
from jax import lax
from jax.sharding import PartitionSpec as P

epsilon = 1e-06
outer_rate = 0.7
momentum_decay = 0.9
level_limit = 7.0
scale_factor = 2.0 / 7.0


def hadamard_pair():
    index = jnp.arange(64, dtype=jnp.int32)
    parity = jnp.zeros((64, 64), jnp.int32)
    for bit_number in range(6):
        parity = parity + (index[:, None] >> bit_number & index[None, :] >> bit_number & 1)
    signs = (1 - 2 * (parity % 2)).astype(jnp.float32)
    return jnp.kron(jnp.eye(2, dtype=jnp.float32), signs)


def rotate(values, table):
    flat = values.reshape(-1, 128)
    turned = (
        jnp.dot(flat, table, precision=lax.Precision.HIGHEST, preferred_element_type=jnp.float32)
        / 8.0
    )
    return turned.reshape(values.shape)


def compress(values):
    blocks = values.reshape(values.shape[0], -1, 64)
    scales = scale_factor * jnp.sqrt(jnp.mean(blocks * blocks, axis=-1) + epsilon)
    levels = jnp.clip(blocks / scales[..., None], -level_limit, level_limit).astype(jnp.bfloat16)
    return (levels.reshape(values.shape), scales)


def expand(levels, scales):
    blocks = levels.astype(jnp.float32).reshape(levels.shape[0], -1, 64)
    return (blocks * scales[..., None]).reshape(levels.shape)


def shards(local_params, shared_base, momentum):
    table = hadamard_pair()
    replica_count = lax.axis_size("replica")
    owner_index = lax.axis_index("replica")
    owned_width = momentum.shape[1]
    base_float = shared_base.astype(jnp.float32)
    pseudo_grad = base_float - local_params[0].astype(jnp.float32)
    levels, scales = compress(rotate(pseudo_grad, table))
    summed = lax.psum_scatter(expand(levels, scales), "replica", scatter_dimension=1, tiled=True)
    outer_grad = rotate(summed / float(replica_count), table)
    new_momentum = momentum_decay * momentum + outer_grad
    base_owned = lax.dynamic_slice_in_dim(base_float, owner_index * owned_width, owned_width, 1)
    updated = base_owned - outer_rate * (outer_grad + momentum_decay * new_momentum)
    new_fragment = lax.all_gather(updated.astype(jnp.bfloat16), "replica", axis=1, tiled=True)
    return (new_fragment, new_momentum)


def solution(mesh):
    in_specs = (P("replica", "shard", None), P("shard", None), P("shard", "replica"))
    out_specs = (P("shard", None), P("shard", "replica"))
    return jax.shard_map(shards, mesh=mesh, in_specs=in_specs, out_specs=out_specs, check_vma=False)
```

profile of v0, /device:TPU:16, one launch (start us, length us, event | category | flops | bytes accessed | tf_op | source)
XLA Modules:
  0.0 418.4 jit_solution(17356564957048337343)
XLA Ops:
  7.2 0.0 reduce-scatter.2.cloned.1.call-start
  7.3 8.1 %convert_subtract_fusion = f32[256,8192]{1,0:T(8,128)} fusion(bf16[1,256,8192]{2,1,0:T(8,128)(2,1)} %param.3, bf16[256,8192]{1,0:T(8,128)(2,1)} %param.4), kind=kLoop, calls=%fused_computation.5 | loop fusion | flops 6291456 | bytes 16777216 | tf_op jit(solution)/shard_map/sub | solution.py:49
  15.4 9.3 %reshape.298 = f32[16384,128]{1,0:T(8,128)} reshape(f32[256,8192]{1,0:T(8,128)} %convert_subtract_fusion) | data formatting | bytes 16777216 | tf_op jit(solution)/shard_map/reshape | solution.py:23
  24.7 0.1 fusion.5
  24.8 0.1 broadcast_multiply_fusion.1
  24.9 0.1 mul.95
  25.1 17.7 %fusion.6 = (f32[16384,128]{1,0:T(8,128)}, f32[16384,128]{1,0:T(8,128)}) fusion(f32[16384,128]{1,0:T(8,128)} %reshape.298, f32[128,128]{1,0:T(8,128)S(1)} %mul.95), kind=kOutput, calls=%fused_computation.26 | convolution fusion | flops 3225419776 | bytes 25231360 | tf_op jit(solution)/shard_map/dot_general | solution.py:25
  42.8 9.4 %reshape_reshape.3 = f32[256,8192]{1,0:T(8,128)} reshape(f32[16384,128]{1,0:T(8,128)} %get-tuple-element.5) | data formatting | bytes 16777216 | tf_op jit(solution)/shard_map/reshape;reshape | solution.py:32
  52.2 9.0 %copy.9 = f32[256,8192]{0,1:T(8,128)} copy(f32[256,8192]{1,0:T(8,128)} %reshape_reshape.3) | data formatting | bytes 16777216 | tf_op jit(solution)/shard_map/reshape;reshape | solution.py:32
  61.1 12.8 %mul.97 = f32[256,128,64]{2,1,0:T(8,128)} reshape(f32[16384,128]{1,0:T(8,128)} %get-tuple-element.4) | data formatting | bytes 16777216 | tf_op jit(solution)/shard_map/mul | solution.py:33
  73.9 8.2 %reduce_sum.9 = f32[256,128]{1,0:T(8,128)S(1)} reduce(f32[256,128,64]{2,1,0:T(8,128)} %mul.97, f32[]{:T(128)} %constant.32.clone.1), dimensions={2}, to_apply=%region_0.1 | reduce | flops 2064384 | bytes 8519684 | tf_op jit(solution)/shard_map/reduce_sum | solution.py:33
  82.2 0.1 copy.8
  82.3 7.6 %bitcast_multiply_fusion = f32[256,8192]{0,1:T(8,128)} fusion(f32[256,8192]{0,1:T(8,128)} %copy.9, f32[256,128]{0,1:T(8,128)S(1)} %copy.8), kind=kLoop, calls=%fused_computation.1 | loop fusion | flops 10485760 | bytes 16908288 | tf_op jit(solution)/shard_map/mul | solution.py:40
  89.8 0.0 reduce-scatter.2.cloned.1.call-update
  89.9 0.0 copy-start
  89.9 0.0 all-gather.2.cloned.1.call-start
  89.9 6.4 %convert_element_type.41 = f32[256,8192]{1,0:T(8,128)} convert(bf16[256,8192]{1,0:T(8,128)(2,1)} %param.4) | non-fusion elementwise | flops 2097152 | bytes 12582912 | tf_op jit(solution)/shard_map/convert_element_type | solution.py:48
  96.4 225.5 %reduce-scatter.2.cloned.1.call-done = f32[256,256]{0,1:T(8,128)} async-done(((f32[256,8192]{0,1:T(8,128)}), f32[256,256]{0,1:T(8,128)}) %reduce-scatter.2.cloned.1.call-update) | async-done | bytes 262160 | tf_op jit(solution)/shard_map/reduce_scatter | solution.py:51
  321.8 1.0 broadcast_multiply_fusion
  322.8 0.1 copy.10
  323.0 0.4 convolution_multiply_fusion.1
  323.3 0.1 reshape.300
  323.4 0.0 copy-done
  323.4 1.8 subtract_convert_fusion
  325.2 0.0 all-gather.2.cloned.1.call-update
  325.2 81.7 %all-gather.2.cloned.1.call-done = bf16[256,8192]{1,0:T(8,128)(2,1)} async-done(((bf16[256,256]{1,0:T(8,128)(2,1)}), bf16[256,8192]{1,0:T(8,128)(2,1)}) %all-gather.2.cloned.1.call-update) | async-done | bytes 4194320 | tf_op jit(solution)/shard_map/all_gather | solution.py:56
  406.9 4.6 %copy.12 = bf16[256,8192]{1,0:T(8,128)(2,1)} copy(bf16[256,8192]{1,0:T(8,128)(2,1)} %all-gather.2.cloned.1.call-done) | data formatting | bytes 8388608
  (6 shorter events, 0.1 us)
Async XLA Ops:
  7.2 314.7 %reduce-scatter.2.cloned.1.call-start = ((), (), s32[]{:S(2)}) async-start(), calls=%async_computation.1 | async-start | bytes 8650752 | tf_op jit(solution)/shard_map/reduce_scatter | solution.py:51
  89.9 233.6 %copy-start = (f32[256,256]{1,0:T(8,128)S(1)}, f32[256,256]{1,0:T(8,128)}, u32[]{:S(2)}) copy-start(f32[256,256]{1,0:T(8,128)} %param.5) | copy-start | bytes 786436
  89.9 317.0 %all-gather.2.cloned.1.call-start = ((), (), s32[]{:S(2)}) async-start(), calls=%async_computation.2 | async-start | bytes 4325376 | tf_op jit(solution)/shard_map/all_gather | solution.py:56
Sparse Core Ops, SparseCore 0:
  90.0 231.8 reduce-scatter.1
  325.3 81.5 all-gather.1
where the time goes:
time: 421 us; the launch traced here: 418 us
  waiting for transfers between devices  307 us (73%)
  local copies, waits for them, and re-layouts  45.5 us (11%)
  other arithmetic  33.4 us (8%)
  matrix products  18.1 us (4%)
  between operations  14.2 us (3%)
    reduce_scatter x1, waiting for transfers between devices, shards(): lax.psum_scatter(expand(levels, scales), 'replica', scatter_dimension=1,...  225 us
    all_gather x1, waiting for transfers between devices, shards(): lax.all_gather(updated.astype(jnp.bfloat16), 'replica', axis=1, tiled=True)  81.7 us
    another operation x2, local copies, waits for them, and re-layouts, compress(): blocks = values.reshape(values.shape[0], -1, 64)  18.4 us
    dot_general x2, matrix products, rotate(): jnp.dot(flat, table, precision=lax.Precision.HIGHEST, preferred_element_t...  18.1 us
    mul x1, local copies, waits for them, and re-layouts, compress(): blocks * blocks  12.8 us
    reshape x2, local copies, waits for them, and re-layouts, rotate(): flat = values.reshape(-1, 128)  9.3 us
  transfers between devices with their start and end apart: 2, of which 2 were waited for; matrix products, arithmetic and copies ran while one was open for 2% of the time, Pallas kernels for 0%

commit v1 on v0

v1 whole, which is shorter than its diff:
```python
import functools

import jax
import jax.numpy as jnp
import numpy as np
from jax import lax
from jax.experimental import pallas as pl
from jax.experimental.pallas import tpu as pltpu
from jax.sharding import PartitionSpec as P

epsilon = 1e-06
outer_rate = 0.7
momentum_decay = 0.9

NX, NZ = 4, 8
W = 256
ROWS_A = 144
ROWS_B = 112
BF, F32 = jnp.bfloat16, jnp.float32
VM = 48 * 2**20

Z_ORDER = (1, -2, 4, -1, 2, 0, 3, -3)
ANY = pl.BlockSpec(memory_space=pl.ANY)


def hadamard_blocks():
    index = np.arange(64)
    parity = np.zeros((64, 64), np.int64)
    for bit in range(6):
        parity += (index[:, None] >> bit) & (index[None, :] >> bit) & 1
    signs = (1 - 2 * (parity % 2)).astype(np.float32)
    return np.kron(np.eye(2, dtype=np.float32), signs) / 8.0


def params(**kw):
    return pltpu.CompilerParams(vmem_limit_bytes=VM, **kw)


def cost(flops, nbytes):
    return pl.CostEstimate(flops=flops, bytes_accessed=nbytes, transcendentals=0)


def position():
    replica = lax.axis_index("replica")
    return replica // NZ, lax.rem(replica, NZ)


def shift(value, dx, dz):
    pairs = [
        (x * NZ + z, (x + dx) % NX * NZ + (z + dz) % NZ) for x in range(NX) for z in range(NZ)
    ]
    return lax.ppermute(value, "replica", pairs)


def column_of(x, z, dx, dz):
    block = lax.rem(x + dx + NX, NX) * NZ + lax.rem(z + dz + NZ, NZ)
    return pl.multiple_of(block * W, W)


def contribute_kernel(row0, rows, slots, outs, place, local, base, turn, mean, *rest):
    out_refs = rest[: len(outs)]
    local_in, base_in, sent, in_sem, out_sem = rest[len(outs) :]
    x, z = place[0], place[1]

    def fetches(i, dx, dz):
        column = pl.ds(column_of(x, z, dx, dz), W)
        row = pl.ds(row0, rows)
        return (
            pltpu.make_async_copy(local.at[row, column], local_in.at[i], in_sem.at[0, i]),
            pltpu.make_async_copy(base.at[row, column], base_in.at[i], in_sem.at[1, i]),
        )

    for i, (dx, dz) in enumerate(slots):
        for copy in fetches(i, dx, dz):
            copy.start()
    first = 0
    for out, count in zip(out_refs, outs):

        def body(j, carry, out=out, first=first):
            i = first + j
            row = pl.ds(row0, rows)
            column = pl.ds(0, W)
            pltpu.make_async_copy(local.at[row, column], local_in.at[i], in_sem.at[0, i]).wait()
            pltpu.make_async_copy(base.at[row, column], base_in.at[i], in_sem.at[1, i]).wait()
            for half in range(2):
                lanes = pl.ds(half * 128, 128)
                pair = jnp.concatenate([base_in[i, :, lanes], local_in[i, :, lanes]], axis=1)
                rotated = jnp.dot(pair, turn[...], preferred_element_type=F32)
                square = rotated * rotated
                high = square.astype(BF)
                low = (square - high.astype(F32)).astype(BF)
                power = jnp.dot(
                    jnp.concatenate([high, low], axis=1), mean[...], preferred_element_type=F32
                )
                limit = 2.0 * jnp.sqrt(power + epsilon)
                sent[i, :, lanes] = jnp.clip(rotated, -limit, limit).astype(BF)
            target = out.at[:, pl.ds(pl.multiple_of(j * W, W), W)]
            pltpu.make_async_copy(sent.at[i], target, out_sem.at[i]).start()
            return carry

        lax.fori_loop(0, count, body, 0)
        first += count
    first = 0
    for out, count in zip(out_refs, outs):
        for j in range(count):
            target = out.at[:, pl.ds(j * W, W)]
            pltpu.make_async_copy(sent.at[first + j], target, out_sem.at[first + j]).wait()
        first += count


def contribute(row0, rows, slots, outs, place, local, base):
    table = hadamard_blocks()
    turn = jnp.asarray(np.concatenate([table, -table], axis=0), BF)
    ones = np.kron(np.eye(2, dtype=np.float32), np.ones((64, 64), np.float32)) / 64.0
    mean = jnp.asarray(np.concatenate([ones, ones], axis=0), BF)
    n = len(slots)
    return pl.pallas_call(
        functools.partial(contribute_kernel, row0, rows, slots, outs),
        out_shape=[jax.ShapeDtypeStruct((rows, count * W), BF) for count in outs],
        in_specs=[pl.BlockSpec(memory_space=pltpu.SMEM), ANY, ANY]
        + [pl.BlockSpec(memory_space=pltpu.VMEM)] * 2,
        out_specs=[ANY] * len(outs),
        scratch_shapes=[
            pltpu.VMEM((n, rows, W), BF),
            pltpu.VMEM((n, rows, W), BF),
            pltpu.VMEM((n, rows, W), BF),
            pltpu.SemaphoreType.DMA((2, n)),
            pltpu.SemaphoreType.DMA((n,)),
        ],
        compiler_params=params(),
        cost_estimate=cost(rows * 8192 * 1024, rows * 8192 * 6),
        name="contribute",
    )(place, local, base, turn, mean)


def call(kernel, outs, *args, nbytes=2**20, name=None):
    return pl.pallas_call(
        kernel,
        out_shape=[jax.ShapeDtypeStruct(s, d) for s, d in outs],
        in_specs=[pl.BlockSpec(memory_space=pltpu.VMEM)] * len(args),
        out_specs=[pl.BlockSpec(memory_space=pltpu.VMEM)] * len(outs),
        compiler_params=params(),
        cost_estimate=cost(nbytes, nbytes),
        name=name,
    )(*args)


def f(ref, start, size):
    return ref[:, pl.ds(start, size)].astype(F32)


def sum_x_kernel(a0, r1, r2, r3, plus, minus, keep0, keep3p, keep3m):
    for start, size, out in (
        (0, 640, plus),
        (640, 640, minus),
        (1280, 256, keep0),
        (1536, 256, keep3p),
        (1792, 256, keep3m),
    ):
        total = (f(a0, start, size) + f(r1, start, size)) + (f(r2, start, size) + f(r3, start, size))
        out[...] = total.astype(out.dtype)


def relay_kernel(w, keep3p, keep3m, from_minus, from_plus, to3p, to3m):
    h = w // 2
    to3p[:, pl.ds(0, h)] = (
        f(keep3p, 0, h) + f(from_plus, h + w, h) + f(from_minus, 2 * w, h)
    ).astype(BF)
    to3p[:, pl.ds(h, h)] = (f(keep3p, h, h) + f(from_plus, 2 * w, h)).astype(BF)
    to3m[:, pl.ds(0, h)] = (f(keep3m, 0, h) + f(from_minus, w, h)).astype(BF)
    to3m[:, pl.ds(h, h)] = (f(keep3m, h, h) + f(from_minus, w + h, h) + f(from_plus, 0, h)).astype(
        BF
    )


def near(w, keep0, from_minus, from_plus, r3p, r3m, start, size):
    return (f(keep0, start, size) + f(from_minus, start, size)) + (
        f(from_plus, w // 2 + start, size) + f(r3p, start, size) + f(r3m, start, size)
    )


def sum_z_kernel(keep0, from_minus, from_plus, r3p, r3m, own, s1, s2, s3):
    for k, out in enumerate((own, s1, s2, s3)):
        out[...] = near(NX * W, keep0, from_minus, from_plus, r3p, r3m, k * W, W).astype(out.dtype)


def update_kernel(
    place, keep0, from_minus, from_plus, r3p, r3m, own, b1, b2, b3, base, momentum, table,
    new_momentum, shard_a, shard_b, base_in, sem,
):
    columns = pl.ds(column_of(place[0], place[1], 0, 0), W)
    copy = pltpu.make_async_copy(base.at[:, columns], base_in, sem)
    copy.start()
    summed_a = near(W, keep0, from_minus, from_plus, r3p, r3m, 0, W)
    summed_b = (own[...] + b1[...].astype(F32)) + (b2[...].astype(F32) + b3[...].astype(F32))
    copy.wait()
    for row0, rows, summed, out in (
        (0, ROWS_A, summed_a, shard_a),
        (ROWS_A, ROWS_B, summed_b, shard_b),
    ):
        for half in range(2):
            lanes = pl.ds(half * 128, 128)
            row = pl.ds(row0, rows)
            outer_grad = jnp.dot(
                summed[:, half * 128 : half * 128 + 128] * (1.0 / 32.0),
                table[...],
                precision=lax.Precision.HIGHEST,
                preferred_element_type=F32,
            )
            moved = momentum_decay * momentum[row, lanes] + outer_grad
            new_momentum[row, lanes] = moved
            updated = base_in[row, lanes].astype(F32) - outer_rate * (
                outer_grad + momentum_decay * moved
            )
            out[:, lanes] = updated.astype(BF)


def update(place, base, momentum, *args):
    table = jnp.asarray(hadamard_blocks(), F32)
    vmem = pl.BlockSpec(memory_space=pltpu.VMEM)
    return pl.pallas_call(
        update_kernel,
        out_shape=[
            jax.ShapeDtypeStruct((ROWS_A + ROWS_B, W), F32),
            jax.ShapeDtypeStruct((ROWS_A, W), BF),
            jax.ShapeDtypeStruct((ROWS_B, W), BF),
        ],
        in_specs=[pl.BlockSpec(memory_space=pltpu.SMEM)] + [vmem] * 9 + [ANY] + [vmem] * 2,
        out_specs=[vmem] * 3,
        scratch_shapes=[pltpu.VMEM((ROWS_A + ROWS_B, W), BF), pltpu.SemaphoreType.DMA],
        compiler_params=params(),
        cost_estimate=cost(2**22, 2**20),
        name="update",
    )(place, *args, base, momentum, table)


def pieces_a():
    return (
        (0, 256, 0, 0), (256, 256, 3, 0), (512, 256, -3, 0), (768, 256, -1, 0), (1024, 256, 2, 0),
        (1280, 128, 4, 0), (1408, 256, 1, 0), (1664, 256, -2, 0), (1920, 128, 4, 128),
    )


def assemble_kernel(place, g0, g1, g2, g3, b0, b3p, b3m, bm, bp, out, sem):
    x, z = place[0], place[1]
    row_a, row_b = pl.ds(0, ROWS_A), pl.ds(ROWS_A, ROWS_B)
    copies = []

    def put(source, start, width, row, dx, dz, inner):
        block = lax.rem(x + dx + NX, NX) * NZ + lax.rem(z + dz + NZ, NZ)
        column = pl.ds(pl.multiple_of(block * W + inner, 128), width)
        k = len(copies)
        copy = pltpu.make_async_copy(source.at[:, pl.ds(start, width)], out.at[row, column], sem.at[k])
        copy.start()
        copies.append(copy)

    for e, block in enumerate((g0, g1, g2, g3)):
        for start, width, dz, inner in pieces_a():
            put(block, start, width, row_a, -e, dz, inner)
    for block, start, parts, dz, first in (
        (b0, 0, 4, 0, 0), (b3p, 0, 4, 3, 0), (b3m, 0, 4, -3, 0), (bm, 0, 4, -1, 0), (bm, 1024, 4, 2, 0),
        (bm, 2048, 2, 4, 0), (bp, 0, 4, 1, 0), (bp, 1024, 4, -2, 0), (bp, 2048, 2, 4, 2),
    ):
        for k in range(parts):
            put(block, start + k * W, W, row_b, -(first + k), dz, 0)
    for copy in copies:
        copy.wait()


def assemble(place, *blocks):
    return pl.pallas_call(
        assemble_kernel,
        out_shape=jax.ShapeDtypeStruct((ROWS_A + ROWS_B, NX * NZ * W), BF),
        in_specs=[pl.BlockSpec(memory_space=pltpu.SMEM)] + [ANY] * 9,
        out_specs=ANY,
        scratch_shapes=[pltpu.SemaphoreType.DMA((68,))],
        compiler_params=params(),
        cost_estimate=cost(0, 2**23),
        name="assemble",
    )(place, *blocks)


def shards(local_params, shared_base, momentum):
    x, z = position()
    place = jnp.stack([x, z]).astype(jnp.int32)
    local = local_params[0]
    slots_a = tuple((dx, dz) for dx in range(NX) for dz in Z_ORDER)
    slots_b = tuple((dx, dz) for dz in Z_ORDER for dx in range(NX))

    plus_b, minus_b, keep0_b, keep3p_b, keep3m_b = contribute(
        ROWS_A, ROWS_B, slots_b, (10, 10, 4, 4, 4), place, local, shared_base
    )
    a0, a1, a2, a3 = contribute(0, ROWS_A, slots_a, (8, 8, 8, 8), place, local, shared_base)
    from_minus_b, from_plus_b = shift(plus_b, 0, 1), shift(minus_b, 0, -1)
    r1, r2, r3 = shift(a1, 1, 0), shift(a2, 2, 0), shift(a3, 3, 0)

    half = (ROWS_B, NX * W)
    to3p, to3m = call(
        functools.partial(relay_kernel, NX * W), [(half, BF), (half, BF)],
        keep3p_b, keep3m_b, from_minus_b, from_plus_b, name="relay_b",
    )
    r3p, r3m = shift(to3p, 0, 3), shift(to3m, 0, -3)
    strip = (ROWS_B, W)
    own, s1, s2, s3 = call(
        sum_z_kernel, [(strip, F32), (strip, BF), (strip, BF), (strip, BF)],
        keep0_b, from_minus_b, from_plus_b, r3p, r3m, name="sum_b",
    )
    b1, b2, b3 = shift(s1, 1, 0), shift(s2, 2, 0), shift(s3, 3, 0)

    strip = (ROWS_A, W)
    group = (ROWS_A, 640)
    plus_a, minus_a, keep0, keep3p, keep3m = call(
        sum_x_kernel, [(group, BF), (group, BF), (strip, F32), (strip, F32), (strip, F32)],
        a0, r1, r2, r3, name="sum_a",
    )
    from_minus, from_plus = shift(plus_a, 0, 1), shift(minus_a, 0, -1)
    to3p, to3m = call(
        functools.partial(relay_kernel, W), [(strip, BF), (strip, BF)],
        keep3p, keep3m, from_minus, from_plus, name="relay_a",
    )
    r3p, r3m = shift(to3p, 0, 3), shift(to3m, 0, -3)

    new_momentum, own_a, own_b = update(
        place, shared_base, momentum, keep0, from_minus, from_plus, r3p, r3m, own, b1, b2, b3
    )

    p3, m3 = shift(own_a, 0, -3), shift(own_a, 0, 3)
    strips = [own_b] + [shift(own_b, e, 0) for e in (1, 2, 3)]
    from_minus = shift(jnp.concatenate([own_a, p3, m3[:, :128]], axis=1), 0, 1)
    from_plus = shift(jnp.concatenate([own_a, m3, p3[:, 128:]], axis=1), 0, -1)
    row_b = jnp.concatenate(strips, axis=1)
    p3_b, m3_b = shift(row_b, 0, -3), shift(row_b, 0, 3)
    from_minus_b = shift(jnp.concatenate([row_b, p3_b, m3_b[:, :512]], axis=1), 0, 1)
    from_plus_b = shift(jnp.concatenate([row_b, m3_b, p3_b[:, 512:]], axis=1), 0, -1)
    g0 = jnp.concatenate([own_a, p3, m3, from_minus, from_plus], axis=1)
    g1, g2, g3 = [shift(g0, e, 0) for e in (1, 2, 3)]
    new_fragment = assemble(
        place, g0, g1, g2, g3, row_b, p3_b, m3_b, from_minus_b, from_plus_b
    )
    return (new_fragment, new_momentum)


def solution(mesh):
    in_specs = (P("replica", "shard", None), P("shard", None), P("shard", "replica"))
    out_specs = (P("shard", None), P("shard", "replica"))
    return jax.shard_map(shards, mesh=mesh, in_specs=in_specs, out_specs=out_specs, check_vma=False)
```

time: 421 us -> 157 us (0.37)
  waiting for transfers between devices: 307 us -> 58.1 us
  starting transfers between devices: 0.08 us -> 59.2 us
  local copies, waits for them, and re-layouts: 45.5 us -> 4.1 us
  other arithmetic: 33.4 us -> 0.11 us
  Pallas kernels: 0 us -> 32.7 us
  matrix products: 18.1 us -> 0 us
  between operations: 14.2 us -> 1.04 us
    reduce_scatter x1 -> x0, waiting for transfers between devices: 225 us -> none  [shards(): lax.psum_scatter(expand(levels, scales), 'replica', scatter_dimension=1,...]
    all_gather x1 -> x0, waiting for transfers between devices: 81.7 us -> none  [shards(): lax.all_gather(updated.astype(jnp.bfloat16), 'replica', axis=1, tiled=True)]
    ppermute x0 -> x28, starting transfers between devices: none -> 59.2 us  [shift(): return lax.ppermute(value, 'replica', pairs)]
    ppermute x0 -> x28, waiting for transfers between devices: none -> 58.1 us  [shift(): return lax.ppermute(value, 'replica', pairs)]
    pallas_call x0 -> x8, Pallas kernels: none -> 32.7 us  [the longest x2 27.2 us: contribute(): pl.pallas_call(functools.partial(contribute_kernel, row0, rows, slots, ou...]
    another operation x2 -> x0, local copies, waits for them, and re-layouts: 18.4 us -> none  [compress(): blocks = values.reshape(values.shape[0], -1, 64)]
    dot_general x2 -> x0, matrix products: 18.1 us -> none  [rotate(): jnp.dot(flat, table, precision=lax.Precision.HIGHEST, preferred_element_t...]
    mul x3 -> x0, local copies, waits for them, and re-layouts: 13 us -> none  [the longest x1 12.8 us: compress(): blocks * blocks]
  transfers between devices with their start and end apart: 2 -> 28, of which waited for: 2 -> 12; matrix products, arithmetic and copies ran while one was open for 2% -> 0% of each run, Pallas kernels for 0% -> 9%
where the time goes in v1:
time: 157 us; the launch traced here: 155 us
  starting transfers between devices  59.2 us (38%)
  waiting for transfers between devices  58.1 us (37%)
  Pallas kernels  32.7 us (21%)
  local copies, waits for them, and re-layouts  4.1 us (3%)
    ppermute x28, starting transfers between devices, shift(): return lax.ppermute(value, 'replica', pairs)  59.2 us
    ppermute x28, waiting for transfers between devices, shift(): return lax.ppermute(value, 'replica', pairs)  58.1 us
    pallas_call x2, Pallas kernels, contribute(): pl.pallas_call(functools.partial(contribute_kernel, row0, rows, slots, ou...  27.2 us
    unnamed x27, local copies, waits for them, and re-layouts  4.04 us
  transfers between devices with their start and end apart: 28, of which 12 were waited for; matrix products, arithmetic and copies ran while one was open for 0% of the time, Pallas kernels for 9%

profile of v1, /device:TPU:16, one launch (start us, length us, event | category | flops | bytes accessed | tf_op | source)
XLA Modules:
  0.0 155.2 jit_solution(10366180443465495141)
XLA Ops:
  0.7 2.2 %copy-done.1 = bf16[1,256,8192]{2,1,0:T(8,128)(2,1)S(1)} copy-done((bf16[1,256,8192]{2,1,0:T(8,128)(2,1)S(1)}, bf16[1,256,8192]{2,1,0:T(8,128)(2,1)}, u32[]{:S(2)}) %copy-start.1) | copy-done | bytes 4194328
  2.9 0.8 copy-done.2
  3.8 0.8 copy-done.4
  4.6 13.2 %contribute.3 = (bf16[112,2560]{1,0:T(8,128)(2,1)S(1)}, bf16[112,2560]{1,0:T(8,128)(2,1)S(1)}, bf16[112,1024]{1,0:T(8,128)(2,1)S(1)}, bf16[112,1024]{1,0:T(8,128)(2,1)S(1)}, bf16[112,1024]{1,0:T(8,128)(2,1)S(1)}) custom-call(s32[2]{0:T(128)S(1)} %pad_add_fusion.place, bf16[256,8192]{1,0:T(8,128)(2,1)S(1)} %bitcast.4, bf16[256,8192]{1,0:T(8,128)(2,1)} %base.5, ...), custom_call_target="tpu_custom_call" | custom-call | flops 939524096 | bytes 5505024 | tf_op jit(solution)/shard_map/contribute/pallas_call | solution.py:117
  17.8 2.0 %collective-permute-start.7 = (bf16[112,2560]{1,0:T(8,128)(2,1)S(1)}, bf16[112,2560]{1,0:T(8,128)(2,1)S(1)}, u32[]{:S(2)}, u32[]{:S(2)}) collective-permute-start(bf16[112,2560]{1,0:T(8,128)(2,1)S(1)} %get-tuple-element.39), channel_id=1, source_target_pairs={{0,8},{8,16},{16,24},{24,32},{32,40},{40,48},{48,56},{56,0},{64,72... | collective-permute-start | bytes 1720328 | tf_op jit(solution)/shard_map/ppermute | solution.py:52
  19.8 4.0 %collective-permute-start.8 = (bf16[112,2560]{1,0:T(8,128)(2,1)S(1)}, bf16[112,2560]{1,0:T(8,128)(2,1)S(1)}, u32[]{:S(2)}, u32[]{:S(2)}) collective-permute-start(bf16[112,2560]{1,0:T(8,128)(2,1)S(1)} %get-tuple-element.40), channel_id=1, source_target_pairs={{0,56},{8,0},{16,8},{24,16},{32,24},{40,32},{48,40},{56,48},{64,12... | collective-permute-start | bytes 1720328 | tf_op jit(solution)/shard_map/ppermute | solution.py:52
  23.8 14.0 %contribute.2 = (bf16[144,2048]{1,0:T(8,128)(2,1)S(1)}, bf16[144,2048]{1,0:T(8,128)(2,1)S(1)}, bf16[144,2048]{1,0:T(8,128)(2,1)S(1)}, bf16[144,2048]{1,0:T(8,128)(2,1)S(1)}) custom-call(s32[2]{0:T(128)S(1)} %pad_add_fusion.place, bf16[256,8192]{1,0:T(8,128)(2,1)} %bitcast.3, bf16[256,8192]{1,0:T(8,128)(2,1)} %base.5, bf16[256,128]{1,0:T(8,128)(2,1)S(1)} %copy-done.5, ...), custom_call_target="tpu_custom_call" | custom-call | flops 1207959552 | bytes 7077888 | tf_op jit(solution)/shard_map/contribute/pallas_call | solution.py:117
  37.8 1.6 %collective-permute-start = (bf16[144,2048]{1,0:T(8,128)(2,1)S(1)}, bf16[144,2048]{1,0:T(8,128)(2,1)S(1)}, u32[]{:S(2)}, u32[]{:S(2)}) collective-permute-start(bf16[144,2048]{1,0:T(8,128)(2,1)S(1)} %get-tuple-element.28), channel_id=1, source_target_pairs={{0,64},{8,72},{16,80},{24,88},{32,96},{40,104},{48,112},{56,120},{... | collective-permute-start | bytes 1769480 | tf_op jit(solution)/shard_map/ppermute | solution.py:52
  39.4 2.7 %collective-permute-start.1 = (bf16[144,2048]{1,0:T(8,128)(2,1)S(1)}, bf16[144,2048]{1,0:T(8,128)(2,1)S(1)}, u32[]{:S(2)}, u32[]{:S(2)}) collective-permute-start(bf16[144,2048]{1,0:T(8,128)(2,1)S(1)} %get-tuple-element.29), channel_id=1, source_target_pairs={{0,128},{8,136},{16,144},{24,152},{32,160},{40,168},{48,176},{56,1... | collective-permute-start | bytes 1769480 | tf_op jit(solution)/shard_map/ppermute | solution.py:52
  42.1 1.4 collective-permute-start.2
  43.6 0.1 relay_b.1
  43.7 1.9 %collective-permute-start.9 = (bf16[112,1024]{1,0:T(8,128)(2,1)S(1)}, bf16[112,1024]{1,0:T(8,128)(2,1)S(1)}, u32[]{:S(2)}, u32[]{:S(2)}) collective-permute-start(bf16[112,1024]{1,0:T(8,128)(2,1)S(1)} %get-tuple-element.43), channel_id=1, source_target_pairs={{0,24},{8,32},{16,40},{24,48},{32,56},{40,0},{48,8},{56,16},{64,88... | collective-permute-start | bytes 688136 | tf_op jit(solution)/shard_map/ppermute | solution.py:52
  45.6 3.2 %collective-permute-start.10 = (bf16[112,1024]{1,0:T(8,128)(2,1)S(1)}, bf16[112,1024]{1,0:T(8,128)(2,1)S(1)}, u32[]{:S(2)}, u32[]{:S(2)}) collective-permute-start(bf16[112,1024]{1,0:T(8,128)(2,1)S(1)} %get-tuple-element.44), channel_id=1, source_target_pairs={{0,40},{8,48},{16,56},{24,0},{32,8},{40,16},{48,24},{56,32},{64,10... | collective-permute-start | bytes 688136 | tf_op jit(solution)/shard_map/ppermute | solution.py:52
  48.8 5.6 %collective-permute-done.r1 = bf16[144,2048]{1,0:T(8,128)(2,1)S(1)} collective-permute-done((bf16[144,2048]{1,0:T(8,128)(2,1)S(1)}, bf16[144,2048]{1,0:T(8,128)(2,1)S(1)}, u32[]{:S(2)}, u32[]{:S(2)}) %collective-permute-start) | collective-permute-done | bytes 589856 | tf_op jit(solution)/shard_map/ppermute | solution.py:52
  54.4 13.1 %collective-permute-done.1.r2 = bf16[144,2048]{1,0:T(8,128)(2,1)S(1)} collective-permute-done((bf16[144,2048]{1,0:T(8,128)(2,1)S(1)}, bf16[144,2048]{1,0:T(8,128)(2,1)S(1)}, u32[]{:S(2)}, u32[]{:S(2)}) %collective-permute-start.1) | collective-permute-done | bytes 589856 | tf_op jit(solution)/shard_map/ppermute | solution.py:52
  67.5 0.3 sum_a.1
  67.8 0.1 collective-permute-start.3
  67.9 3.2 %collective-permute-start.4 = (bf16[144,640]{1,0:T(8,128)(2,1)S(1)}, bf16[144,640]{1,0:T(8,128)(2,1)S(1)}, u32[]{:S(2)}, u32[]{:S(2)}) collective-permute-start(bf16[144,640]{1,0:T(8,128)(2,1)S(1)} %get-tuple-element.33), channel_id=1, source_target_pairs={{0,56},{8,0},{16,8},{24,16},{32,24},{40,32},{48,40},{56,48},{64,12... | collective-permute-start | bytes 552968 | tf_op jit(solution)/shard_map/ppermute | solution.py:52
  71.1 3.5 %collective-permute-done.3.from_minus = bf16[144,640]{1,0:T(8,128)(2,1)S(1)} collective-permute-done((bf16[144,640]{1,0:T(8,128)(2,1)S(1)}, bf16[144,640]{1,0:T(8,128)(2,1)S(1)}, u32[]{:S(2)}, u32[]{:S(2)}) %collective-permute-start.3) | collective-permute-done | bytes 184352 | tf_op jit(solution)/shard_map/ppermute | solution.py:52
  74.7 4.8 %collective-permute-start.5 = (bf16[144,256]{1,0:T(8,128)(2,1)S(1)}, bf16[144,256]{1,0:T(8,128)(2,1)S(1)}, u32[]{:S(2)}, u32[]{:S(2)}) collective-permute-start(bf16[144,256]{1,0:T(8,128)(2,1)S(1)} %get-tuple-element.36), channel_id=1, source_target_pairs={{0,24},{8,32},{16,40},{24,48},{32,56},{40,0},{48,8},{56,16},{64,88... | collective-permute-start | bytes 221192 | tf_op jit(solution)/shard_map/ppermute | solution.py:52
  79.6 0.3 collective-permute-start.6
  79.8 0.2 sum_b.1
  80.0 1.9 %collective-permute-start.11 = (bf16[112,256]{1,0:T(8,128)(2,1)S(1)}, bf16[112,256]{1,0:T(8,128)(2,1)S(1)}, u32[]{:S(2)}, u32[]{:S(2)}) collective-permute-start(bf16[112,256]{1,0:T(8,128)(2,1)S(1)} %get-tuple-element.46), channel_id=1, source_target_pairs={{0,64},{8,72},{16,80},{24,88},{32,96},{40,104},{48,112},{56,120},{... | collective-permute-start | bytes 172040 | tf_op jit(solution)/shard_map/ppermute | solution.py:52
  81.9 3.1 %collective-permute-start.12 = (bf16[112,256]{1,0:T(8,128)(2,1)S(1)}, bf16[112,256]{1,0:T(8,128)(2,1)S(1)}, u32[]{:S(2)}, u32[]{:S(2)}) collective-permute-start(bf16[112,256]{1,0:T(8,128)(2,1)S(1)} %get-tuple-element.47), channel_id=1, source_target_pairs={{0,128},{8,136},{16,144},{24,152},{32,160},{40,168},{48,176},{56,1... | collective-permute-start | bytes 172040 | tf_op jit(solution)/shard_map/ppermute | solution.py:52
  85.0 0.5 collective-permute-start.13
  85.5 0.8 collective-permute-done.6.r3m
  86.4 1.4 collective-permute-done.12.b2
  87.8 1.4 collective-permute-done.13.b3
  89.2 1.8 %update.1 = (f32[256,256]{1,0:T(8,128)}, bf16[144,256]{1,0:T(8,128)(2,1)S(1)}, bf16[112,256]{1,0:T(8,128)(2,1)S(1)}) custom-call(s32[2]{0:T(128)S(1)} %pad_add_fusion.place, f32[144,256]{1,0:T(8,128)S(1)} %get-tuple-element.31.keep0, bf16[144,640]{1,0:T(8,128)(2,1)S(1)} %collective-permute-done.3.from_minus, ...), custom_call_target="tpu_custom_call" | custom-call | flops 4194304 | bytes 1048576 | tf_op jit(solution)/shard_map/update/pallas_call | solution.py:221
  91.0 1.8 %collective-permute-start.23 = (bf16[112,256]{1,0:T(8,128)(2,1)S(1)}, bf16[112,256]{1,0:T(8,128)(2,1)S(1)}, u32[]{:S(2)}, u32[]{:S(2)}) collective-permute-start(bf16[112,256]{1,0:T(8,128)(2,1)S(1)} %get-tuple-element.50), channel_id=1, source_target_pairs={{0,192},{8,200},{16,208},{24,216},{32,224},{40,232},{48,240},{56,2... | collective-permute-start | bytes 172040 | tf_op jit(solution)/shard_map/ppermute | solution.py:52
  92.8 0.3 collective-permute-start.22
  93.1 0.9 collective-permute-start.21
  94.0 3.3 %collective-permute-start.15 = (bf16[144,256]{1,0:T(8,128)(2,1)S(1)}, bf16[144,256]{1,0:T(8,128)(2,1)S(1)}, u32[]{:S(2)}, u32[]{:S(2)}) collective-permute-start(bf16[144,256]{1,0:T(8,128)(2,1)S(1)} %get-tuple-element.49), channel_id=1, source_target_pairs={{0,24},{8,32},{16,40},{24,48},{32,56},{40,0},{48,8},{56,16},{64,88... | collective-permute-start | bytes 221192 | tf_op jit(solution)/shard_map/ppermute | solution.py:52
  97.3 1.7 %collective-permute-start.14 = (bf16[144,256]{1,0:T(8,128)(2,1)S(1)}, bf16[144,256]{1,0:T(8,128)(2,1)S(1)}, u32[]{:S(2)}, u32[]{:S(2)}) collective-permute-start(bf16[144,256]{1,0:T(8,128)(2,1)S(1)} %get-tuple-element.49), channel_id=1, source_target_pairs={{0,40},{8,48},{16,56},{24,0},{32,8},{40,16},{48,24},{56,32},{64,10... | collective-permute-start | bytes 221192 | tf_op jit(solution)/shard_map/ppermute | solution.py:52
  99.2 3.6 %collective-permute-start.25 = (bf16[112,1024]{1,0:T(8,128)(2,1)S(1)}, bf16[112,1024]{1,0:T(8,128)(2,1)S(1)}, u32[]{:S(2)}, u32[]{:S(2)}) collective-permute-start(bf16[112,1024]{1,0:T(8,128)(2,1)S(1)} %get-tuple-element.55.b0), channel_id=1, source_target_pairs={{0,24},{8,32},{16,40},{24,48},{32,56},{40,0},{48,8},{56,16},{64,88... | collective-permute-start | bytes 688136 | tf_op jit(solution)/shard_map/ppermute | solution.py:52
  102.8 1.5 collective-permute-start.24
  104.3 0.1 collective-permute-done.14
  104.5 6.2 %collective-permute-start.17 = (bf16[144,640]{1,0:T(8,128)(2,1)S(1)}, bf16[144,640]{1,0:T(8,128)(2,1)S(1)}, u32[]{:S(2)}, u32[]{:S(2)}) collective-permute-start(bf16[144,640]{1,0:T(8,128)(2,1)S(1)} %get-tuple-element.52), channel_id=1, source_target_pairs={{0,56},{8,0},{16,8},{24,16},{32,24},{40,32},{48,40},{56,48},{64,12... | collective-permute-start | bytes 552968 | tf_op jit(solution)/shard_map/ppermute | solution.py:52
  110.7 2.0 %collective-permute-start.16 = (bf16[144,640]{1,0:T(8,128)(2,1)S(1)}, bf16[144,640]{1,0:T(8,128)(2,1)S(1)}, u32[]{:S(2)}, u32[]{:S(2)}) collective-permute-start(bf16[144,640]{1,0:T(8,128)(2,1)S(1)} %get-tuple-element.53), channel_id=1, source_target_pairs={{0,8},{8,16},{16,24},{24,32},{32,40},{40,48},{48,56},{56,0},{64,72... | collective-permute-start | bytes 552968 | tf_op jit(solution)/shard_map/ppermute | solution.py:52
  112.7 7.9 %collective-permute-done.16 = bf16[144,640]{1,0:T(8,128)(2,1)S(1)} collective-permute-done((bf16[144,640]{1,0:T(8,128)(2,1)S(1)}, bf16[144,640]{1,0:T(8,128)(2,1)S(1)}, u32[]{:S(2)}, u32[]{:S(2)}) %collective-permute-start.16) | collective-permute-done | bytes 184352 | tf_op jit(solution)/shard_map/ppermute | solution.py:52
  120.6 1.3 collective-permute-done.17
  121.9 2.3 %collective-permute-start.20 = (bf16[144,2048]{1,0:T(8,128)(2,1)S(1)}, bf16[144,2048]{1,0:T(8,128)(2,1)S(1)}, u32[]{:S(2)}, u32[]{:S(2)}) collective-permute-start(bf16[144,2048]{1,0:T(8,128)(2,1)S(1)} %constant_dynamic-update-slice_fusion.g0), channel_id=1, source_target_pairs={{0,192},{8,200},{16,208},{24,216},{32,224},{40,232},{48,240},{56,2... | collective-permute-start | bytes 1769480 | tf_op jit(solution)/shard_map/ppermute | solution.py:52
  124.2 1.7 %collective-permute-start.19 = (bf16[144,2048]{1,0:T(8,128)(2,1)S(1)}, bf16[144,2048]{1,0:T(8,128)(2,1)S(1)}, u32[]{:S(2)}, u32[]{:S(2)}) collective-permute-start(bf16[144,2048]{1,0:T(8,128)(2,1)S(1)} %constant_dynamic-update-slice_fusion.g0), channel_id=1, source_target_pairs={{0,128},{8,136},{16,144},{24,152},{32,160},{40,168},{48,176},{56,1... | collective-permute-start | bytes 1769480 | tf_op jit(solution)/shard_map/ppermute | solution.py:52
  126.0 0.1 collective-permute-start.18
  126.2 2.8 %collective-permute-start.27 = (bf16[112,2560]{1,0:T(8,128)(2,1)S(1)}, bf16[112,2560]{1,0:T(8,128)(2,1)S(1)}, u32[]{:S(2)}, u32[]{:S(2)}) collective-permute-start(bf16[112,2560]{1,0:T(8,128)(2,1)S(1)} %slice_dynamic-update-slice_fusion), channel_id=1, source_target_pairs={{0,56},{8,0},{16,8},{24,16},{32,24},{40,32},{48,40},{56,48},{64,12... | collective-permute-start | bytes 1720328 | tf_op jit(solution)/shard_map/ppermute | solution.py:52
  129.1 19.2 %collective-permute-done.20.g3 = bf16[144,2048]{1,0:T(8,128)(2,1)S(1)} collective-permute-done((bf16[144,2048]{1,0:T(8,128)(2,1)S(1)}, bf16[144,2048]{1,0:T(8,128)(2,1)S(1)}, u32[]{:S(2)}, u32[]{:S(2)}) %collective-permute-start.20) | collective-permute-done | bytes 589856 | tf_op jit(solution)/shard_map/ppermute | solution.py:52
  148.2 3.7 %collective-permute-done.18.g1 = bf16[144,2048]{1,0:T(8,128)(2,1)S(1)} collective-permute-done((bf16[144,2048]{1,0:T(8,128)(2,1)S(1)}, bf16[144,2048]{1,0:T(8,128)(2,1)S(1)}, u32[]{:S(2)}, u32[]{:S(2)}) %collective-permute-start.18) | collective-permute-done | bytes 589856 | tf_op jit(solution)/shard_map/ppermute | solution.py:52
  151.9 3.1 %assemble.1 = bf16[256,8192]{1,0:T(8,128)(2,1)} custom-call(s32[2]{0:T(128)S(1)} %pad_add_fusion.place, bf16[144,2048]{1,0:T(8,128)(2,1)S(1)} %constant_dynamic-update-slice_fusion.g0, bf16[144,2048]{1,0:T(8,128)(2,1)S(1)} %collective-permute-done.18.g1, bf16[144,2048]{1,0:T(8,128)(2,1)S(1)} %collective-permute-done.19.g2, ...), custom_call_target="tpu_custom_call" | custom-call | bytes 8388608 | tf_op jit(solution)/shard_map/assemble/pallas_call | solution.py:271
  (50 shorter events, 0.6 us)
Async XLA Ops:
  0.7 2.2 %copy-start.1 = (bf16[1,256,8192]{2,1,0:T(8,128)(2,1)S(1)}, bf16[1,256,8192]{2,1,0:T(8,128)(2,1)}, u32[]{:S(2)}) copy-start(bf16[1,256,8192]{2,1,0:T(8,128)(2,1)} %param.8) | copy-start | bytes 12582916
  2.9 0.8 copy-start.2
  3.7 0.8 copy-start.4
  4.6 19.2 %copy-start.3 = (bf16[256,128]{1,0:T(8,128)(2,1)S(1)}, bf16[256,128]{1,0:T(8,128)(2,1)}, u32[]{:S(2)}) copy-start(bf16[256,128]{1,0:T(8,128)(2,1)} %constant.29.clone.mean) | copy-start | bytes 196612
  4.6 19.2 %copy-start.5 = (bf16[256,128]{1,0:T(8,128)(2,1)S(1)}, bf16[256,128]{1,0:T(8,128)(2,1)}, u32[]{:S(2)}) copy-start(bf16[256,128]{1,0:T(8,128)(2,1)} %constant.28.clone.turn) | copy-start | bytes 196612
  17.8 25.8 %collective-permute-start.7 = (bf16[112,2560]{1,0:T(8,128)(2,1)S(1)}, bf16[112,2560]{1,0:T(8,128)(2,1)S(1)}, u32[]{:S(2)}, u32[]{:S(2)}) collective-permute-start(bf16[112,2560]{1,0:T(8,128)(2,1)S(1)} %get-tuple-element.39), channel_id=1, source_target_pairs={{0,8},{8,16},{16,24},{24,32},{32,40},{40,48},{48,56},{56,0},{64,72... | collective-permute-start | bytes 1720328 | tf_op jit(solution)/shard_map/ppermute | solution.py:52
  19.8 23.8 %collective-permute-start.8 = (bf16[112,2560]{1,0:T(8,128)(2,1)S(1)}, bf16[112,2560]{1,0:T(8,128)(2,1)S(1)}, u32[]{:S(2)}, u32[]{:S(2)}) collective-permute-start(bf16[112,2560]{1,0:T(8,128)(2,1)S(1)} %get-tuple-element.40), channel_id=1, source_target_pairs={{0,56},{8,0},{16,8},{24,16},{32,24},{40,32},{48,40},{56,48},{64,12... | collective-permute-start | bytes 1720328 | tf_op jit(solution)/shard_map/ppermute | solution.py:52
  37.8 51.4 %copy-start = (bf16[256,8192]{1,0:T(8,128)(2,1)S(1)}, bf16[256,8192]{1,0:T(8,128)(2,1)}, u32[]{:S(2)}) copy-start(bf16[256,8192]{1,0:T(8,128)(2,1)} %base.5) | copy-start | bytes 12582916
  37.8 51.4 %copy-start.6 = (f32[256,256]{1,0:T(8,128)S(1)}, f32[256,256]{1,0:T(8,128)}, u32[]{:S(2)}) copy-start(f32[256,256]{1,0:T(8,128)} %momentum.1) | copy-start | bytes 786436
  37.8 51.4 %copy-start.7 = (f32[128,128]{1,0:T(8,128)S(1)}, f32[128,128]{1,0:T(8,128)}, u32[]{:S(2)}) copy-start(f32[128,128]{1,0:T(8,128)} %constant.30.clone.table) | copy-start | bytes 196612
  37.8 16.6 %collective-permute-start = (bf16[144,2048]{1,0:T(8,128)(2,1)S(1)}, bf16[144,2048]{1,0:T(8,128)(2,1)S(1)}, u32[]{:S(2)}, u32[]{:S(2)}) collective-permute-start(bf16[144,2048]{1,0:T(8,128)(2,1)S(1)} %get-tuple-element.28), channel_id=1, source_target_pairs={{0,64},{8,72},{16,80},{24,88},{32,96},{40,104},{48,112},{56,120},{... | collective-permute-start | bytes 1769480 | tf_op jit(solution)/shard_map/ppermute | solution.py:52
  39.4 28.1 %collective-permute-start.1 = (bf16[144,2048]{1,0:T(8,128)(2,1)S(1)}, bf16[144,2048]{1,0:T(8,128)(2,1)S(1)}, u32[]{:S(2)}, u32[]{:S(2)}) collective-permute-start(bf16[144,2048]{1,0:T(8,128)(2,1)S(1)} %get-tuple-element.29), channel_id=1, source_target_pairs={{0,128},{8,136},{16,144},{24,152},{32,160},{40,168},{48,176},{56,1... | collective-permute-start | bytes 1769480 | tf_op jit(solution)/shard_map/ppermute | solution.py:52
  42.1 25.4 %collective-permute-start.2 = (bf16[144,2048]{1,0:T(8,128)(2,1)S(1)}, bf16[144,2048]{1,0:T(8,128)(2,1)S(1)}, u32[]{:S(2)}, u32[]{:S(2)}) collective-permute-start(bf16[144,2048]{1,0:T(8,128)(2,1)S(1)} %get-tuple-element.30), channel_id=1, source_target_pairs={{0,192},{8,200},{16,208},{24,216},{32,224},{40,232},{48,240},{56,2... | collective-permute-start | bytes 1769480 | tf_op jit(solution)/shard_map/ppermute | solution.py:52
  43.7 36.1 %collective-permute-start.9 = (bf16[112,1024]{1,0:T(8,128)(2,1)S(1)}, bf16[112,1024]{1,0:T(8,128)(2,1)S(1)}, u32[]{:S(2)}, u32[]{:S(2)}) collective-permute-start(bf16[112,1024]{1,0:T(8,128)(2,1)S(1)} %get-tuple-element.43), channel_id=1, source_target_pairs={{0,24},{8,32},{16,40},{24,48},{32,56},{40,0},{48,8},{56,16},{64,88... | collective-permute-start | bytes 688136 | tf_op jit(solution)/shard_map/ppermute | solution.py:52
  45.6 34.2 %collective-permute-start.10 = (bf16[112,1024]{1,0:T(8,128)(2,1)S(1)}, bf16[112,1024]{1,0:T(8,128)(2,1)S(1)}, u32[]{:S(2)}, u32[]{:S(2)}) collective-permute-start(bf16[112,1024]{1,0:T(8,128)(2,1)S(1)} %get-tuple-element.44), channel_id=1, source_target_pairs={{0,40},{8,48},{16,56},{24,0},{32,8},{40,16},{48,24},{56,32},{64,10... | collective-permute-start | bytes 688136 | tf_op jit(solution)/shard_map/ppermute | solution.py:52
  67.8 6.8 %collective-permute-start.3 = (bf16[144,640]{1,0:T(8,128)(2,1)S(1)}, bf16[144,640]{1,0:T(8,128)(2,1)S(1)}, u32[]{:S(2)}, u32[]{:S(2)}) collective-permute-start(bf16[144,640]{1,0:T(8,128)(2,1)S(1)} %get-tuple-element.32), channel_id=1, source_target_pairs={{0,8},{8,16},{16,24},{24,32},{32,40},{40,48},{48,56},{56,0},{64,72... | collective-permute-start | bytes 552968 | tf_op jit(solution)/shard_map/ppermute | solution.py:52
  67.9 6.7 %collective-permute-start.4 = (bf16[144,640]{1,0:T(8,128)(2,1)S(1)}, bf16[144,640]{1,0:T(8,128)(2,1)S(1)}, u32[]{:S(2)}, u32[]{:S(2)}) collective-permute-start(bf16[144,640]{1,0:T(8,128)(2,1)S(1)} %get-tuple-element.33), channel_id=1, source_target_pairs={{0,56},{8,0},{16,8},{24,16},{32,24},{40,32},{48,40},{56,48},{64,12... | collective-permute-start | bytes 552968 | tf_op jit(solution)/shard_map/ppermute | solution.py:52
  74.7 10.8 %collective-permute-start.5 = (bf16[144,256]{1,0:T(8,128)(2,1)S(1)}, bf16[144,256]{1,0:T(8,128)(2,1)S(1)}, u32[]{:S(2)}, u32[]{:S(2)}) collective-permute-start(bf16[144,256]{1,0:T(8,128)(2,1)S(1)} %get-tuple-element.36), channel_id=1, source_target_pairs={{0,24},{8,32},{16,40},{24,48},{32,56},{40,0},{48,8},{56,16},{64,88... | collective-permute-start | bytes 221192 | tf_op jit(solution)/shard_map/ppermute | solution.py:52
  79.6 6.8 %collective-permute-start.6 = (bf16[144,256]{1,0:T(8,128)(2,1)S(1)}, bf16[144,256]{1,0:T(8,128)(2,1)S(1)}, u32[]{:S(2)}, u32[]{:S(2)}) collective-permute-start(bf16[144,256]{1,0:T(8,128)(2,1)S(1)} %get-tuple-element.37), channel_id=1, source_target_pairs={{0,40},{8,48},{16,56},{24,0},{32,8},{40,16},{48,24},{56,32},{64,10... | collective-permute-start | bytes 221192 | tf_op jit(solution)/shard_map/ppermute | solution.py:52
  80.0 6.4 %collective-permute-start.11 = (bf16[112,256]{1,0:T(8,128)(2,1)S(1)}, bf16[112,256]{1,0:T(8,128)(2,1)S(1)}, u32[]{:S(2)}, u32[]{:S(2)}) collective-permute-start(bf16[112,256]{1,0:T(8,128)(2,1)S(1)} %get-tuple-element.46), channel_id=1, source_target_pairs={{0,64},{8,72},{16,80},{24,88},{32,96},{40,104},{48,112},{56,120},{... | collective-permute-start | bytes 172040 | tf_op jit(solution)/shard_map/ppermute | solution.py:52
  81.9 5.9 %collective-permute-start.12 = (bf16[112,256]{1,0:T(8,128)(2,1)S(1)}, bf16[112,256]{1,0:T(8,128)(2,1)S(1)}, u32[]{:S(2)}, u32[]{:S(2)}) collective-permute-start(bf16[112,256]{1,0:T(8,128)(2,1)S(1)} %get-tuple-element.47), channel_id=1, source_target_pairs={{0,128},{8,136},{16,144},{24,152},{32,160},{40,168},{48,176},{56,1... | collective-permute-start | bytes 172040 | tf_op jit(solution)/shard_map/ppermute | solution.py:52
  85.0 4.2 %collective-permute-start.13 = (bf16[112,256]{1,0:T(8,128)(2,1)S(1)}, bf16[112,256]{1,0:T(8,128)(2,1)S(1)}, u32[]{:S(2)}, u32[]{:S(2)}) collective-permute-start(bf16[112,256]{1,0:T(8,128)(2,1)S(1)} %get-tuple-element.48), channel_id=1, source_target_pairs={{0,192},{8,200},{16,208},{24,216},{32,224},{40,232},{48,240},{56,2... | collective-permute-start | bytes 172040 | tf_op jit(solution)/shard_map/ppermute | solution.py:52
  91.0 8.2 %collective-permute-start.23 = (bf16[112,256]{1,0:T(8,128)(2,1)S(1)}, bf16[112,256]{1,0:T(8,128)(2,1)S(1)}, u32[]{:S(2)}, u32[]{:S(2)}) collective-permute-start(bf16[112,256]{1,0:T(8,128)(2,1)S(1)} %get-tuple-element.50), channel_id=1, source_target_pairs={{0,192},{8,200},{16,208},{24,216},{32,224},{40,232},{48,240},{56,2... | collective-permute-start | bytes 172040 | tf_op jit(solution)/shard_map/ppermute | solution.py:52
  92.8 6.3 %collective-permute-start.22 = (bf16[112,256]{1,0:T(8,128)(2,1)S(1)}, bf16[112,256]{1,0:T(8,128)(2,1)S(1)}, u32[]{:S(2)}, u32[]{:S(2)}) collective-permute-start(bf16[112,256]{1,0:T(8,128)(2,1)S(1)} %get-tuple-element.50), channel_id=1, source_target_pairs={{0,128},{8,136},{16,144},{24,152},{32,160},{40,168},{48,176},{56,1... | collective-permute-start | bytes 172040 | tf_op jit(solution)/shard_map/ppermute | solution.py:52
  93.1 6.0 %collective-permute-start.21 = (bf16[112,256]{1,0:T(8,128)(2,1)S(1)}, bf16[112,256]{1,0:T(8,128)(2,1)S(1)}, u32[]{:S(2)}, u32[]{:S(2)}) collective-permute-start(bf16[112,256]{1,0:T(8,128)(2,1)S(1)} %get-tuple-element.50), channel_id=1, source_target_pairs={{0,64},{8,72},{16,80},{24,88},{32,96},{40,104},{48,112},{56,120},{... | collective-permute-start | bytes 172040 | tf_op jit(solution)/shard_map/ppermute | solution.py:52
  94.0 10.3 %collective-permute-start.15 = (bf16[144,256]{1,0:T(8,128)(2,1)S(1)}, bf16[144,256]{1,0:T(8,128)(2,1)S(1)}, u32[]{:S(2)}, u32[]{:S(2)}) collective-permute-start(bf16[144,256]{1,0:T(8,128)(2,1)S(1)} %get-tuple-element.49), channel_id=1, source_target_pairs={{0,24},{8,32},{16,40},{24,48},{32,56},{40,0},{48,8},{56,16},{64,88... | collective-permute-start | bytes 221192 | tf_op jit(solution)/shard_map/ppermute | solution.py:52
  97.3 7.1 %collective-permute-start.14 = (bf16[144,256]{1,0:T(8,128)(2,1)S(1)}, bf16[144,256]{1,0:T(8,128)(2,1)S(1)}, u32[]{:S(2)}, u32[]{:S(2)}) collective-permute-start(bf16[144,256]{1,0:T(8,128)(2,1)S(1)} %get-tuple-element.49), channel_id=1, source_target_pairs={{0,40},{8,48},{16,56},{24,0},{32,8},{40,16},{48,24},{56,32},{64,10... | collective-permute-start | bytes 221192 | tf_op jit(solution)/shard_map/ppermute | solution.py:52
  99.2 26.9 %collective-permute-start.25 = (bf16[112,1024]{1,0:T(8,128)(2,1)S(1)}, bf16[112,1024]{1,0:T(8,128)(2,1)S(1)}, u32[]{:S(2)}, u32[]{:S(2)}) collective-permute-start(bf16[112,1024]{1,0:T(8,128)(2,1)S(1)} %get-tuple-element.55.b0), channel_id=1, source_target_pairs={{0,24},{8,32},{16,40},{24,48},{32,56},{40,0},{48,8},{56,16},{64,88... | collective-permute-start | bytes 688136 | tf_op jit(solution)/shard_map/ppermute | solution.py:52
  102.8 23.4 %collective-permute-start.24 = (bf16[112,1024]{1,0:T(8,128)(2,1)S(1)}, bf16[112,1024]{1,0:T(8,128)(2,1)S(1)}, u32[]{:S(2)}, u32[]{:S(2)}) collective-permute-start(bf16[112,1024]{1,0:T(8,128)(2,1)S(1)} %get-tuple-element.55.b0), channel_id=1, source_target_pairs={{0,40},{8,48},{16,56},{24,0},{32,8},{40,16},{48,24},{56,32},{64,10... | collective-permute-start | bytes 688136 | tf_op jit(solution)/shard_map/ppermute | solution.py:52
  104.5 17.4 %collective-permute-start.17 = (bf16[144,640]{1,0:T(8,128)(2,1)S(1)}, bf16[144,640]{1,0:T(8,128)(2,1)S(1)}, u32[]{:S(2)}, u32[]{:S(2)}) collective-permute-start(bf16[144,640]{1,0:T(8,128)(2,1)S(1)} %get-tuple-element.52), channel_id=1, source_target_pairs={{0,56},{8,0},{16,8},{24,16},{32,24},{40,32},{48,40},{56,48},{64,12... | collective-permute-start | bytes 552968 | tf_op jit(solution)/shard_map/ppermute | solution.py:52
  110.7 9.9 %collective-permute-start.16 = (bf16[144,640]{1,0:T(8,128)(2,1)S(1)}, bf16[144,640]{1,0:T(8,128)(2,1)S(1)}, u32[]{:S(2)}, u32[]{:S(2)}) collective-permute-start(bf16[144,640]{1,0:T(8,128)(2,1)S(1)} %get-tuple-element.53), channel_id=1, source_target_pairs={{0,8},{8,16},{16,24},{24,32},{32,40},{40,48},{48,56},{56,0},{64,72... | collective-permute-start | bytes 552968 | tf_op jit(solution)/shard_map/ppermute | solution.py:52
  121.9 26.3 %collective-permute-start.20 = (bf16[144,2048]{1,0:T(8,128)(2,1)S(1)}, bf16[144,2048]{1,0:T(8,128)(2,1)S(1)}, u32[]{:S(2)}, u32[]{:S(2)}) collective-permute-start(bf16[144,2048]{1,0:T(8,128)(2,1)S(1)} %constant_dynamic-update-slice_fusion.g0), channel_id=1, source_target_pairs={{0,192},{8,200},{16,208},{24,216},{32,224},{40,232},{48,240},{56,2... | collective-permute-start | bytes 1769480 | tf_op jit(solution)/shard_map/ppermute | solution.py:52
  124.2 24.0 %collective-permute-start.19 = (bf16[144,2048]{1,0:T(8,128)(2,1)S(1)}, bf16[144,2048]{1,0:T(8,128)(2,1)S(1)}, u32[]{:S(2)}, u32[]{:S(2)}) collective-permute-start(bf16[144,2048]{1,0:T(8,128)(2,1)S(1)} %constant_dynamic-update-slice_fusion.g0), channel_id=1, source_target_pairs={{0,128},{8,136},{16,144},{24,152},{32,160},{40,168},{48,176},{56,1... | collective-permute-start | bytes 1769480 | tf_op jit(solution)/shard_map/ppermute | solution.py:52
  126.0 25.9 %collective-permute-start.18 = (bf16[144,2048]{1,0:T(8,128)(2,1)S(1)}, bf16[144,2048]{1,0:T(8,128)(2,1)S(1)}, u32[]{:S(2)}, u32[]{:S(2)}) collective-permute-start(bf16[144,2048]{1,0:T(8,128)(2,1)S(1)} %constant_dynamic-update-slice_fusion.g0), channel_id=1, source_target_pairs={{0,64},{8,72},{16,80},{24,88},{32,96},{40,104},{48,112},{56,120},{... | collective-permute-start | bytes 1769480 | tf_op jit(solution)/shard_map/ppermute | solution.py:52
  126.2 25.8 %collective-permute-start.27 = (bf16[112,2560]{1,0:T(8,128)(2,1)S(1)}, bf16[112,2560]{1,0:T(8,128)(2,1)S(1)}, u32[]{:S(2)}, u32[]{:S(2)}) collective-permute-start(bf16[112,2560]{1,0:T(8,128)(2,1)S(1)} %slice_dynamic-update-slice_fusion), channel_id=1, source_target_pairs={{0,56},{8,0},{16,8},{24,16},{32,24},{40,32},{48,40},{56,48},{64,12... | collective-permute-start | bytes 1720328 | tf_op jit(solution)/shard_map/ppermute | solution.py:52
  129.0 22.9 %collective-permute-start.26 = (bf16[112,2560]{1,0:T(8,128)(2,1)S(1)}, bf16[112,2560]{1,0:T(8,128)(2,1)S(1)}, u32[]{:S(2)}, u32[]{:S(2)}) collective-permute-start(bf16[112,2560]{1,0:T(8,128)(2,1)S(1)} %slice_dynamic-update-slice_fusion.1), channel_id=1, source_target_pairs={{0,8},{8,16},{16,24},{24,32},{32,40},{40,48},{48,56},{56,0},{64,72... | collective-permute-start | bytes 1720328 | tf_op jit(solution)/shard_map/ppermute | solution.py:52

commit v2 on v1

v2 whole, which is shorter than its diff:
```python
import functools

import jax
import jax.numpy as jnp
import numpy as np
from jax import lax
from jax.experimental import pallas as pl
from jax.experimental.pallas import tpu as pltpu
from jax.sharding import PartitionSpec as P

epsilon = 1e-06
outer_rate = 0.7
momentum_decay = 0.9

NX, NZ = 4, 8
W = 256
ROWS_A = 160
ROWS_B = 96
BF, F32 = jnp.bfloat16, jnp.float32
VM = 32 * 2**20
GROUP = 5

Z_ORDER = (1, -2, 4, -1, 2, 0, 3, -3)
ANY = pl.BlockSpec(memory_space=pl.ANY)


def hadamard_blocks():
    index = np.arange(64)
    parity = np.zeros((64, 64), np.int64)
    for bit in range(6):
        parity += (index[:, None] >> bit) & (index[None, :] >> bit) & 1
    signs = (1 - 2 * (parity % 2)).astype(np.float32)
    return np.kron(np.eye(2, dtype=np.float32), signs) / 8.0


def params(**kw):
    return pltpu.CompilerParams(vmem_limit_bytes=VM, **kw)


def cost(flops, nbytes):
    return pl.CostEstimate(flops=flops, bytes_accessed=nbytes, transcendentals=0)


def position():
    replica = lax.axis_index("replica")
    return replica // NZ, lax.rem(replica, NZ)


def shift(value, dx, dz):
    pairs = [
        (x * NZ + z, (x + dx) % NX * NZ + (z + dz) % NZ) for x in range(NX) for z in range(NZ)
    ]
    return lax.ppermute(value, "replica", pairs)


def column_of(x, z, dx, dz):
    block = lax.rem(x + dx + NX, NX) * NZ + lax.rem(z + dz + NZ, NZ)
    return pl.multiple_of(block * W, W)


def tables():
    row = lax.broadcasted_iota(jnp.int32, (256, 128), 0)
    column = lax.broadcasted_iota(jnp.int32, (256, 128), 1)
    bits = row & column & 63
    bits = bits ^ (bits >> 3)
    odd = (bits ^ (bits >> 1) ^ (bits >> 2)) & 1
    sign = (1 - 2 * odd).astype(F32) * 0.125
    sign = jnp.where(((row ^ column) & 64) == 0, sign, 0.0)
    turn = jnp.where(row < 128, sign, -sign).astype(BF)
    row = lax.broadcasted_iota(jnp.int32, (256, 256), 0)
    column = lax.broadcasted_iota(jnp.int32, (256, 256), 1)
    mean4 = jnp.where((row >> 6) == (column >> 6), 4.0 / 64.0, 0.0).astype(BF)
    return turn, mean4


def contribute_kernel(jobs, local, base, *rest):
    n_out = sum(len(outs) for _, _, _, outs in jobs)
    out_refs, rest = rest[:n_out], rest[n_out:]
    turn_ref, mean_ref, sem = rest[-3:]
    x, z = position()
    fetches = []
    k = 0
    for job, (row0, rows, slots, _) in enumerate(jobs):
        local_in, base_in = rest[2 * job : 2 * job + 2]
        for i, (dx, dz) in enumerate(slots):
            column = pl.ds(column_of(x, z, dx, dz), W)
            row = pl.ds(row0, rows)
            pair = (
                pltpu.make_async_copy(local.at[0, row, column], local_in.at[i], sem.at[0, k]),
                pltpu.make_async_copy(base.at[row, column], base_in.at[i], sem.at[1, k]),
            )
            for copy in pair:
                copy.start()
            fetches.append(pair)
            k += 1
    turn_ref[...], mean_ref[...] = tables()
    k = 0
    o = 0
    for job, (_, rows, _, outs) in enumerate(jobs):
        local_in, base_in = rest[2 * job : 2 * job + 2]
        first = 0
        for count in outs:
            for j0 in range(0, count, GROUP):
                group = min(GROUP, count - j0)
                i = first + j0
                for pair in fetches[k : k + group]:
                    for copy in pair:
                        copy.wait()
                k += group
                height = group * rows
                turned, squares = [], []
                for half in range(2):
                    lanes = pl.ds(half * 128, 128)
                    pair = jnp.concatenate(
                        [
                            base_in[i : i + group, :, lanes].reshape(height, 128),
                            local_in[i : i + group, :, lanes].reshape(height, 128),
                        ],
                        axis=1,
                    )
                    rotated = jnp.dot(pair, turn_ref[...], preferred_element_type=F32)
                    turned.append(rotated)
                    squares.append((rotated * rotated).astype(BF))
                power = jnp.dot(
                    jnp.concatenate(squares, axis=1), mean_ref[...], preferred_element_type=F32
                )
                power = power + 4.0 * epsilon
                limit = power * lax.rsqrt(power)
                for half in range(2):
                    bound = limit[:, half * 128 : half * 128 + 128]
                    value = jnp.minimum(jnp.maximum(turned[half], -bound), bound).astype(BF)
                    for g in range(group):
                        out_refs[o][:, pl.ds((j0 + g) * W + half * 128, 128)] = value[
                            g * rows : (g + 1) * rows
                        ]
            first += count
            o += 1


def contribute(jobs, local, base):
    n = sum(len(slots) for _, _, slots, _ in jobs)
    shapes = [
        jax.ShapeDtypeStruct((rows, count * W), BF) for _, rows, _, outs in jobs for count in outs
    ]
    scratch = []
    for _, rows, slots, _ in jobs:
        scratch += [pltpu.VMEM((len(slots), rows, W), BF)] * 2
    size = sum(rows * len(slots) * W for _, rows, slots, _ in jobs)
    return pl.pallas_call(
        functools.partial(contribute_kernel, jobs),
        out_shape=shapes,
        in_specs=[pl.BlockSpec(memory_space=pltpu.HBM)] * 2,
        out_specs=[pl.BlockSpec(memory_space=pltpu.VMEM)] * len(shapes),
        scratch_shapes=scratch
        + [
            pltpu.VMEM((256, 128), BF),
            pltpu.VMEM((256, 256), BF),
            pltpu.SemaphoreType.DMA((2, n)),
        ],
        compiler_params=params(),
        cost_estimate=cost(size * 1024, size * 6),
        name="contribute",
    )(local, base)


def call(kernel, outs, *args, nbytes=2**20, name=None):
    return pl.pallas_call(
        kernel,
        out_shape=[jax.ShapeDtypeStruct(s, d) for s, d in outs],
        in_specs=[pl.BlockSpec(memory_space=pltpu.VMEM)] * len(args),
        out_specs=[pl.BlockSpec(memory_space=pltpu.VMEM)] * len(outs),
        compiler_params=params(),
        cost_estimate=cost(nbytes, nbytes),
        name=name,
    )(*args)


def f(ref, start, size):
    return ref[:, pl.ds(start, size)].astype(F32)


def relay_x_kernel(near_pa, near_ma, near_mb, low, high, to_pa, to_ma, to_mb):
    to_pa[:, pl.ds(0, 1024)] = (f(near_pa, 0, 1024) + f(low, 0, 1024)).astype(BF)
    to_pa[:, pl.ds(1024, 256)] = near_pa[:, pl.ds(1024, 256)]
    to_ma[:, pl.ds(0, 1024)] = near_ma[:, pl.ds(0, 1024)]
    to_ma[:, pl.ds(1024, 256)] = (f(near_ma, 1024, 256) + f(high, 0, 256)).astype(BF)
    to_mb[...] = (f(near_mb, 0, 768) + f(high, 256, 768)).astype(BF)


def sum_x_kernel(own, r1, r2, *outs):
    start = 0
    for out in outs:
        size = out.shape[1]
        total = f(own, start, size) + f(r1, start, size) + f(r2, start, size)
        out[...] = total.astype(out.dtype)
        start += size


def relay_kernel(w, keep3p, keep3m, from_minus, from_plus, to3p, to3m):
    h = w // 2
    to3p[:, pl.ds(0, h)] = (
        f(keep3p, 0, h) + f(from_plus, h + w, h) + f(from_minus, 2 * w, h)
    ).astype(BF)
    to3p[:, pl.ds(h, h)] = (f(keep3p, h, h) + f(from_plus, 2 * w, h)).astype(BF)
    to3m[:, pl.ds(0, h)] = (f(keep3m, 0, h) + f(from_minus, w, h)).astype(BF)
    to3m[:, pl.ds(h, h)] = (f(keep3m, h, h) + f(from_minus, w + h, h) + f(from_plus, 0, h)).astype(
        BF
    )


def near(w, keep0, from_minus, from_plus, r3p, r3m, start, size):
    return (f(keep0, start, size) + f(from_minus, start, size)) + (
        f(from_plus, w // 2 + start, size) + f(r3p, start, size) + f(r3m, start, size)
    )


def sum_z_kernel(keep0, from_minus, from_plus, r3p, r3m, own, s1, s2, s3):
    for k, out in enumerate((own, s1, s2, s3)):
        out[...] = near(NX * W, keep0, from_minus, from_plus, r3p, r3m, k * W, W).astype(out.dtype)


def update_kernel(
    keep0, from_minus, from_plus, r3p, r3m, own, b1, b2, b3, base, momentum, table,
    new_momentum, shard_a, shard_b, base_in, sem,
):
    x, z = position()
    columns = pl.ds(column_of(x, z, 0, 0), W)
    copy = pltpu.make_async_copy(base.at[:, columns], base_in, sem)
    copy.start()
    summed_a = near(W, keep0, from_minus, from_plus, r3p, r3m, 0, W)
    summed_b = (own[...] + b1[...].astype(F32)) + (b2[...].astype(F32) + b3[...].astype(F32))
    copy.wait()
    for row0, rows, summed, out in (
        (0, ROWS_A, summed_a, shard_a),
        (ROWS_A, ROWS_B, summed_b, shard_b),
    ):
        for half in range(2):
            lanes = pl.ds(half * 128, 128)
            row = pl.ds(row0, rows)
            outer_grad = jnp.dot(
                summed[:, half * 128 : half * 128 + 128] * (1.0 / 32.0),
                table[...],
                precision=lax.Precision.HIGHEST,
                preferred_element_type=F32,
            )
            moved = momentum_decay * momentum[row, lanes] + outer_grad
            new_momentum[row, lanes] = moved
            updated = base_in[row, lanes].astype(F32) - outer_rate * (
                outer_grad + momentum_decay * moved
            )
            out[:, lanes] = updated.astype(BF)


def update(base, momentum, *args):
    table = jnp.asarray(hadamard_blocks(), F32)
    vmem = pl.BlockSpec(memory_space=pltpu.VMEM)
    return pl.pallas_call(
        update_kernel,
        out_shape=[
            jax.ShapeDtypeStruct((ROWS_A + ROWS_B, W), F32),
            jax.ShapeDtypeStruct((ROWS_A, W), BF),
            jax.ShapeDtypeStruct((ROWS_B, W), BF),
        ],
        in_specs=[vmem] * 9 + [pl.BlockSpec(memory_space=pltpu.HBM)] + [vmem] * 2,
        out_specs=[vmem] * 3,
        scratch_shapes=[pltpu.VMEM((ROWS_A + ROWS_B, W), BF), pltpu.SemaphoreType.DMA],
        compiler_params=params(),
        cost_estimate=cost(2**22, 2**20),
        name="update",
    )(*args, base, momentum, table)


PART_1 = ((0, 256, 0, 0), (256, 256, 3, 0), (512, 256, -3, 0))
PART_2 = (
    (0, 256, -1, 0), (256, 256, 2, 0), (512, 128, 4, 0),
    (640, 256, 1, 0), (896, 256, -2, 0), (1152, 128, 4, 128),
)
LOW = PART_1 + ((768, 256, -1, 0),)
HIGH = ((0, 256, 2, 0), (256, 128, 4, 0), (384, 256, 1, 0), (640, 256, -2, 0), (896, 128, 4, 128))


def assemble_kernel(o1, o2, m1, m2, p1, p2, low, high, b0, b3p, b3m, bm, bp, out, sem):
    x, z = position()
    row_a, row_b = pl.ds(0, ROWS_A), pl.ds(ROWS_A, ROWS_B)
    copies = []

    def put(source, start, width, row, dx, dz, inner):
        column = column_of(x, z, dx, dz) + inner
        column = pl.ds(pl.multiple_of(column, 128), width)
        k = len(copies)
        copy = pltpu.make_async_copy(source.at[:, pl.ds(start, width)], out.at[row, column], sem.at[k])
        copy.start()
        copies.append(copy)

    for source, dx, pieces in (
        (o1, 0, PART_1), (o2, 0, PART_2), (m1, -1, PART_1), (m2, -1, PART_2),
        (p1, 1, PART_1), (p2, 1, PART_2), (low, 2, LOW), (high, 2, HIGH),
    ):
        for start, width, dz, inner in pieces:
            put(source, start, width, row_a, dx, dz, inner)
    for block, start, parts, dz, first in (
        (b0, 0, 4, 0, 0), (b3p, 0, 4, 3, 0), (b3m, 0, 4, -3, 0), (bm, 0, 4, -1, 0), (bm, 1024, 4, 2, 0),
        (bm, 2048, 2, 4, 0), (bp, 0, 4, 1, 0), (bp, 1024, 4, -2, 0), (bp, 2048, 2, 4, 2),
    ):
        for k in range(parts):
            put(block, start + k * W, W, row_b, -(first + k), dz, 0)
    for copy in copies:
        copy.wait()


def assemble(*blocks):
    return pl.pallas_call(
        assemble_kernel,
        out_shape=jax.ShapeDtypeStruct((ROWS_A + ROWS_B, NX * NZ * W), BF),
        in_specs=[ANY] * len(blocks),
        out_specs=ANY,
        scratch_shapes=[pltpu.SemaphoreType.DMA((80,))],
        compiler_params=params(),
        cost_estimate=cost(0, 2**23),
        name="assemble",
    )(*blocks)


def shards(local, base, momentum):
    z_a, z_b = Z_ORDER[:5], Z_ORDER[5:]

    far = tuple((2, dz) for dz in Z_ORDER)
    far_low, far_high = contribute(((0, ROWS_A, far, (4, 4)),), local, base)
    sent_b = tuple((dx, dz) for dz in z_a for dx in range(NX))
    plus_b, minus_b = contribute(((ROWS_A, ROWS_B, sent_b, (10, 10)),), local, base)
    near = tuple((dx, dz) for dx in (1, -1, 0) for dz in Z_ORDER)
    kept_b = tuple((dx, dz) for dz in z_b for dx in range(NX))
    near_pa, near_pb, near_ma, near_mb, own_xa, own_xb, keep0_b, keep3p_b, keep3m_b = contribute(
        ((0, ROWS_A, near, (5, 3) * 3), (ROWS_A, ROWS_B, kept_b, (4, 4, 4))), local, base
    )
    low, high = shift(far_low, 1, 0), shift(far_high, -1, 0)
    from_minus_b, from_plus_b = shift(plus_b, 0, 1), shift(minus_b, 0, -1)

    wide, thin = (ROWS_A, 1280), (ROWS_A, 768)
    to_pa, to_ma, to_mb = call(
        relay_x_kernel, [(wide, BF), (wide, BF), (thin, BF)],
        near_pa, near_ma, near_mb, low, high, name="relay_x",
    )
    r_pa, r_ma = shift(to_pa, 1, 0), shift(to_ma, -1, 0)
    r_pb, r_mb = shift(near_pb, 1, 0), shift(to_mb, -1, 0)
    strip, group = (ROWS_A, W), (ROWS_A, 640)
    plus_a, minus_a = call(
        sum_x_kernel, [(group, BF), (group, BF)], own_xa, r_pa, r_ma, name="sum_a1"
    )
    from_minus, from_plus = shift(plus_a, 0, 1), shift(minus_a, 0, -1)
    keep0, keep3p, keep3m = call(
        sum_x_kernel, [(strip, F32)] * 3, own_xb, r_pb, r_mb, name="sum_a2"
    )

    half = (ROWS_B, NX * W)
    to3p, to3m = call(
        functools.partial(relay_kernel, NX * W), [(half, BF), (half, BF)],
        keep3p_b, keep3m_b, from_minus_b, from_plus_b, name="relay_b",
    )
    r3p_b, r3m_b = shift(to3p, 0, 3), shift(to3m, 0, -3)

    to3p, to3m = call(
        functools.partial(relay_kernel, W), [(strip, BF), (strip, BF)],
        keep3p, keep3m, from_minus, from_plus, name="relay_a",
    )
    r3p, r3m = shift(to3p, 0, 3), shift(to3m, 0, -3)

    strip = (ROWS_B, W)
    own, s1, s2, s3 = call(
        sum_z_kernel, [(strip, F32), (strip, BF), (strip, BF), (strip, BF)],
        keep0_b, from_minus_b, from_plus_b, r3p_b, r3m_b, name="sum_b",
    )
    b1, b2, b3 = shift(s1, 1, 0), shift(s2, 2, 0), shift(s3, 3, 0)

    new_momentum, own_a, own_b = update(
        base, momentum, keep0, from_minus, from_plus, r3p, r3m, own, b1, b2, b3
    )

    p3, m3 = shift(own_a, 0, -3), shift(own_a, 0, 3)
    strips = [own_b] + [shift(own_b, e, 0) for e in (1, 2, 3)]
    from_minus = shift(jnp.concatenate([own_a, p3, m3[:, :128]], axis=1), 0, 1)
    from_plus = shift(jnp.concatenate([own_a, m3, p3[:, 128:]], axis=1), 0, -1)
    part1 = jnp.concatenate([own_a, p3, m3], axis=1)
    m1, p1 = shift(part1, 1, 0), shift(part1, -1, 0)
    part2 = jnp.concatenate([from_minus, from_plus], axis=1)
    m2, p2 = shift(part2, 1, 0), shift(part2, -1, 0)
    low = shift(jnp.concatenate([m1, m2[:, :256]], axis=1), 1, 0)
    high = shift(p2[:, 256:], -1, 0)
    row_b = jnp.concatenate(strips, axis=1)
    p3_b, m3_b = shift(row_b, 0, -3), shift(row_b, 0, 3)
    from_minus_b = shift(jnp.concatenate([row_b, p3_b, m3_b[:, :512]], axis=1), 0, 1)
    from_plus_b = shift(jnp.concatenate([row_b, m3_b, p3_b[:, 512:]], axis=1), 0, -1)
    new_fragment = assemble(
        part1, part2, m1, m2, p1, p2, low, high, row_b, p3_b, m3_b, from_minus_b, from_plus_b
    )
    return (new_fragment, new_momentum)


def solution(mesh):
    in_specs = (P("replica", "shard", None), P("shard", None), P("shard", "replica"))
    out_specs = (P("shard", None), P("shard", "replica"))
    return jax.shard_map(shards, mesh=mesh, in_specs=in_specs, out_specs=out_specs, check_vma=False)
```

time: 157 us -> 126 us (0.80)
  waiting for transfers between devices: 58.1 us -> 39.5 us
  Pallas kernels: 32.7 us -> 15.1 us
  starting transfers between devices: 59.2 us -> 65.4 us
    ppermute x28 -> x34, waiting for transfers between devices: 58.1 us -> 39.5 us  [shift(): return lax.ppermute(value, 'replica', pairs)]
    pallas_call x2 -> x3, Pallas kernels: 27.2 us -> 10.5 us  [contribute(): pl.pallas_call(functools.partial(contribute_kernel, jobs), out_shape=shap...]
    ppermute x28 -> x34, starting transfers between devices: 59.2 us -> 65.4 us  [shift(): return lax.ppermute(value, 'replica', pairs)]
    unnamed x27 -> x20, local copies, waits for them, and re-layouts: 4.04 us -> 4.52 us
  transfers between devices with their start and end apart: 28 -> 34, of which waited for: 12 -> 12; matrix products, arithmetic and copies ran while one was open for 0% -> 0% of each run, Pallas kernels for 9% -> 8%
where the time goes in v2:
time: 126 us
  starting transfers between devices  65.4 us (52%)
  waiting for transfers between devices  39.5 us (31%)
  Pallas kernels  15.1 us (12%)
  local copies, waits for them, and re-layouts  4.61 us (4%)
    ppermute x34, starting transfers between devices, shift(): return lax.ppermute(value, 'replica', pairs)  65.4 us
    ppermute x34, waiting for transfers between devices, shift(): return lax.ppermute(value, 'replica', pairs)  39.5 us
    pallas_call x3, Pallas kernels, contribute(): pl.pallas_call(functools.partial(contribute_kernel, jobs), out_shape=shap...  10.5 us
    unnamed x20, local copies, waits for them, and re-layouts  4.52 us
    pallas_call x1, Pallas kernels, assemble(): pl.pallas_call(assemble_kernel, out_shape=jax.ShapeDtypeStruct((ROWS_A +...  2.68 us
  transfers between devices with their start and end apart: 34, of which 12 were waited for; matrix products, arithmetic and copies ran while one was open for 0% of the time, Pallas kernels for 8%

profile of v2, /device:TPU:16, one launch (start us, length us, event | category | flops | bytes accessed | tf_op | source)
XLA Modules:
  0.0 125.7 jit_solution(9201847335498282456)
XLA Ops:
  0.6 2.2 %copy-done = bf16[256,8192]{1,0:T(8,128)(2,1)S(1)} copy-done((bf16[256,8192]{1,0:T(8,128)(2,1)S(1)}, bf16[256,8192]{1,0:T(8,128)(2,1)}, u32[]{:S(2)}) %copy-start) | copy-done | bytes 4194328
  2.8 2.2 %copy-done.2 = bf16[1,256,8192]{2,1,0:T(8,128)(2,1)S(1)} copy-done((bf16[1,256,8192]{2,1,0:T(8,128)(2,1)S(1)}, bf16[1,256,8192]{2,1,0:T(8,128)(2,1)}, u32[]{:S(2)}) %copy-start.2) | copy-done | bytes 4194328
  5.0 1.5 %contribute.4 = (bf16[160,1024]{1,0:T(8,128)(2,1)S(1)}, bf16[160,1024]{1,0:T(8,128)(2,1)S(1)}) custom-call(bf16[1,256,8192]{2,1,0:T(8,128)(2,1)S(1)} %copy-done.2, bf16[256,8192]{1,0:T(8,128)(2,1)S(1)} %copy-done), custom_call_target="tpu_custom_call" | custom-call | flops 335544320 | bytes 1966080 | tf_op jit(solution)/shard_map/contribute/pallas_call | solution.py:149
  6.5 1.6 %collective-permute-start.1 = (bf16[160,1024]{1,0:T(8,128)(2,1)S(1)}, bf16[160,1024]{1,0:T(8,128)(2,1)S(1)}, u32[]{:S(2)}, u32[]{:S(2)}) collective-permute-start(bf16[160,1024]{1,0:T(8,128)(2,1)S(1)} %get-tuple-element.39), channel_id=1, source_target_pairs={{0,64},{8,72},{16,80},{24,88},{32,96},{40,104},{48,112},{56,120},{... | collective-permute-start | bytes 983048 | tf_op jit(solution)/shard_map/ppermute | solution.py:53
  8.1 1.7 %collective-permute-start.2 = (bf16[160,1024]{1,0:T(8,128)(2,1)S(1)}, bf16[160,1024]{1,0:T(8,128)(2,1)S(1)}, u32[]{:S(2)}, u32[]{:S(2)}) collective-permute-start(bf16[160,1024]{1,0:T(8,128)(2,1)S(1)} %get-tuple-element.40), channel_id=1, source_target_pairs={{0,192},{8,200},{16,208},{24,216},{32,224},{40,232},{48,240},{56,2... | collective-permute-start | bytes 983048 | tf_op jit(solution)/shard_map/ppermute | solution.py:53
  9.9 2.6 %contribute.5 = (bf16[96,2560]{1,0:T(8,128)(2,1)S(1)}, bf16[96,2560]{1,0:T(8,128)(2,1)S(1)}) custom-call(bf16[1,256,8192]{2,1,0:T(8,128)(2,1)S(1)} %copy-done.2, bf16[256,8192]{1,0:T(8,128)(2,1)S(1)} %copy-done), custom_call_target="tpu_custom_call" | custom-call | flops 503316480 | bytes 2949120 | tf_op jit(solution)/shard_map/contribute/pallas_call | solution.py:149
  12.5 2.0 %collective-permute-start.10 = (bf16[96,2560]{1,0:T(8,128)(2,1)S(1)}, bf16[96,2560]{1,0:T(8,128)(2,1)S(1)}, u32[]{:S(2)}, u32[]{:S(2)}) collective-permute-start(bf16[96,2560]{1,0:T(8,128)(2,1)S(1)} %get-tuple-element.53), channel_id=1, source_target_pairs={{0,8},{8,16},{16,24},{24,32},{32,40},{40,48},{48,56},{56,0},{64,72... | collective-permute-start | bytes 1474568 | tf_op jit(solution)/shard_map/ppermute | solution.py:53
  14.5 4.0 %collective-permute-start.11 = (bf16[96,2560]{1,0:T(8,128)(2,1)S(1)}, bf16[96,2560]{1,0:T(8,128)(2,1)S(1)}, u32[]{:S(2)}, u32[]{:S(2)}) collective-permute-start(bf16[96,2560]{1,0:T(8,128)(2,1)S(1)} %get-tuple-element.54), channel_id=1, source_target_pairs={{0,56},{8,0},{16,8},{24,16},{32,24},{40,32},{48,40},{56,48},{64,12... | collective-permute-start | bytes 1474568 | tf_op jit(solution)/shard_map/ppermute | solution.py:53
  18.5 6.3 %contribute.3 = (bf16[160,1280]{1,0:T(8,128)(2,1)S(1)}, bf16[160,768]{1,0:T(8,128)(2,1)S(1)}, bf16[160,1280]{1,0:T(8,128)(2,1)S(1)}, bf16[160,768]{1,0:T(8,128)(...) custom-call(bf16[1,256,8192]{2,1,0:T(8,128)(2,1)S(1)} %copy-done.2, ...), custom_call_target="tpu_custom_call" | custom-call | flops 1308622848 | bytes 7667712 | tf_op jit(solution)/shard_map/contribute/pallas_call | solution.py:149
  24.9 0.2 relay_x.1
  25.1 0.5 collective-permute-start.4
  25.6 3.0 %collective-permute-start.5 = (bf16[160,1280]{1,0:T(8,128)(2,1)S(1)}, bf16[160,1280]{1,0:T(8,128)(2,1)S(1)}, u32[]{:S(2)}, u32[]{:S(2)}) collective-permute-start(bf16[160,1280]{1,0:T(8,128)(2,1)S(1)} %get-tuple-element.45), channel_id=1, source_target_pairs={{0,192},{8,200},{16,208},{24,216},{32,224},{40,232},{48,240},{56,2... | collective-permute-start | bytes 1228808 | tf_op jit(solution)/shard_map/ppermute | solution.py:53
  28.6 10.4 %collective-permute-done.4.r1 = bf16[160,1280]{1,0:T(8,128)(2,1)S(1)} collective-permute-done((bf16[160,1280]{1,0:T(8,128)(2,1)S(1)}, bf16[160,1280]{1,0:T(8,128)(2,1)S(1)}, u32[]{:S(2)}, u32[]{:S(2)}) %collective-permute-start.4) | collective-permute-done | bytes 409632 | tf_op jit(solution)/shard_map/ppermute | solution.py:53
  39.0 0.3 collective-permute-start.3
  39.3 0.2 sum_a1.1
  39.6 3.2 %collective-permute-start.7 = (bf16[160,640]{1,0:T(8,128)(2,1)S(1)}, bf16[160,640]{1,0:T(8,128)(2,1)S(1)}, u32[]{:S(2)}, u32[]{:S(2)}) collective-permute-start(bf16[160,640]{1,0:T(8,128)(2,1)S(1)} %get-tuple-element.47), channel_id=1, source_target_pairs={{0,56},{8,0},{16,8},{24,16},{32,24},{40,32},{48,40},{56,48},{64,12... | collective-permute-start | bytes 614408 | tf_op jit(solution)/shard_map/ppermute | solution.py:53
  42.9 1.9 %collective-permute-start.12 = (bf16[96,1024]{1,0:T(8,128)(2,1)S(1)}, bf16[96,1024]{1,0:T(8,128)(2,1)S(1)}, u32[]{:S(2)}, u32[]{:S(2)}) collective-permute-start(bf16[96,1024]{1,0:T(8,128)(2,1)S(1)} %get-tuple-element.57), channel_id=1, source_target_pairs={{0,24},{8,32},{16,40},{24,48},{32,56},{40,0},{48,8},{56,16},{64,88... | collective-permute-start | bytes 589832 | tf_op jit(solution)/shard_map/ppermute | solution.py:53
  44.8 3.2 %collective-permute-start.13 = (bf16[96,1024]{1,0:T(8,128)(2,1)S(1)}, bf16[96,1024]{1,0:T(8,128)(2,1)S(1)}, u32[]{:S(2)}, u32[]{:S(2)}) collective-permute-start(bf16[96,1024]{1,0:T(8,128)(2,1)S(1)} %get-tuple-element.58), channel_id=1, source_target_pairs={{0,40},{8,48},{16,56},{24,0},{32,8},{40,16},{48,24},{56,32},{64,10... | collective-permute-start | bytes 589832 | tf_op jit(solution)/shard_map/ppermute | solution.py:53
  48.1 3.2 %collective-permute-done.6.from_minus = bf16[160,640]{1,0:T(8,128)(2,1)S(1)} collective-permute-done((bf16[160,640]{1,0:T(8,128)(2,1)S(1)}, bf16[160,640]{1,0:T(8,128)(2,1)S(1)}, u32[]{:S(2)}, u32[]{:S(2)}) %collective-permute-start.6) | collective-permute-done | bytes 204832 | tf_op jit(solution)/shard_map/ppermute | solution.py:53
  51.3 3.3 %collective-permute-done.7.from_plus = bf16[160,640]{1,0:T(8,128)(2,1)S(1)} collective-permute-done((bf16[160,640]{1,0:T(8,128)(2,1)S(1)}, bf16[160,640]{1,0:T(8,128)(2,1)S(1)}, u32[]{:S(2)}, u32[]{:S(2)}) %collective-permute-start.7) | collective-permute-done | bytes 204832 | tf_op jit(solution)/shard_map/ppermute | solution.py:53
  54.6 2.7 %collective-permute-start.8 = (bf16[160,256]{1,0:T(8,128)(2,1)S(1)}, bf16[160,256]{1,0:T(8,128)(2,1)S(1)}, u32[]{:S(2)}, u32[]{:S(2)}) collective-permute-start(bf16[160,256]{1,0:T(8,128)(2,1)S(1)} %get-tuple-element.50), channel_id=1, source_target_pairs={{0,24},{8,32},{16,40},{24,48},{32,56},{40,0},{48,8},{56,16},{64,88... | collective-permute-start | bytes 245768 | tf_op jit(solution)/shard_map/ppermute | solution.py:53
  57.3 2.4 %collective-permute-start.9 = (bf16[160,256]{1,0:T(8,128)(2,1)S(1)}, bf16[160,256]{1,0:T(8,128)(2,1)S(1)}, u32[]{:S(2)}, u32[]{:S(2)}) collective-permute-start(bf16[160,256]{1,0:T(8,128)(2,1)S(1)} %get-tuple-element.51), channel_id=1, source_target_pairs={{0,40},{8,48},{16,56},{24,0},{32,8},{40,16},{48,24},{56,32},{64,10... | collective-permute-start | bytes 245768 | tf_op jit(solution)/shard_map/ppermute | solution.py:53
  59.7 1.7 %collective-permute-done.13.r3m = bf16[96,1024]{1,0:T(8,128)(2,1)S(1)} collective-permute-done((bf16[96,1024]{1,0:T(8,128)(2,1)S(1)}, bf16[96,1024]{1,0:T(8,128)(2,1)S(1)}, u32[]{:S(2)}, u32[]{:S(2)}) %collective-permute-start.13) | collective-permute-done | bytes 196640 | tf_op jit(solution)/shard_map/ppermute | solution.py:53
  61.6 3.2 %collective-permute-start.15 = (bf16[96,256]{1,0:T(8,128)(2,1)S(1)}, bf16[96,256]{1,0:T(8,128)(2,1)S(1)}, u32[]{:S(2)}, u32[]{:S(2)}) collective-permute-start(bf16[96,256]{1,0:T(8,128)(2,1)S(1)} %get-tuple-element.61), channel_id=1, source_target_pairs={{0,128},{8,136},{16,144},{24,152},{32,160},{40,168},{48,176},{56,1... | collective-permute-start | bytes 147464 | tf_op jit(solution)/shard_map/ppermute | solution.py:53
  64.8 1.2 collective-permute-start.16
  66.0 2.5 %collective-permute-done.14.b1 = bf16[96,256]{1,0:T(8,128)(2,1)S(1)} collective-permute-done((bf16[96,256]{1,0:T(8,128)(2,1)S(1)}, bf16[96,256]{1,0:T(8,128)(2,1)S(1)}, u32[]{:S(2)}, u32[]{:S(2)}) %collective-permute-start.14) | collective-permute-done | bytes 49184 | tf_op jit(solution)/shard_map/ppermute | solution.py:53
  68.5 0.4 collective-permute-done.16.b3
  68.9 1.3 update.1
  70.2 2.5 %collective-permute-start.29 = (bf16[96,256]{1,0:T(8,128)(2,1)S(1)}, bf16[96,256]{1,0:T(8,128)(2,1)S(1)}, u32[]{:S(2)}, u32[]{:S(2)}) collective-permute-start(bf16[96,256]{1,0:T(8,128)(2,1)S(1)} %get-tuple-element.64), channel_id=1, source_target_pairs={{0,192},{8,200},{16,208},{24,216},{32,224},{40,232},{48,240},{56,2... | collective-permute-start | bytes 147464 | tf_op jit(solution)/shard_map/ppermute | solution.py:53
  72.7 0.6 collective-permute-start.28
  73.3 0.4 collective-permute-start.27
  73.7 2.6 %collective-permute-start.18 = (bf16[160,256]{1,0:T(8,128)(2,1)S(1)}, bf16[160,256]{1,0:T(8,128)(2,1)S(1)}, u32[]{:S(2)}, u32[]{:S(2)}) collective-permute-start(bf16[160,256]{1,0:T(8,128)(2,1)S(1)} %get-tuple-element.63), channel_id=1, source_target_pairs={{0,24},{8,32},{16,40},{24,48},{32,56},{40,0},{48,8},{56,16},{64,88... | collective-permute-start | bytes 245768 | tf_op jit(solution)/shard_map/ppermute | solution.py:53
  76.3 2.8 %collective-permute-start.17 = (bf16[160,256]{1,0:T(8,128)(2,1)S(1)}, bf16[160,256]{1,0:T(8,128)(2,1)S(1)}, u32[]{:S(2)}, u32[]{:S(2)}) collective-permute-start(bf16[160,256]{1,0:T(8,128)(2,1)S(1)} %get-tuple-element.63), channel_id=1, source_target_pairs={{0,40},{8,48},{16,56},{24,0},{32,8},{40,16},{48,24},{56,32},{64,10... | collective-permute-start | bytes 245768 | tf_op jit(solution)/shard_map/ppermute | solution.py:53
  79.2 2.0 %collective-permute-start.31 = (bf16[96,1024]{1,0:T(8,128)(2,1)S(1)}, bf16[96,1024]{1,0:T(8,128)(2,1)S(1)}, u32[]{:S(2)}, u32[]{:S(2)}) collective-permute-start(bf16[96,1024]{1,0:T(8,128)(2,1)S(1)} %get-tuple-element.69.b0), channel_id=1, source_target_pairs={{0,24},{8,32},{16,40},{24,48},{32,56},{40,0},{48,8},{56,16},{64,88... | collective-permute-start | bytes 589832 | tf_op jit(solution)/shard_map/ppermute | solution.py:53
  81.2 3.3 %collective-permute-start.30 = (bf16[96,1024]{1,0:T(8,128)(2,1)S(1)}, bf16[96,1024]{1,0:T(8,128)(2,1)S(1)}, u32[]{:S(2)}, u32[]{:S(2)}) collective-permute-start(bf16[96,1024]{1,0:T(8,128)(2,1)S(1)} %get-tuple-element.69.b0), channel_id=1, source_target_pairs={{0,40},{8,48},{16,56},{24,0},{32,8},{40,16},{48,24},{56,32},{64,10... | collective-permute-start | bytes 589832 | tf_op jit(solution)/shard_map/ppermute | solution.py:53
  84.6 4.7 %collective-permute-start.20 = (bf16[160,640]{1,0:T(8,128)(2,1)S(1)}, bf16[160,640]{1,0:T(8,128)(2,1)S(1)}, u32[]{:S(2)}, u32[]{:S(2)}) collective-permute-start(bf16[160,640]{1,0:T(8,128)(2,1)S(1)} %get-tuple-element.66), channel_id=1, source_target_pairs={{0,56},{8,0},{16,8},{24,16},{32,24},{40,32},{48,40},{56,48},{64,12... | collective-permute-start | bytes 614408 | tf_op jit(solution)/shard_map/ppermute | solution.py:53
  89.4 2.1 %collective-permute-start.21 = (bf16[160,768]{1,0:T(8,128)(2,1)S(1)}, bf16[160,768]{1,0:T(8,128)(2,1)S(1)}, u32[]{:S(2)}, u32[]{:S(2)}) collective-permute-start(bf16[160,768]{1,0:T(8,128)(2,1)S(1)} %constant_dynamic-update-slice_fusion.o1), channel_id=1, source_target_pairs={{0,64},{8,72},{16,80},{24,88},{32,96},{40,104},{48,112},{56,120},{... | collective-permute-start | bytes 737288 | tf_op jit(solution)/shard_map/ppermute | solution.py:53
  91.5 1.2 collective-permute-done.31.b3m
  92.7 4.4 %collective-permute-done.19 = bf16[160,640]{1,0:T(8,128)(2,1)S(1)} collective-permute-done((bf16[160,640]{1,0:T(8,128)(2,1)S(1)}, bf16[160,640]{1,0:T(8,128)(2,1)S(1)}, u32[]{:S(2)}, u32[]{:S(2)}) %collective-permute-start.19) | collective-permute-done | bytes 204832 | tf_op jit(solution)/shard_map/ppermute | solution.py:53
  97.2 0.9 collective-permute-done.20
  98.1 3.9 %collective-permute-start.24 = (bf16[160,1280]{1,0:T(8,128)(2,1)S(1)}, bf16[160,1280]{1,0:T(8,128)(2,1)S(1)}, u32[]{:S(2)}, u32[]{:S(2)}) collective-permute-start(bf16[160,1280]{1,0:T(8,128)(2,1)S(1)} %constant_dynamic-update-slice_fusion.3.o2), channel_id=1, source_target_pairs={{0,192},{8,200},{16,208},{24,216},{32,224},{40,232},{48,240},{56,2... | collective-permute-start | bytes 1228808 | tf_op jit(solution)/shard_map/ppermute | solution.py:53
  102.0 2.0 %collective-permute-start.33 = (bf16[96,2560]{1,0:T(8,128)(2,1)S(1)}, bf16[96,2560]{1,0:T(8,128)(2,1)S(1)}, u32[]{:S(2)}, u32[]{:S(2)}) collective-permute-start(bf16[96,2560]{1,0:T(8,128)(2,1)S(1)} %slice_dynamic-update-slice_fusion), channel_id=1, source_target_pairs={{0,56},{8,0},{16,8},{24,16},{32,24},{40,32},{48,40},{56,48},{64,12... | collective-permute-start | bytes 1474568 | tf_op jit(solution)/shard_map/ppermute | solution.py:53
  104.2 6.4 %collective-permute-done.24.p2 = bf16[160,1280]{1,0:T(8,128)(2,1)S(1)} collective-permute-done((bf16[160,1280]{1,0:T(8,128)(2,1)S(1)}, bf16[160,1280]{1,0:T(8,128)(2,1)S(1)}, u32[]{:S(2)}, u32[]{:S(2)}) %collective-permute-start.24) | collective-permute-done | bytes 409632 | tf_op jit(solution)/shard_map/ppermute | solution.py:53
  110.7 3.8 %collective-permute-start.26 = (bf16[160,1024]{1,0:T(8,128)(2,1)S(1)}, bf16[160,1024]{1,0:T(8,128)(2,1)S(1)}, u32[]{:S(2)}, u32[]{:S(2)}) collective-permute-start(bf16[160,1024]{1,0:T(8,128)(2,1)S(1)} %slice.27), channel_id=1, source_target_pairs={{0,192},{8,200},{16,208},{24,216},{32,224},{40,232},{48,240},{56,2... | collective-permute-start | bytes 983048 | tf_op jit(solution)/shard_map/ppermute | solution.py:53
  114.6 3.2 %collective-permute-start.23 = (bf16[160,768]{1,0:T(8,128)(2,1)S(1)}, bf16[160,768]{1,0:T(8,128)(2,1)S(1)}, u32[]{:S(2)}, u32[]{:S(2)}) collective-permute-start(bf16[160,768]{1,0:T(8,128)(2,1)S(1)} %constant_dynamic-update-slice_fusion.o1), channel_id=1, source_target_pairs={{0,192},{8,200},{16,208},{24,216},{32,224},{40,232},{48,240},{56,2... | collective-permute-start | bytes 737288 | tf_op jit(solution)/shard_map/ppermute | solution.py:53
  117.8 3.9 %collective-permute-done.23.p1 = bf16[160,768]{1,0:T(8,128)(2,1)S(1)} collective-permute-done((bf16[160,768]{1,0:T(8,128)(2,1)S(1)}, bf16[160,768]{1,0:T(8,128)(2,1)S(1)}, u32[]{:S(2)}, u32[]{:S(2)}) %collective-permute-start.23) | collective-permute-done | bytes 245792 | tf_op jit(solution)/shard_map/ppermute | solution.py:53
  121.7 1.2 collective-permute-done.25.low
  122.9 2.7 %assemble.1 = bf16[256,8192]{1,0:T(8,128)(2,1)} custom-call(bf16[160,768]{1,0:T(8,128)(2,1)S(1)} %constant_dynamic-update-slice_fusion.o1, bf16[160,1280]{1,0:T(8,128)(2,1)S(1)} %constant_dynamic-update-slice_fusion.3.o2, bf16[160,768]{1,0:T(8,128)(2,1)S(1)} %collective-permute-done.21.m1, bf16[160,1280]{1,0:T(8,128)(2,1)S(1)} %collective-permute-done.22.m2, ...), custom_call_target="tpu_custom_call" | custom-call | bytes 8388608 | tf_op jit(solution)/shard_map/assemble/pallas_call | solution.py:312
  (61 shorter events, 1.2 us)
Async XLA Ops:
  0.6 2.2 %copy-start = (bf16[256,8192]{1,0:T(8,128)(2,1)S(1)}, bf16[256,8192]{1,0:T(8,128)(2,1)}, u32[]{:S(2)}) copy-start(bf16[256,8192]{1,0:T(8,128)(2,1)} %base.7) | copy-start | bytes 12582916
  2.8 2.2 %copy-start.2 = (bf16[1,256,8192]{2,1,0:T(8,128)(2,1)S(1)}, bf16[1,256,8192]{2,1,0:T(8,128)(2,1)}, u32[]{:S(2)}) copy-start(bf16[1,256,8192]{2,1,0:T(8,128)(2,1)} %local.5) | copy-start | bytes 12582916
  6.5 18.4 %collective-permute-start.1 = (bf16[160,1024]{1,0:T(8,128)(2,1)S(1)}, bf16[160,1024]{1,0:T(8,128)(2,1)S(1)}, u32[]{:S(2)}, u32[]{:S(2)}) collective-permute-start(bf16[160,1024]{1,0:T(8,128)(2,1)S(1)} %get-tuple-element.39), channel_id=1, source_target_pairs={{0,64},{8,72},{16,80},{24,88},{32,96},{40,104},{48,112},{56,120},{... | collective-permute-start | bytes 983048 | tf_op jit(solution)/shard_map/ppermute | solution.py:53
  8.1 16.8 %collective-permute-start.2 = (bf16[160,1024]{1,0:T(8,128)(2,1)S(1)}, bf16[160,1024]{1,0:T(8,128)(2,1)S(1)}, u32[]{:S(2)}, u32[]{:S(2)}) collective-permute-start(bf16[160,1024]{1,0:T(8,128)(2,1)S(1)} %get-tuple-element.40), channel_id=1, source_target_pairs={{0,192},{8,200},{16,208},{24,216},{32,224},{40,232},{48,240},{56,2... | collective-permute-start | bytes 983048 | tf_op jit(solution)/shard_map/ppermute | solution.py:53
  12.5 27.1 %collective-permute-start.10 = (bf16[96,2560]{1,0:T(8,128)(2,1)S(1)}, bf16[96,2560]{1,0:T(8,128)(2,1)S(1)}, u32[]{:S(2)}, u32[]{:S(2)}) collective-permute-start(bf16[96,2560]{1,0:T(8,128)(2,1)S(1)} %get-tuple-element.53), channel_id=1, source_target_pairs={{0,8},{8,16},{16,24},{24,32},{32,40},{40,48},{48,56},{56,0},{64,72... | collective-permute-start | bytes 1474568 | tf_op jit(solution)/shard_map/ppermute | solution.py:53
  14.5 28.3 %collective-permute-start.11 = (bf16[96,2560]{1,0:T(8,128)(2,1)S(1)}, bf16[96,2560]{1,0:T(8,128)(2,1)S(1)}, u32[]{:S(2)}, u32[]{:S(2)}) collective-permute-start(bf16[96,2560]{1,0:T(8,128)(2,1)S(1)} %get-tuple-element.54), channel_id=1, source_target_pairs={{0,56},{8,0},{16,8},{24,16},{32,24},{40,32},{48,40},{56,48},{64,12... | collective-permute-start | bytes 1474568 | tf_op jit(solution)/shard_map/ppermute | solution.py:53
  24.9 44.1 %copy-start.1 = (bf16[256,8192]{1,0:T(8,128)(2,1)S(1)}, bf16[256,8192]{1,0:T(8,128)(2,1)}, u32[]{:S(2)}) copy-start(bf16[256,8192]{1,0:T(8,128)(2,1)} %base.7) | copy-start | bytes 12582916
  24.9 44.1 %copy-start.3 = (f32[256,256]{1,0:T(8,128)S(1)}, f32[256,256]{1,0:T(8,128)}, u32[]{:S(2)}) copy-start(f32[256,256]{1,0:T(8,128)} %momentum.1) | copy-start | bytes 786436
  24.9 44.1 %copy-start.4 = (f32[128,128]{1,0:T(8,128)S(1)}, f32[128,128]{1,0:T(8,128)}, u32[]{:S(2)}) copy-start(f32[128,128]{1,0:T(8,128)} %constant.2.clone.table) | copy-start | bytes 196612
  25.1 13.9 %collective-permute-start.4 = (bf16[160,1280]{1,0:T(8,128)(2,1)S(1)}, bf16[160,1280]{1,0:T(8,128)(2,1)S(1)}, u32[]{:S(2)}, u32[]{:S(2)}) collective-permute-start(bf16[160,1280]{1,0:T(8,128)(2,1)S(1)} %get-tuple-element.44), channel_id=1, source_target_pairs={{0,64},{8,72},{16,80},{24,88},{32,96},{40,104},{48,112},{56,120},{... | collective-permute-start | bytes 1228808 | tf_op jit(solution)/shard_map/ppermute | solution.py:53
  25.6 13.7 %collective-permute-start.5 = (bf16[160,1280]{1,0:T(8,128)(2,1)S(1)}, bf16[160,1280]{1,0:T(8,128)(2,1)S(1)}, u32[]{:S(2)}, u32[]{:S(2)}) collective-permute-start(bf16[160,1280]{1,0:T(8,128)(2,1)S(1)} %get-tuple-element.45), channel_id=1, source_target_pairs={{0,192},{8,200},{16,208},{24,216},{32,224},{40,232},{48,240},{56,2... | collective-permute-start | bytes 1228808 | tf_op jit(solution)/shard_map/ppermute | solution.py:53
  28.6 16.2 %collective-permute-start = (bf16[160,768]{1,0:T(8,128)(2,1)S(1)}, bf16[160,768]{1,0:T(8,128)(2,1)S(1)}, u32[]{:S(2)}, u32[]{:S(2)}) collective-permute-start(bf16[160,768]{1,0:T(8,128)(2,1)S(1)} %get-tuple-element.35), channel_id=1, source_target_pairs={{0,64},{8,72},{16,80},{24,88},{32,96},{40,104},{48,112},{56,120},{... | collective-permute-start | bytes 737288 | tf_op jit(solution)/shard_map/ppermute | solution.py:53
  39.0 9.1 %collective-permute-start.3 = (bf16[160,768]{1,0:T(8,128)(2,1)S(1)}, bf16[160,768]{1,0:T(8,128)(2,1)S(1)}, u32[]{:S(2)}, u32[]{:S(2)}) collective-permute-start(bf16[160,768]{1,0:T(8,128)(2,1)S(1)} %get-tuple-element.41), channel_id=1, source_target_pairs={{0,192},{8,200},{16,208},{24,216},{32,224},{40,232},{48,240},{56,2... | collective-permute-start | bytes 737288 | tf_op jit(solution)/shard_map/ppermute | solution.py:53
  39.5 11.8 %collective-permute-start.6 = (bf16[160,640]{1,0:T(8,128)(2,1)S(1)}, bf16[160,640]{1,0:T(8,128)(2,1)S(1)}, u32[]{:S(2)}, u32[]{:S(2)}) collective-permute-start(bf16[160,640]{1,0:T(8,128)(2,1)S(1)} %get-tuple-element.46), channel_id=1, source_target_pairs={{0,8},{8,16},{16,24},{24,32},{32,40},{40,48},{48,56},{56,0},{64,72... | collective-permute-start | bytes 614408 | tf_op jit(solution)/shard_map/ppermute | solution.py:53
  39.6 15.0 %collective-permute-start.7 = (bf16[160,640]{1,0:T(8,128)(2,1)S(1)}, bf16[160,640]{1,0:T(8,128)(2,1)S(1)}, u32[]{:S(2)}, u32[]{:S(2)}) collective-permute-start(bf16[160,640]{1,0:T(8,128)(2,1)S(1)} %get-tuple-element.47), channel_id=1, source_target_pairs={{0,56},{8,0},{16,8},{24,16},{32,24},{40,32},{48,40},{56,48},{64,12... | collective-permute-start | bytes 614408 | tf_op jit(solution)/shard_map/ppermute | solution.py:53
  42.9 16.8 %collective-permute-start.12 = (bf16[96,1024]{1,0:T(8,128)(2,1)S(1)}, bf16[96,1024]{1,0:T(8,128)(2,1)S(1)}, u32[]{:S(2)}, u32[]{:S(2)}) collective-permute-start(bf16[96,1024]{1,0:T(8,128)(2,1)S(1)} %get-tuple-element.57), channel_id=1, source_target_pairs={{0,24},{8,32},{16,40},{24,48},{32,56},{40,0},{48,8},{56,16},{64,88... | collective-permute-start | bytes 589832 | tf_op jit(solution)/shard_map/ppermute | solution.py:53
  44.8 16.6 %collective-permute-start.13 = (bf16[96,1024]{1,0:T(8,128)(2,1)S(1)}, bf16[96,1024]{1,0:T(8,128)(2,1)S(1)}, u32[]{:S(2)}, u32[]{:S(2)}) collective-permute-start(bf16[96,1024]{1,0:T(8,128)(2,1)S(1)} %get-tuple-element.58), channel_id=1, source_target_pairs={{0,40},{8,48},{16,56},{24,0},{32,8},{40,16},{48,24},{56,32},{64,10... | collective-permute-start | bytes 589832 | tf_op jit(solution)/shard_map/ppermute | solution.py:53
  54.6 14.3 %collective-permute-start.8 = (bf16[160,256]{1,0:T(8,128)(2,1)S(1)}, bf16[160,256]{1,0:T(8,128)(2,1)S(1)}, u32[]{:S(2)}, u32[]{:S(2)}) collective-permute-start(bf16[160,256]{1,0:T(8,128)(2,1)S(1)} %get-tuple-element.50), channel_id=1, source_target_pairs={{0,24},{8,32},{16,40},{24,48},{32,56},{40,0},{48,8},{56,16},{64,88... | collective-permute-start | bytes 245768 | tf_op jit(solution)/shard_map/ppermute | solution.py:53
  57.3 11.6 %collective-permute-start.9 = (bf16[160,256]{1,0:T(8,128)(2,1)S(1)}, bf16[160,256]{1,0:T(8,128)(2,1)S(1)}, u32[]{:S(2)}, u32[]{:S(2)}) collective-permute-start(bf16[160,256]{1,0:T(8,128)(2,1)S(1)} %get-tuple-element.51), channel_id=1, source_target_pairs={{0,40},{8,48},{16,56},{24,0},{32,8},{40,16},{48,24},{56,32},{64,10... | collective-permute-start | bytes 245768 | tf_op jit(solution)/shard_map/ppermute | solution.py:53
  61.6 6.9 %collective-permute-start.14 = (bf16[96,256]{1,0:T(8,128)(2,1)S(1)}, bf16[96,256]{1,0:T(8,128)(2,1)S(1)}, u32[]{:S(2)}, u32[]{:S(2)}) collective-permute-start(bf16[96,256]{1,0:T(8,128)(2,1)S(1)} %get-tuple-element.60), channel_id=1, source_target_pairs={{0,64},{8,72},{16,80},{24,88},{32,96},{40,104},{48,112},{56,120},{... | collective-permute-start | bytes 147464 | tf_op jit(solution)/shard_map/ppermute | solution.py:53
  61.6 6.8 %collective-permute-start.15 = (bf16[96,256]{1,0:T(8,128)(2,1)S(1)}, bf16[96,256]{1,0:T(8,128)(2,1)S(1)}, u32[]{:S(2)}, u32[]{:S(2)}) collective-permute-start(bf16[96,256]{1,0:T(8,128)(2,1)S(1)} %get-tuple-element.61), channel_id=1, source_target_pairs={{0,128},{8,136},{16,144},{24,152},{32,160},{40,168},{48,176},{56,1... | collective-permute-start | bytes 147464 | tf_op jit(solution)/shard_map/ppermute | solution.py:53
  64.8 4.1 %collective-permute-start.16 = (bf16[96,256]{1,0:T(8,128)(2,1)S(1)}, bf16[96,256]{1,0:T(8,128)(2,1)S(1)}, u32[]{:S(2)}, u32[]{:S(2)}) collective-permute-start(bf16[96,256]{1,0:T(8,128)(2,1)S(1)} %get-tuple-element.62), channel_id=1, source_target_pairs={{0,192},{8,200},{16,208},{24,216},{32,224},{40,232},{48,240},{56,2... | collective-permute-start | bytes 147464 | tf_op jit(solution)/shard_map/ppermute | solution.py:53
  70.2 9.0 %collective-permute-start.29 = (bf16[96,256]{1,0:T(8,128)(2,1)S(1)}, bf16[96,256]{1,0:T(8,128)(2,1)S(1)}, u32[]{:S(2)}, u32[]{:S(2)}) collective-permute-start(bf16[96,256]{1,0:T(8,128)(2,1)S(1)} %get-tuple-element.64), channel_id=1, source_target_pairs={{0,192},{8,200},{16,208},{24,216},{32,224},{40,232},{48,240},{56,2... | collective-permute-start | bytes 147464 | tf_op jit(solution)/shard_map/ppermute | solution.py:53
  72.7 6.5 %collective-permute-start.28 = (bf16[96,256]{1,0:T(8,128)(2,1)S(1)}, bf16[96,256]{1,0:T(8,128)(2,1)S(1)}, u32[]{:S(2)}, u32[]{:S(2)}) collective-permute-start(bf16[96,256]{1,0:T(8,128)(2,1)S(1)} %get-tuple-element.64), channel_id=1, source_target_pairs={{0,128},{8,136},{16,144},{24,152},{32,160},{40,168},{48,176},{56,1... | collective-permute-start | bytes 147464 | tf_op jit(solution)/shard_map/ppermute | solution.py:53
  73.3 5.9 %collective-permute-start.27 = (bf16[96,256]{1,0:T(8,128)(2,1)S(1)}, bf16[96,256]{1,0:T(8,128)(2,1)S(1)}, u32[]{:S(2)}, u32[]{:S(2)}) collective-permute-start(bf16[96,256]{1,0:T(8,128)(2,1)S(1)} %get-tuple-element.64), channel_id=1, source_target_pairs={{0,64},{8,72},{16,80},{24,88},{32,96},{40,104},{48,112},{56,120},{... | collective-permute-start | bytes 147464 | tf_op jit(solution)/shard_map/ppermute | solution.py:53
  73.7 10.9 %collective-permute-start.18 = (bf16[160,256]{1,0:T(8,128)(2,1)S(1)}, bf16[160,256]{1,0:T(8,128)(2,1)S(1)}, u32[]{:S(2)}, u32[]{:S(2)}) collective-permute-start(bf16[160,256]{1,0:T(8,128)(2,1)S(1)} %get-tuple-element.63), channel_id=1, source_target_pairs={{0,24},{8,32},{16,40},{24,48},{32,56},{40,0},{48,8},{56,16},{64,88... | collective-permute-start | bytes 245768 | tf_op jit(solution)/shard_map/ppermute | solution.py:53
  76.3 8.3 %collective-permute-start.17 = (bf16[160,256]{1,0:T(8,128)(2,1)S(1)}, bf16[160,256]{1,0:T(8,128)(2,1)S(1)}, u32[]{:S(2)}, u32[]{:S(2)}) collective-permute-start(bf16[160,256]{1,0:T(8,128)(2,1)S(1)} %get-tuple-element.63), channel_id=1, source_target_pairs={{0,40},{8,48},{16,56},{24,0},{32,8},{40,16},{48,24},{56,32},{64,10... | collective-permute-start | bytes 245768 | tf_op jit(solution)/shard_map/ppermute | solution.py:53
  79.2 13.5 %collective-permute-start.31 = (bf16[96,1024]{1,0:T(8,128)(2,1)S(1)}, bf16[96,1024]{1,0:T(8,128)(2,1)S(1)}, u32[]{:S(2)}, u32[]{:S(2)}) collective-permute-start(bf16[96,1024]{1,0:T(8,128)(2,1)S(1)} %get-tuple-element.69.b0), channel_id=1, source_target_pairs={{0,24},{8,32},{16,40},{24,48},{32,56},{40,0},{48,8},{56,16},{64,88... | collective-permute-start | bytes 589832 | tf_op jit(solution)/shard_map/ppermute | solution.py:53
  81.2 20.8 %collective-permute-start.30 = (bf16[96,1024]{1,0:T(8,128)(2,1)S(1)}, bf16[96,1024]{1,0:T(8,128)(2,1)S(1)}, u32[]{:S(2)}, u32[]{:S(2)}) collective-permute-start(bf16[96,1024]{1,0:T(8,128)(2,1)S(1)} %get-tuple-element.69.b0), channel_id=1, source_target_pairs={{0,40},{8,48},{16,56},{24,0},{32,8},{40,16},{48,24},{56,32},{64,10... | collective-permute-start | bytes 589832 | tf_op jit(solution)/shard_map/ppermute | solution.py:53
  84.6 13.4 %collective-permute-start.20 = (bf16[160,640]{1,0:T(8,128)(2,1)S(1)}, bf16[160,640]{1,0:T(8,128)(2,1)S(1)}, u32[]{:S(2)}, u32[]{:S(2)}) collective-permute-start(bf16[160,640]{1,0:T(8,128)(2,1)S(1)} %get-tuple-element.66), channel_id=1, source_target_pairs={{0,56},{8,0},{16,8},{24,16},{32,24},{40,32},{48,40},{56,48},{64,12... | collective-permute-start | bytes 614408 | tf_op jit(solution)/shard_map/ppermute | solution.py:53
  89.4 7.8 %collective-permute-start.19 = (bf16[160,640]{1,0:T(8,128)(2,1)S(1)}, bf16[160,640]{1,0:T(8,128)(2,1)S(1)}, u32[]{:S(2)}, u32[]{:S(2)}) collective-permute-start(bf16[160,640]{1,0:T(8,128)(2,1)S(1)} %get-tuple-element.67), channel_id=1, source_target_pairs={{0,8},{8,16},{16,24},{24,32},{32,40},{40,48},{48,56},{56,0},{64,72... | collective-permute-start | bytes 614408 | tf_op jit(solution)/shard_map/ppermute | solution.py:53
  89.4 25.1 %collective-permute-start.21 = (bf16[160,768]{1,0:T(8,128)(2,1)S(1)}, bf16[160,768]{1,0:T(8,128)(2,1)S(1)}, u32[]{:S(2)}, u32[]{:S(2)}) collective-permute-start(bf16[160,768]{1,0:T(8,128)(2,1)S(1)} %constant_dynamic-update-slice_fusion.o1), channel_id=1, source_target_pairs={{0,64},{8,72},{16,80},{24,88},{32,96},{40,104},{48,112},{56,120},{... | collective-permute-start | bytes 737288 | tf_op jit(solution)/shard_map/ppermute | solution.py:53
  98.1 12.6 %collective-permute-start.24 = (bf16[160,1280]{1,0:T(8,128)(2,1)S(1)}, bf16[160,1280]{1,0:T(8,128)(2,1)S(1)}, u32[]{:S(2)}, u32[]{:S(2)}) collective-permute-start(bf16[160,1280]{1,0:T(8,128)(2,1)S(1)} %constant_dynamic-update-slice_fusion.3.o2), channel_id=1, source_target_pairs={{0,192},{8,200},{16,208},{24,216},{32,224},{40,232},{48,240},{56,2... | collective-permute-start | bytes 1228808 | tf_op jit(solution)/shard_map/ppermute | solution.py:53
  102.0 12.5 %collective-permute-start.22 = (bf16[160,1280]{1,0:T(8,128)(2,1)S(1)}, bf16[160,1280]{1,0:T(8,128)(2,1)S(1)}, u32[]{:S(2)}, u32[]{:S(2)}) collective-permute-start(bf16[160,1280]{1,0:T(8,128)(2,1)S(1)} %constant_dynamic-update-slice_fusion.3.o2), channel_id=1, source_target_pairs={{0,64},{8,72},{16,80},{24,88},{32,96},{40,104},{48,112},{56,120},{... | collective-permute-start | bytes 1228808 | tf_op jit(solution)/shard_map/ppermute | solution.py:53
  102.0 19.7 %collective-permute-start.33 = (bf16[96,2560]{1,0:T(8,128)(2,1)S(1)}, bf16[96,2560]{1,0:T(8,128)(2,1)S(1)}, u32[]{:S(2)}, u32[]{:S(2)}) collective-permute-start(bf16[96,2560]{1,0:T(8,128)(2,1)S(1)} %slice_dynamic-update-slice_fusion), channel_id=1, source_target_pairs={{0,56},{8,0},{16,8},{24,16},{32,24},{40,32},{48,40},{56,48},{64,12... | collective-permute-start | bytes 1474568 | tf_op jit(solution)/shard_map/ppermute | solution.py:53
  104.1 17.6 %collective-permute-start.32 = (bf16[96,2560]{1,0:T(8,128)(2,1)S(1)}, bf16[96,2560]{1,0:T(8,128)(2,1)S(1)}, u32[]{:S(2)}, u32[]{:S(2)}) collective-permute-start(bf16[96,2560]{1,0:T(8,128)(2,1)S(1)} %slice_dynamic-update-slice_fusion.1), channel_id=1, source_target_pairs={{0,8},{8,16},{16,24},{24,32},{32,40},{40,48},{48,56},{56,0},{64,72... | collective-permute-start | bytes 1474568 | tf_op jit(solution)/shard_map/ppermute | solution.py:53
  110.7 11.0 %collective-permute-start.26 = (bf16[160,1024]{1,0:T(8,128)(2,1)S(1)}, bf16[160,1024]{1,0:T(8,128)(2,1)S(1)}, u32[]{:S(2)}, u32[]{:S(2)}) collective-permute-start(bf16[160,1024]{1,0:T(8,128)(2,1)S(1)} %slice.27), channel_id=1, source_target_pairs={{0,192},{8,200},{16,208},{24,216},{32,224},{40,232},{48,240},{56,2... | collective-permute-start | bytes 983048 | tf_op jit(solution)/shard_map/ppermute | solution.py:53
  114.5 8.4 %collective-permute-start.25 = (bf16[160,1024]{1,0:T(8,128)(2,1)S(1)}, bf16[160,1024]{1,0:T(8,128)(2,1)S(1)}, u32[]{:S(2)}, u32[]{:S(2)}) collective-permute-start(bf16[160,1024]{1,0:T(8,128)(2,1)S(1)} %pad_maximum_fusion), channel_id=1, source_target_pairs={{0,64},{8,72},{16,80},{24,88},{32,96},{40,104},{48,112},{56,120},{... | collective-permute-start | bytes 983048 | tf_op jit(solution)/shard_map/ppermute | solution.py:53
  114.6 7.1 %collective-permute-start.23 = (bf16[160,768]{1,0:T(8,128)(2,1)S(1)}, bf16[160,768]{1,0:T(8,128)(2,1)S(1)}, u32[]{:S(2)}, u32[]{:S(2)}) collective-permute-start(bf16[160,768]{1,0:T(8,128)(2,1)S(1)} %constant_dynamic-update-slice_fusion.o1), channel_id=1, source_target_pairs={{0,192},{8,200},{16,208},{24,216},{32,224},{40,232},{48,240},{56,2... | collective-permute-start | bytes 737288 | tf_op jit(solution)/shard_map/ppermute | solution.py:53

commit v3 on v0

v3 whole, which is shorter than its diff:
```python
import functools

import jax
import jax.numpy as jnp
import numpy as np
from jax import lax
from jax.experimental import pallas as pl
from jax.experimental.pallas import tpu as pltpu
from jax.sharding import PartitionSpec as P

epsilon = 1e-06
outer_rate = 0.7
momentum_decay = 0.9

NX, NZ = 4, 8
W = 256
ROWS_A = 128
ROWS_B = 128
BF, F32 = jnp.bfloat16, jnp.float32
VM = 32 * 2**20
GROUP = 8

Z_ORDER = (1, -2, 4, -1, 2, 0, 3, -3)
ANY = pl.BlockSpec(memory_space=pl.ANY)


def hadamard_blocks():
    index = np.arange(64)
    parity = np.zeros((64, 64), np.int64)
    for bit in range(6):
        parity += (index[:, None] >> bit) & (index[None, :] >> bit) & 1
    signs = (1 - 2 * (parity % 2)).astype(np.float32)
    return np.kron(np.eye(2, dtype=np.float32), signs) / 8.0


def params(**kw):
    return pltpu.CompilerParams(vmem_limit_bytes=VM, **kw)


def cost(flops, nbytes):
    return pl.CostEstimate(flops=flops, bytes_accessed=nbytes, transcendentals=0)


def position():
    replica = lax.axis_index("replica")
    return replica // NZ, lax.rem(replica, NZ)


def shift(value, dx, dz):
    pairs = [
        (x * NZ + z, (x + dx) % NX * NZ + (z + dz) % NZ) for x in range(NX) for z in range(NZ)
    ]
    return lax.ppermute(value, "replica", pairs)


def column_of(x, z, dx, dz):
    block = lax.rem(x + dx + NX, NX) * NZ + lax.rem(z + dz + NZ, NZ)
    return pl.multiple_of(block * W, W)


def tables():
    row = lax.broadcasted_iota(jnp.int32, (256, 256), 0)
    column = lax.broadcasted_iota(jnp.int32, (256, 256), 1)
    same = (row >> 6) == (column >> 6)
    bits = row & column & 63
    bits = bits ^ (bits >> 3)
    odd = (bits ^ (bits >> 1) ^ (bits >> 2)) & 1
    turn = jnp.where(same, (1 - 2 * odd).astype(F32) * 0.125, 0.0).astype(BF)
    mean4 = jnp.where(same, 4.0 / 64.0, 0.0).astype(BF)
    return turn, mean4


def contribute_kernel(jobs, after, local, base, *rest):
    n_out = sum(len(outs) + (own is not None) for _, _, _, outs, own in jobs)
    rest = rest[after:]
    out_refs, rest = list(rest[:n_out]), rest[n_out:]
    turn_ref, mean_ref, sem = rest[-3:]
    x, z = position()
    fetches = []
    k = 0
    for job, (row0, rows, slots, _, _) in enumerate(jobs):
        local_in, base_in = rest[2 * job : 2 * job + 2]
        for i, (dx, dz) in enumerate(slots):
            column = pl.ds(column_of(x, z, dx, dz), W)
            row = pl.ds(row0, rows)
            pair = (
                pltpu.make_async_copy(local.at[0, row, column], local_in.at[i], sem.at[0, k]),
                pltpu.make_async_copy(base.at[row, column], base_in.at[i], sem.at[1, k]),
            )
            for copy in pair:
                copy.start()
            fetches.append(pair)
            k += 1
    turn_ref[...], mean_ref[...] = tables()
    k = 0
    for job, (_, rows, slots, outs, own) in enumerate(jobs):
        local_in, base_in = rest[2 * job : 2 * job + 2]
        heads = [(out_refs.pop(0), count) for count in outs]
        places = [(ref, j) for ref, count in heads for j in range(count)]
        for i in range(0, len(slots), GROUP):
            group = min(GROUP, len(slots) - i)
            for pair in fetches[k : k + group]:
                for copy in pair:
                    copy.wait()
            k += group
            height = group * rows
            pseudo = base_in[i : i + group] - local_in[i : i + group]
            pseudo = pseudo.reshape(height, W)
            rotated = jnp.dot(pseudo, turn_ref[...], preferred_element_type=F32)
            power = jnp.dot(pseudo * pseudo, mean_ref[...], preferred_element_type=F32)
            power = power + 4.0 * epsilon
            limit = power * lax.rsqrt(power)
            value = jnp.minimum(jnp.maximum(rotated, -limit), limit).astype(BF)
            for g in range(group):
                out, j = places[i + g]
                out[:, pl.ds(j * W, W)] = value[g * rows : (g + 1) * rows]
        if own is not None:
            out_refs.pop(0)[...] = base_in[own]


def contribute(jobs, local, base, *after):
    n = sum(len(slots) for _, _, slots, _, _ in jobs)
    shapes, scratch = [], []
    for _, rows, slots, outs, own in jobs:
        for count in outs + (() if own is None else (1,)):
            shapes.append(jax.ShapeDtypeStruct((rows, count * W), BF))
        scratch += [pltpu.VMEM((len(slots), rows, W), BF)] * 2
    size = sum(rows * len(slots) * W for _, rows, slots, _, _ in jobs)
    return pl.pallas_call(
        functools.partial(contribute_kernel, jobs, len(after)),
        out_shape=shapes,
        in_specs=[pl.BlockSpec(memory_space=pltpu.HBM)] * 2 + [ANY] * len(after),
        out_specs=[pl.BlockSpec(memory_space=pltpu.VMEM)] * len(shapes),
        scratch_shapes=scratch
        + [
            pltpu.VMEM((256, 256), BF),
            pltpu.VMEM((256, 256), BF),
            pltpu.SemaphoreType.DMA((2, n)),
        ],
        compiler_params=params(),
        cost_estimate=cost(size * 1024, size * 6),
        name="contribute",
    )(local, base, *after)


def call(kernel, outs, *args, after=(), nbytes=2**20, name=None):
    n, skip = len(args), len(after)

    def body(*refs):
        kernel(*refs[:n], *refs[n + skip :])

    return pl.pallas_call(
        body,
        out_shape=[jax.ShapeDtypeStruct(s, d) for s, d in outs],
        in_specs=[pl.BlockSpec(memory_space=pltpu.VMEM)] * n + [ANY] * skip,
        out_specs=[pl.BlockSpec(memory_space=pltpu.VMEM)] * len(outs),
        compiler_params=params(),
        cost_estimate=cost(nbytes, nbytes),
        name=name,
    )(*args, *after)


def join(groups, *args, after=(), name=None):
    def kernel(*refs):
        for out, group in zip(refs[len(args) :], groups):
            at = 0
            for k, start, size in group:
                out[:, pl.ds(at, size)] = refs[k][:, pl.ds(start, size)]
                at += size

    outs = [((args[0].shape[0], sum(size for _, _, size in group)), BF) for group in groups]
    return call(kernel, outs, *args, after=after, name=name)


def f(ref, start, size):
    return ref[:, pl.ds(start, size)].astype(F32)


def relay_x_kernel(near_p, near_m, low, high, to_p, to_m):
    to_p[:, pl.ds(0, 1024)] = (f(near_p, 0, 1024) + f(low, 0, 1024)).astype(BF)
    to_p[:, pl.ds(1024, 1024)] = near_p[:, pl.ds(1024, 1024)]
    to_m[:, pl.ds(0, 1024)] = near_m[:, pl.ds(0, 1024)]
    to_m[:, pl.ds(1024, 1024)] = (f(near_m, 1024, 1024) + f(high, 0, 1024)).astype(BF)


def sum_x_kernel(own, r1, r2, *outs):
    start = 0
    for out in outs:
        size = out.shape[1]
        total = f(own, start, size) + f(r1, start, size) + f(r2, start, size)
        out[...] = total.astype(out.dtype)
        start += size


def relay_kernel(w, keep3p, keep3m, from_minus, from_plus, to3p, to3m):
    h = w // 2
    to3p[:, pl.ds(0, h)] = (
        f(keep3p, 0, h) + f(from_plus, h + w, h) + f(from_minus, 2 * w, h)
    ).astype(BF)
    to3p[:, pl.ds(h, h)] = (f(keep3p, h, h) + f(from_plus, 2 * w, h)).astype(BF)
    to3m[:, pl.ds(0, h)] = (f(keep3m, 0, h) + f(from_minus, w, h)).astype(BF)
    to3m[:, pl.ds(h, h)] = (f(keep3m, h, h) + f(from_minus, w + h, h) + f(from_plus, 0, h)).astype(
        BF
    )


def near(w, keep0, from_minus, from_plus, r3p, r3m, start, size):
    return (f(keep0, start, size) + f(from_minus, start, size)) + (
        f(from_plus, w // 2 + start, size) + f(r3p, start, size) + f(r3m, start, size)
    )


def sum_z_kernel(keep0, from_minus, from_plus, r3p, r3m, own, s1, s2, s3):
    for k, out in enumerate((own, s1, s2, s3)):
        out[...] = near(NX * W, keep0, from_minus, from_plus, r3p, r3m, k * W, W).astype(out.dtype)


def finish(summed, base, momentum, table, new_momentum, shard):
    for half in range(2):
        lanes = pl.ds(half * 128, 128)
        outer_grad = jnp.dot(
            summed[:, half * 128 : half * 128 + 128] * (1.0 / 32.0),
            table[...],
            precision=lax.Precision.HIGHEST,
            preferred_element_type=F32,
        )
        moved = momentum_decay * momentum[:, lanes] + outer_grad
        new_momentum[:, lanes] = moved
        updated = base[:, lanes].astype(F32) - outer_rate * (outer_grad + momentum_decay * moved)
        shard[:, lanes] = updated.astype(BF)


def update_a_kernel(keep0, from_minus, from_plus, r3p, r3m, *rest):
    finish(near(W, keep0, from_minus, from_plus, r3p, r3m, 0, W), *rest)


def update_b_kernel(own, b1, b2, b3, *rest):
    summed = (own[...] + b1[...].astype(F32)) + (b2[...].astype(F32) + b3[...].astype(F32))
    finish(summed, *rest)


def update(kernel, base, momentum, *args, after=()):
    table = jnp.asarray(hadamard_blocks(), F32)
    outs = [(momentum.shape, F32), (momentum.shape, BF)]
    return call(kernel, outs, *args, base, momentum, table, after=after, name="update")


LOW = ((0, 256, 0, 0), (256, 256, 3, 0), (512, 256, -3, 0), (768, 256, -1, 0))
HIGH = ((0, 256, 2, 0), (256, 128, 4, 0), (384, 256, 1, 0), (640, 256, -2, 0), (896, 128, 4, 128))
WHOLE = LOW + tuple((1024 + start, width, dz, inner) for start, width, dz, inner in HIGH)
ONE = ((0, 4, 0, 0),)
FROM_MINUS = ((0, 4, -1, 0), (1024, 4, 2, 0), (2048, 2, 4, 0))
FROM_PLUS = ((0, 4, 1, 0), (1024, 4, -2, 0), (2048, 2, 4, 2))


def assemble_kernel(plan, *refs):
    sources, out, sem = refs[: len(plan)], refs[-2], refs[-1]
    x, z = position()
    copies = []

    def put(source, start, width, row, dx, dz, inner):
        column = column_of(x, z, dx, dz) + inner
        column = pl.ds(pl.multiple_of(column, 128), width)
        k = len(copies)
        copy = pltpu.make_async_copy(source.at[:, pl.ds(start, width)], out.at[row, column], sem.at[k])
        copy.start()
        copies.append(copy)

    for source, (rows_b, shifted, pieces) in zip(sources, plan):
        if rows_b:
            for start, parts, dz, first in pieces:
                for k in range(parts):
                    row = pl.ds(ROWS_A, ROWS_B)
                    put(source, start + k * W, W, row, -(first + k), dz + shifted, 0)
        else:
            for start, width, dz, inner in pieces:
                put(source, start, width, pl.ds(0, ROWS_A), shifted, dz, inner)
    for copy in copies:
        copy.wait()


def assemble(plan, *blocks):
    aliases = {len(plan): 0} if len(blocks) > len(plan) else {}
    return pl.pallas_call(
        functools.partial(assemble_kernel, plan),
        out_shape=jax.ShapeDtypeStruct((ROWS_A + ROWS_B, NX * NZ * W), BF),
        in_specs=[ANY] * len(blocks),
        out_specs=ANY,
        scratch_shapes=[pltpu.SemaphoreType.DMA((80,))],
        input_output_aliases=aliases,
        compiler_params=params(),
        cost_estimate=cost(0, 2**22),
        name="assemble",
    )(*blocks)


def shards(local, base, momentum):
    z_a, z_b = Z_ORDER[:5], Z_ORDER[5:]
    local = pltpu.with_memory_space_constraint(local, pltpu.HBM)
    base = pltpu.with_memory_space_constraint(base, pltpu.HBM)

    far = tuple((2, dz) for dz in Z_ORDER)
    far_low, far_high = contribute(((0, ROWS_A, far, (4, 4), None),), local, base)
    low, high = shift(far_low, 1, 0), shift(far_high, -1, 0)
    sent_b = tuple((dx, dz) for dz in z_a for dx in range(NX))
    plus_b, minus_b = contribute(
        ((ROWS_A, ROWS_B, sent_b, (10, 10), None),), local, base, far_low
    )
    from_minus_b, from_plus_b = shift(plus_b, 0, 1), shift(minus_b, 0, -1)
    near_x = tuple((dx, dz) for dx in (1, -1) for dz in Z_ORDER)
    near_p, near_m = contribute(((0, ROWS_A, near_x, (8, 8), None),), local, base)

    wide = (ROWS_A, 2048)
    to_p, to_m = call(relay_x_kernel, [(wide, BF)] * 2, near_p, near_m, low, high, name="relay_x")
    r_p, r_m = shift(to_p, 1, 0), shift(to_m, -1, 0)
    own_x = tuple((0, dz) for dz in Z_ORDER)
    kept_b = tuple((dx, dz) for dz in z_b for dx in range(NX))
    own_x, base_a, keep0_b, keep3p_b, keep3m_b, base_b = contribute(
        ((0, ROWS_A, own_x, (8,), 5), (ROWS_A, ROWS_B, kept_b, (4, 4, 4), 0)), local, base
    )

    half = (ROWS_B, NX * W)
    to3p_b, to3m_b = call(
        functools.partial(relay_kernel, NX * W), [(half, BF), (half, BF)],
        keep3p_b, keep3m_b, from_minus_b, from_plus_b, name="relay_b",
    )
    r3p_b, r3m_b = shift(to3p_b, 0, 3), shift(to3m_b, 0, -3)

    strip, group = (ROWS_A, W), (ROWS_A, 640)
    plus_a, minus_a, keep0, keep3p, keep3m = call(
        sum_x_kernel, [(group, BF), (group, BF)] + [(strip, F32)] * 3, own_x, r_p, r_m,
        name="sum_a",
    )
    from_minus, from_plus = shift(plus_a, 0, 1), shift(minus_a, 0, -1)
    to3p, to3m = call(
        functools.partial(relay_kernel, W), [(strip, BF), (strip, BF)],
        keep3p, keep3m, from_minus, from_plus, name="relay_a",
    )
    r3p, r3m = shift(to3p, 0, 3), shift(to3m, 0, -3)

    strip = (ROWS_B, W)
    own, s1, s2, s3 = call(
        sum_z_kernel, [(strip, F32), (strip, BF), (strip, BF), (strip, BF)],
        keep0_b, from_minus_b, from_plus_b, r3p_b, r3m_b, after=(to3p,), name="sum_b",
    )
    b1, b2, b3 = shift(s1, 1, 0), shift(s2, 2, 0), shift(s3, 3, 0)

    momentum_a, own_a = update(
        update_a_kernel, base_a, momentum[:ROWS_A], keep0, from_minus, from_plus, r3p, r3m
    )
    p3, m3 = shift(own_a, 0, -3), shift(own_a, 0, 3)
    momentum_b, own_b = update(
        update_b_kernel, base_b, momentum[ROWS_A:], own, b1, b2, b3, after=(own_a,)
    )
    b1, b2, b3 = [shift(own_b, e, 0) for e in (1, 2, 3)]
    plus_a, minus_a = join(
        (((0, 0, W), (1, 0, W), (2, 0, 128)), ((0, 0, W), (2, 0, W), (1, 128, 128))),
        own_a, p3, m3, after=(own_b,), name="join_a",
    )
    from_minus, from_plus = shift(plus_a, 0, 1), shift(minus_a, 0, -1)
    (row_b,) = join(
        (((0, 0, W), (1, 0, W), (2, 0, W), (3, 0, W)),),
        own_b, b1, b2, b3, after=(plus_a,), name="join_b",
    )
    p3_b, m3_b = shift(row_b, 0, -3), shift(row_b, 0, 3)
    (row_a,) = join(
        (((0, 0, W), (1, 0, W), (2, 0, W), (3, 0, 640), (4, 0, 640)),),
        own_a, p3, m3, from_minus, from_plus, after=(row_b,), name="join_row_a",
    )
    m1, p1 = shift(row_a, 1, 0), shift(row_a, -1, 0)
    plus_b, minus_b = join(
        (((0, 0, 1024), (1, 0, 1024), (2, 0, 512)), ((0, 0, 1024), (2, 0, 1024), (1, 512, 512))),
        row_b, p3_b, m3_b, after=(row_a,), name="join_row_b",
    )
    from_minus_b, from_plus_b = shift(plus_b, 0, 1), shift(minus_b, 0, -1)
    low, high = join(
        (((0, 0, 1024),), ((1, 1024, 1024),)), m1, p1, after=(plus_b,), name="relay_row_a"
    )
    low, high = shift(low, 1, 0), shift(high, -1, 0)
    new_momentum = jnp.concatenate([momentum_a, momentum_b], axis=0)
    early = ((0, 0, WHOLE), (0, -1, WHOLE), (0, 1, WHOLE), (1, 0, ONE), (1, 3, ONE), (1, -3, ONE))
    late = ((0, 2, LOW), (0, 2, HIGH), (1, 0, FROM_MINUS), (1, 0, FROM_PLUS))
    partial = assemble(early, row_a, m1, p1, row_b, p3_b, m3_b)
    new_fragment = assemble(late, low, high, from_minus_b, from_plus_b, partial)
    return (new_fragment, new_momentum)


def solution(mesh):
    in_specs = (P("replica", "shard", None), P("shard", None), P("shard", "replica"))
    out_specs = (P("shard", None), P("shard", "replica"))
    return jax.shard_map(shards, mesh=mesh, in_specs=in_specs, out_specs=out_specs, check_vma=False)
```

time: 421 us -> 119 us (0.28)
  waiting for transfers between devices: 307 us -> 43.1 us
  starting transfers between devices: 0.08 us -> 56.3 us
  local copies, waits for them, and re-layouts: 45.5 us -> 0.03 us
  other arithmetic: 33.4 us -> 0.72 us
  matrix products: 18.1 us -> 0 us
  Pallas kernels: 0 us -> 15.6 us
  between operations: 14.2 us -> 1.02 us
    reduce_scatter x1 -> x0, waiting for transfers between devices: 225 us -> none  [shards(): lax.psum_scatter(expand(levels, scales), 'replica', scatter_dimension=1,...]
    all_gather x1 -> x0, waiting for transfers between devices: 81.7 us -> none  [shards(): lax.all_gather(updated.astype(jnp.bfloat16), 'replica', axis=1, tiled=True)]
    ppermute x0 -> x30, starting transfers between devices: none -> 56.3 us  [shift(): return lax.ppermute(value, 'replica', pairs)]
    ppermute x0 -> x30, waiting for transfers between devices: none -> 43.1 us  [shift(): return lax.ppermute(value, 'replica', pairs)]
    another operation x2 -> x0, local copies, waits for them, and re-layouts: 18.4 us -> none  [compress(): blocks = values.reshape(values.shape[0], -1, 64)]
    dot_general x2 -> x0, matrix products: 18.1 us -> none  [rotate(): jnp.dot(flat, table, precision=lax.Precision.HIGHEST, preferred_element_t...]
    pallas_call x0 -> x18, Pallas kernels: none -> 15.6 us  [the longest x4 10.1 us: contribute(): pl.pallas_call(functools.partial(contribute_kernel, jobs, len(after)), ou...]
    mul x3 -> x0, local copies, waits for them, and re-layouts: 13 us -> none  [the longest x1 12.8 us: compress(): blocks * blocks]
  transfers between devices with their start and end apart: 2 -> 30, of which waited for: 2 -> 12; matrix products, arithmetic and copies ran while one was open for 2% -> 1% of each run, Pallas kernels for 0% -> 10%
where the time goes in v3:
time: 119 us; the launch traced here: 117 us
  starting transfers between devices  56.3 us (47%)
  waiting for transfers between devices  43.1 us (36%)
  Pallas kernels  15.6 us (13%)
    ppermute x30, starting transfers between devices, shift(): return lax.ppermute(value, 'replica', pairs)  56.3 us
    ppermute x30, waiting for transfers between devices, shift(): return lax.ppermute(value, 'replica', pairs)  43.1 us
    pallas_call x4, Pallas kernels, contribute(): pl.pallas_call(functools.partial(contribute_kernel, jobs, len(after)), ou...  10.1 us
    pallas_call x2, Pallas kernels, assemble(): pl.pallas_call(functools.partial(assemble_kernel, plan), out_shape=jax.Sh...  3.99 us
  transfers between devices with their start and end apart: 30, of which 12 were waited for; matrix products, arithmetic and copies ran while one was open for 1% of the time, Pallas kernels for 10%

profile of v3, /device:TPU:16, one launch (start us, length us, event | category | flops | bytes accessed | tf_op | source)
XLA Modules:
  0.0 116.8 jit_solution(15559806954514131501)
XLA Ops:
  0.6 1.9 %contribute.6 = (bf16[128,1024]{1,0:T(8,128)(2,1)S(1)}, bf16[128,1024]{1,0:T(8,128)(2,1)S(1)}) custom-call(bf16[1,256,8192]{2,1,0:T(8,128)(2,1)} %local.7, bf16[256,8192]{1,0:T(8,128)(2,1)} %base.7), custom_call_target="tpu_custom_call" | custom-call | flops 268435456 | bytes 1572864 | tf_op jit(solution)/shard_map/contribute/pallas_call | solution.py:129
  2.5 2.8 %collective-permute-start.1 = (bf16[128,1024]{1,0:T(8,128)(2,1)S(1)}, bf16[128,1024]{1,0:T(8,128)(2,1)S(1)}, u32[]{:S(2)}, u32[]{:S(2)}) collective-permute-start(bf16[128,1024]{1,0:T(8,128)(2,1)S(1)} %get-tuple-element.43), channel_id=1, source_target_pairs={{0,192},{8,200},{16,208},{24,216},{32,224},{40,232},{48,240},{56,2... | collective-permute-start | bytes 786440 | tf_op jit(solution)/shard_map/ppermute | solution.py:53
  5.3 2.9 %contribute.7 = (bf16[128,2560]{1,0:T(8,128)(2,1)S(1)}, bf16[128,2560]{1,0:T(8,128)(2,1)S(1)}) custom-call(bf16[1,256,8192]{2,1,0:T(8,128)(2,1)} %local.7, bf16[256,8192]{1,0:T(8,128)(2,1)} %base.7, bf16[128,1024]{1,0:T(8,128)(2,1)S(1)} %get-tuple-element.42.rest_0_), custom_call_target="tpu_custom_call" | custom-call | flops 671088640 | bytes 3932160 | tf_op jit(solution)/shard_map/contribute/pallas_call | solution.py:129
  8.2 2.0 %collective-permute-start.10 = (bf16[128,2560]{1,0:T(8,128)(2,1)S(1)}, bf16[128,2560]{1,0:T(8,128)(2,1)S(1)}, u32[]{:S(2)}, u32[]{:S(2)}) collective-permute-start(bf16[128,2560]{1,0:T(8,128)(2,1)S(1)} %get-tuple-element.56), channel_id=1, source_target_pairs={{0,8},{8,16},{16,24},{24,32},{32,40},{40,48},{48,56},{56,0},{64,72... | collective-permute-start | bytes 1966088 | tf_op jit(solution)/shard_map/ppermute | solution.py:53
  10.2 4.0 %collective-permute-start.11 = (bf16[128,2560]{1,0:T(8,128)(2,1)S(1)}, bf16[128,2560]{1,0:T(8,128)(2,1)S(1)}, u32[]{:S(2)}, u32[]{:S(2)}) collective-permute-start(bf16[128,2560]{1,0:T(8,128)(2,1)S(1)} %get-tuple-element.57), channel_id=1, source_target_pairs={{0,56},{8,0},{16,8},{24,16},{32,24},{40,32},{48,40},{56,48},{64,12... | collective-permute-start | bytes 1966088 | tf_op jit(solution)/shard_map/ppermute | solution.py:53
  14.2 2.5 %contribute.5 = (bf16[128,2048]{1,0:T(8,128)(2,1)S(1)}, bf16[128,2048]{1,0:T(8,128)(2,1)S(1)}) custom-call(bf16[1,256,8192]{2,1,0:T(8,128)(2,1)} %local.7, bf16[256,8192]{1,0:T(8,128)(2,1)} %base.7), custom_call_target="tpu_custom_call" | custom-call | flops 536870912 | bytes 3145728 | tf_op jit(solution)/shard_map/contribute/pallas_call | solution.py:129
  16.9 0.8 collective-permute-start.2
  17.7 2.6 %collective-permute-start.3 = (bf16[128,2048]{1,0:T(8,128)(2,1)S(1)}, bf16[128,2048]{1,0:T(8,128)(2,1)S(1)}, u32[]{:S(2)}, u32[]{:S(2)}) collective-permute-start(bf16[128,2048]{1,0:T(8,128)(2,1)S(1)} %get-tuple-element.45), channel_id=1, source_target_pairs={{0,192},{8,200},{16,208},{24,216},{32,224},{40,232},{48,240},{56,2... | collective-permute-start | bytes 1572872 | tf_op jit(solution)/shard_map/ppermute | solution.py:53
  20.3 2.9 %contribute.4 = (bf16[128,2048]{1,0:T(8,128)(2,1)S(1)}, bf16[128,256]{1,0:T(8,128)(2,1)S(1)}, bf16[128,1024]{1,0:T(8,128)(2,1)S(1)}, bf16[128,1024]{1,0:T(8,128)...) custom-call(bf16[1,256,8192]{2,1,0:T(8,128)(2,1)} %local.7, bf16[256,8192]{1,0:T(8,128)(2,1)} %base.7), custom_call_target="tpu_custom_call" | custom-call | flops 671088640 | bytes 3932160 | tf_op jit(solution)/shard_map/contribute/pallas_call | solution.py:129
  23.2 5.4 %collective-permute-done.10.refs_2_.refs_1_ = bf16[128,2560]{1,0:T(8,128)(2,1)S(1)} collective-permute-done((bf16[128,2560]{1,0:T(8,128)(2,1)S(1)}, bf16[128,2560]{1,0:T(8,128)(2,1)S(1)}, u32[]{:S(2)}, u32[]{:S(2)}) %collective-permute-start.10) | collective-permute-done | bytes 655392 | tf_op jit(solution)/shard_map/ppermute | solution.py:53
  28.6 0.2 relay_b.1
  28.8 4.6 %collective-permute-start.12 = (bf16[128,1024]{1,0:T(8,128)(2,1)S(1)}, bf16[128,1024]{1,0:T(8,128)(2,1)S(1)}, u32[]{:S(2)}, u32[]{:S(2)}) collective-permute-start(bf16[128,1024]{1,0:T(8,128)(2,1)S(1)} %get-tuple-element.60), channel_id=1, source_target_pairs={{0,24},{8,32},{16,40},{24,48},{32,56},{40,0},{48,8},{56,16},{64,88... | collective-permute-start | bytes 786440 | tf_op jit(solution)/shard_map/ppermute | solution.py:53
  33.4 0.5 collective-permute-start.13
  33.9 0.2 sum_a.1
  34.2 3.2 %collective-permute-start.5 = (bf16[128,640]{1,0:T(8,128)(2,1)S(1)}, bf16[128,640]{1,0:T(8,128)(2,1)S(1)}, u32[]{:S(2)}, u32[]{:S(2)}) collective-permute-start(bf16[128,640]{1,0:T(8,128)(2,1)S(1)} %get-tuple-element.48), channel_id=1, source_target_pairs={{0,56},{8,0},{16,8},{24,16},{32,24},{40,32},{48,40},{56,48},{64,12... | collective-permute-start | bytes 491528 | tf_op jit(solution)/shard_map/ppermute | solution.py:53
  37.4 14.1 %collective-permute-done.4.refs_2_.refs_1_ = bf16[128,640]{1,0:T(8,128)(2,1)S(1)} collective-permute-done((bf16[128,640]{1,0:T(8,128)(2,1)S(1)}, bf16[128,640]{1,0:T(8,128)(2,1)S(1)}, u32[]{:S(2)}, u32[]{:S(2)}) %collective-permute-start.4) | collective-permute-done | bytes 163872 | tf_op jit(solution)/shard_map/ppermute | solution.py:53
  51.5 0.8 collective-permute-done.5.refs_3_.refs_2_
  52.3 5.1 %collective-permute-start.7 = (bf16[128,256]{1,0:T(8,128)(2,1)S(1)}, bf16[128,256]{1,0:T(8,128)(2,1)S(1)}, u32[]{:S(2)}, u32[]{:S(2)}) collective-permute-start(bf16[128,256]{1,0:T(8,128)(2,1)S(1)} %get-tuple-element.52), channel_id=1, source_target_pairs={{0,40},{8,48},{16,56},{24,0},{32,8},{40,16},{48,24},{56,32},{64,10... | collective-permute-start | bytes 196616 | tf_op jit(solution)/shard_map/ppermute | solution.py:53
  57.4 0.5 collective-permute-start.6
  57.9 0.2 sum_b.1
  58.1 0.3 collective-permute-start.14
  58.4 4.0 %collective-permute-start.15 = (bf16[128,256]{1,0:T(8,128)(2,1)S(1)}, bf16[128,256]{1,0:T(8,128)(2,1)S(1)}, u32[]{:S(2)}, u32[]{:S(2)}) collective-permute-start(bf16[128,256]{1,0:T(8,128)(2,1)S(1)} %get-tuple-element.64), channel_id=1, source_target_pairs={{0,128},{8,136},{16,144},{24,152},{32,160},{40,168},{48,176},{56,1... | collective-permute-start | bytes 196616 | tf_op jit(solution)/shard_map/ppermute | solution.py:53
  62.3 0.2 collective-permute-start.16
  62.6 2.2 %collective-permute-done.6.refs_3_ = bf16[128,256]{1,0:T(8,128)(2,1)S(1)} collective-permute-done((bf16[128,256]{1,0:T(8,128)(2,1)S(1)}, bf16[128,256]{1,0:T(8,128)(2,1)S(1)}, u32[]{:S(2)}, u32[]{:S(2)}) %collective-permute-start.6) | collective-permute-done | bytes 65568 | tf_op jit(solution)/shard_map/ppermute | solution.py:53
  64.7 0.3 update.2
  65.0 2.9 %collective-permute-start.9 = (bf16[128,256]{1,0:T(8,128)(2,1)S(1)}, bf16[128,256]{1,0:T(8,128)(2,1)S(1)}, u32[]{:S(2)}, u32[]{:S(2)}) collective-permute-start(bf16[128,256]{1,0:T(8,128)(2,1)S(1)} %get-tuple-element.54.refs_7_.refs_0_), channel_id=1, source_target_pairs={{0,24},{8,32},{16,40},{24,48},{32,56},{40,0},{48,8},{56,16},{64,88... | collective-permute-start | bytes 196616 | tf_op jit(solution)/shard_map/ppermute | solution.py:53
  67.9 2.2 %collective-permute-start.8 = (bf16[128,256]{1,0:T(8,128)(2,1)S(1)}, bf16[128,256]{1,0:T(8,128)(2,1)S(1)}, u32[]{:S(2)}, u32[]{:S(2)}) collective-permute-start(bf16[128,256]{1,0:T(8,128)(2,1)S(1)} %get-tuple-element.54.refs_7_.refs_0_), channel_id=1, source_target_pairs={{0,40},{8,48},{16,56},{24,0},{32,8},{40,16},{48,24},{56,32},{64,10... | collective-permute-start | bytes 196616 | tf_op jit(solution)/shard_map/ppermute | solution.py:53
  70.2 0.3 update.3
  70.5 2.8 %collective-permute-start.21 = (bf16[128,256]{1,0:T(8,128)(2,1)S(1)}, bf16[128,256]{1,0:T(8,128)(2,1)S(1)}, u32[]{:S(2)}, u32[]{:S(2)}) collective-permute-start(bf16[128,256]{1,0:T(8,128)(2,1)S(1)} %get-tuple-element.67.refs_3_.refs_0_), channel_id=1, source_target_pairs={{0,192},{8,200},{16,208},{24,216},{32,224},{40,232},{48,240},{56,2... | collective-permute-start | bytes 196616 | tf_op jit(solution)/shard_map/ppermute | solution.py:53
  73.2 1.0 collective-permute-start.19
  74.2 0.6 collective-permute-done.8.refs_1_
  74.8 3.1 %collective-permute-start.18 = (bf16[128,640]{1,0:T(8,128)(2,1)S(1)}, bf16[128,640]{1,0:T(8,128)(2,1)S(1)}, u32[]{:S(2)}, u32[]{:S(2)}) collective-permute-start(bf16[128,640]{1,0:T(8,128)(2,1)S(1)} %get-tuple-element.69), channel_id=1, source_target_pairs={{0,56},{8,0},{16,8},{24,16},{32,24},{40,32},{48,40},{56,48},{64,12... | collective-permute-start | bytes 491528 | tf_op jit(solution)/shard_map/ppermute | solution.py:53
  77.9 1.2 %collective-permute-done.20.refs_2_ = bf16[128,256]{1,0:T(8,128)(2,1)S(1)} collective-permute-done((bf16[128,256]{1,0:T(8,128)(2,1)S(1)}, bf16[128,256]{1,0:T(8,128)(2,1)S(1)}, u32[]{:S(2)}, u32[]{:S(2)}) %collective-permute-start.20) | collective-permute-done | bytes 65568 | tf_op jit(solution)/shard_map/ppermute | solution.py:53
  79.1 0.3 collective-permute-done.19.refs_1_
  79.4 4.0 %collective-permute-start.25 = (bf16[128,1024]{1,0:T(8,128)(2,1)S(1)}, bf16[128,1024]{1,0:T(8,128)(2,1)S(1)}, u32[]{:S(2)}, u32[]{:S(2)}) collective-permute-start(bf16[128,1024]{1,0:T(8,128)(2,1)S(1)} %join_b.1.refs_5_.refs_0_.refs_3_), channel_id=1, source_target_pairs={{0,24},{8,32},{16,40},{24,48},{32,56},{40,0},{48,8},{56,16},{64,88... | collective-permute-start | bytes 786440 | tf_op jit(solution)/shard_map/ppermute | solution.py:53
  83.5 1.1 collective-permute-start.24
  84.6 4.3 %collective-permute-done.17.refs_3_ = bf16[128,640]{1,0:T(8,128)(2,1)S(1)} collective-permute-done((bf16[128,640]{1,0:T(8,128)(2,1)S(1)}, bf16[128,640]{1,0:T(8,128)(2,1)S(1)}, u32[]{:S(2)}, u32[]{:S(2)}) %collective-permute-start.17) | collective-permute-done | bytes 163872 | tf_op jit(solution)/shard_map/ppermute | solution.py:53
  88.9 1.0 collective-permute-start.23
  89.9 1.1 collective-permute-start.22
  91.1 7.1 %collective-permute-done.25.refs_2_.refs_5_ = bf16[128,1024]{1,0:T(8,128)(2,1)S(1)} collective-permute-done((bf16[128,1024]{1,0:T(8,128)(2,1)S(1)}, bf16[128,1024]{1,0:T(8,128)(2,1)S(1)}, u32[]{:S(2)}, u32[]{:S(2)}) %collective-permute-start.25) | collective-permute-done | bytes 262176 | tf_op jit(solution)/shard_map/ppermute | solution.py:53
  98.2 2.2 %collective-permute-done.24.refs_1_.refs_4_ = bf16[128,1024]{1,0:T(8,128)(2,1)S(1)} collective-permute-done((bf16[128,1024]{1,0:T(8,128)(2,1)S(1)}, bf16[128,1024]{1,0:T(8,128)(2,1)S(1)}, u32[]{:S(2)}, u32[]{:S(2)}) %collective-permute-start.24) | collective-permute-done | bytes 262176 | tf_op jit(solution)/shard_map/ppermute | solution.py:53
  100.5 3.0 %collective-permute-start.28 = (bf16[128,2560]{1,0:T(8,128)(2,1)S(1)}, bf16[128,2560]{1,0:T(8,128)(2,1)S(1)}, u32[]{:S(2)}, u32[]{:S(2)}) collective-permute-start(bf16[128,2560]{1,0:T(8,128)(2,1)S(1)} %get-tuple-element.70.refs_2_), channel_id=1, source_target_pairs={{0,8},{8,16},{16,24},{24,32},{32,40},{40,48},{48,56},{56,0},{64,72... | collective-permute-start | bytes 1966088 | tf_op jit(solution)/shard_map/ppermute | solution.py:53
  103.7 3.3 %collective-permute-start.27 = (bf16[128,1024]{1,0:T(8,128)(2,1)S(1)}, bf16[128,1024]{1,0:T(8,128)(2,1)S(1)}, u32[]{:S(2)}, u32[]{:S(2)}) collective-permute-start(bf16[128,1024]{1,0:T(8,128)(2,1)S(1)} %get-tuple-element.72), channel_id=1, source_target_pairs={{0,192},{8,200},{16,208},{24,216},{32,224},{40,232},{48,240},{56,2... | collective-permute-start | bytes 786440 | tf_op jit(solution)/shard_map/ppermute | solution.py:53
  107.0 0.7 pad_maximum_fusion
  107.7 2.1 %assemble.2.refs_4_ = bf16[256,8192]{1,0:T(8,128)(2,1)} custom-call(bf16[128,2048]{1,0:T(8,128)(2,1)S(1)} %join_row_a.1.refs_3_.refs_0_, bf16[128,2048]{1,0:T(8,128)(2,1)S(1)} %collective-permute-done.22.refs_0_.refs_1_, bf16[128,2048]{1,0:T(8,128)(2,1)S(1)} %collective-permute-done.23.refs_1_.refs_2_, bf16[128,1024]{1,0:T(8,128)(2,1)S(1)} %join_b.1.refs_5_.refs_0_.refs_3_, ...), custom_call_target="tpu_custom_call" | custom-call | bytes 4194304 | tf_op jit(solution)/shard_map/assemble/pallas_call | solution.py:284
  109.8 3.4 %collective-permute-done.29.refs_3_ = bf16[128,2560]{1,0:T(8,128)(2,1)S(1)} collective-permute-done((bf16[128,2560]{1,0:T(8,128)(2,1)S(1)}, bf16[128,2560]{1,0:T(8,128)(2,1)S(1)}, u32[]{:S(2)}, u32[]{:S(2)}) %collective-permute-start.29) | collective-permute-done | bytes 655392 | tf_op jit(solution)/shard_map/ppermute | solution.py:53
  113.2 1.5 %collective-permute-done.28.refs_2_ = bf16[128,2560]{1,0:T(8,128)(2,1)S(1)} collective-permute-done((bf16[128,2560]{1,0:T(8,128)(2,1)S(1)}, bf16[128,2560]{1,0:T(8,128)(2,1)S(1)}, u32[]{:S(2)}, u32[]{:S(2)}) %collective-permute-start.28) | collective-permute-done | bytes 655392 | tf_op jit(solution)/shard_map/ppermute | solution.py:53
  114.7 1.9 %assemble.3 = bf16[256,8192]{1,0:T(8,128)(2,1)} custom-call(bf16[128,1024]{1,0:T(8,128)(2,1)S(1)} %collective-permute-done.26.refs_0_, bf16[128,1024]{1,0:T(8,128)(2,1)S(1)} %collective-permute-done.27.refs_1_, bf16[128,2560]{1,0:T(8,128)(2,1)S(1)} %collective-permute-done.28.refs_2_, ...), custom_call_target="tpu_custom_call", output_to_operand_aliasing={{}: (4, {})} | custom-call | bytes 4194304 | tf_op jit(solution)/shard_map/assemble/pallas_call | solution.py:284
  (36 shorter events, 0.7 us)
Async XLA Ops:
  2.5 14.2 %collective-permute-start.1 = (bf16[128,1024]{1,0:T(8,128)(2,1)S(1)}, bf16[128,1024]{1,0:T(8,128)(2,1)S(1)}, u32[]{:S(2)}, u32[]{:S(2)}) collective-permute-start(bf16[128,1024]{1,0:T(8,128)(2,1)S(1)} %get-tuple-element.43), channel_id=1, source_target_pairs={{0,192},{8,200},{16,208},{24,216},{32,224},{40,232},{48,240},{56,2... | collective-permute-start | bytes 786440 | tf_op jit(solution)/shard_map/ppermute | solution.py:53
  5.3 11.4 %collective-permute-start = (bf16[128,1024]{1,0:T(8,128)(2,1)S(1)}, bf16[128,1024]{1,0:T(8,128)(2,1)S(1)}, u32[]{:S(2)}, u32[]{:S(2)}) collective-permute-start(bf16[128,1024]{1,0:T(8,128)(2,1)S(1)} %get-tuple-element.42.rest_0_), channel_id=1, source_target_pairs={{0,64},{8,72},{16,80},{24,88},{32,96},{40,104},{48,112},{56,120},{... | collective-permute-start | bytes 786440 | tf_op jit(solution)/shard_map/ppermute | solution.py:53
  8.2 20.4 %collective-permute-start.10 = (bf16[128,2560]{1,0:T(8,128)(2,1)S(1)}, bf16[128,2560]{1,0:T(8,128)(2,1)S(1)}, u32[]{:S(2)}, u32[]{:S(2)}) collective-permute-start(bf16[128,2560]{1,0:T(8,128)(2,1)S(1)} %get-tuple-element.56), channel_id=1, source_target_pairs={{0,8},{8,16},{16,24},{24,32},{32,40},{40,48},{48,56},{56,0},{64,72... | collective-permute-start | bytes 1966088 | tf_op jit(solution)/shard_map/ppermute | solution.py:53
  10.2 18.4 %collective-permute-start.11 = (bf16[128,2560]{1,0:T(8,128)(2,1)S(1)}, bf16[128,2560]{1,0:T(8,128)(2,1)S(1)}, u32[]{:S(2)}, u32[]{:S(2)}) collective-permute-start(bf16[128,2560]{1,0:T(8,128)(2,1)S(1)} %get-tuple-element.57), channel_id=1, source_target_pairs={{0,56},{8,0},{16,8},{24,16},{32,24},{40,32},{48,40},{56,48},{64,12... | collective-permute-start | bytes 1966088 | tf_op jit(solution)/shard_map/ppermute | solution.py:53
  16.9 17.0 %collective-permute-start.2 = (bf16[128,2048]{1,0:T(8,128)(2,1)S(1)}, bf16[128,2048]{1,0:T(8,128)(2,1)S(1)}, u32[]{:S(2)}, u32[]{:S(2)}) collective-permute-start(bf16[128,2048]{1,0:T(8,128)(2,1)S(1)} %get-tuple-element.44), channel_id=1, source_target_pairs={{0,64},{8,72},{16,80},{24,88},{32,96},{40,104},{48,112},{56,120},{... | collective-permute-start | bytes 1572872 | tf_op jit(solution)/shard_map/ppermute | solution.py:53
  17.7 16.2 %collective-permute-start.3 = (bf16[128,2048]{1,0:T(8,128)(2,1)S(1)}, bf16[128,2048]{1,0:T(8,128)(2,1)S(1)}, u32[]{:S(2)}, u32[]{:S(2)}) collective-permute-start(bf16[128,2048]{1,0:T(8,128)(2,1)S(1)} %get-tuple-element.45), channel_id=1, source_target_pairs={{0,192},{8,200},{16,208},{24,216},{32,224},{40,232},{48,240},{56,2... | collective-permute-start | bytes 1572872 | tf_op jit(solution)/shard_map/ppermute | solution.py:53
  23.2 39.3 %copy-start.1 = (f32[256,256]{1,0:T(8,128)S(1)}, f32[256,256]{1,0:T(8,128)}, u32[]{:S(2)}) copy-start(f32[256,256]{1,0:T(8,128)} %param.7) | copy-start | bytes 786436
  23.2 41.5 %copy-start = (f32[128,128]{1,0:T(8,128)S(1)}, f32[128,128]{1,0:T(8,128)}, u32[]{:S(2)}) copy-start(f32[128,128]{1,0:T(8,128)} %constant.2.clone.refs_7_.refs_6_) | copy-start | bytes 196612
  28.8 29.2 %collective-permute-start.12 = (bf16[128,1024]{1,0:T(8,128)(2,1)S(1)}, bf16[128,1024]{1,0:T(8,128)(2,1)S(1)}, u32[]{:S(2)}, u32[]{:S(2)}) collective-permute-start(bf16[128,1024]{1,0:T(8,128)(2,1)S(1)} %get-tuple-element.60), channel_id=1, source_target_pairs={{0,24},{8,32},{16,40},{24,48},{32,56},{40,0},{48,8},{56,16},{64,88... | collective-permute-start | bytes 786440 | tf_op jit(solution)/shard_map/ppermute | solution.py:53
  33.4 24.5 %collective-permute-start.13 = (bf16[128,1024]{1,0:T(8,128)(2,1)S(1)}, bf16[128,1024]{1,0:T(8,128)(2,1)S(1)}, u32[]{:S(2)}, u32[]{:S(2)}) collective-permute-start(bf16[128,1024]{1,0:T(8,128)(2,1)S(1)} %get-tuple-element.61), channel_id=1, source_target_pairs={{0,40},{8,48},{16,56},{24,0},{32,8},{40,16},{48,24},{56,32},{64,10... | collective-permute-start | bytes 786440 | tf_op jit(solution)/shard_map/ppermute | solution.py:53
  34.1 17.4 %collective-permute-start.4 = (bf16[128,640]{1,0:T(8,128)(2,1)S(1)}, bf16[128,640]{1,0:T(8,128)(2,1)S(1)}, u32[]{:S(2)}, u32[]{:S(2)}) collective-permute-start(bf16[128,640]{1,0:T(8,128)(2,1)S(1)} %get-tuple-element.47), channel_id=1, source_target_pairs={{0,8},{8,16},{16,24},{24,32},{32,40},{40,48},{48,56},{56,0},{64,72... | collective-permute-start | bytes 491528 | tf_op jit(solution)/shard_map/ppermute | solution.py:53
  34.2 18.1 %collective-permute-start.5 = (bf16[128,640]{1,0:T(8,128)(2,1)S(1)}, bf16[128,640]{1,0:T(8,128)(2,1)S(1)}, u32[]{:S(2)}, u32[]{:S(2)}) collective-permute-start(bf16[128,640]{1,0:T(8,128)(2,1)S(1)} %get-tuple-element.48), channel_id=1, source_target_pairs={{0,56},{8,0},{16,8},{24,16},{32,24},{40,32},{48,40},{56,48},{64,12... | collective-permute-start | bytes 491528 | tf_op jit(solution)/shard_map/ppermute | solution.py:53
  52.3 10.2 %collective-permute-start.7 = (bf16[128,256]{1,0:T(8,128)(2,1)S(1)}, bf16[128,256]{1,0:T(8,128)(2,1)S(1)}, u32[]{:S(2)}, u32[]{:S(2)}) collective-permute-start(bf16[128,256]{1,0:T(8,128)(2,1)S(1)} %get-tuple-element.52), channel_id=1, source_target_pairs={{0,40},{8,48},{16,56},{24,0},{32,8},{40,16},{48,24},{56,32},{64,10... | collective-permute-start | bytes 196616 | tf_op jit(solution)/shard_map/ppermute | solution.py:53
  57.4 7.3 %collective-permute-start.6 = (bf16[128,256]{1,0:T(8,128)(2,1)S(1)}, bf16[128,256]{1,0:T(8,128)(2,1)S(1)}, u32[]{:S(2)}, u32[]{:S(2)}) collective-permute-start(bf16[128,256]{1,0:T(8,128)(2,1)S(1)} %get-tuple-element.51.refs_5_), channel_id=1, source_target_pairs={{0,24},{8,32},{16,40},{24,48},{32,56},{40,0},{48,8},{56,16},{64,88... | collective-permute-start | bytes 196616 | tf_op jit(solution)/shard_map/ppermute | solution.py:53
  58.1 12.1 %collective-permute-start.14 = (bf16[128,256]{1,0:T(8,128)(2,1)S(1)}, bf16[128,256]{1,0:T(8,128)(2,1)S(1)}, u32[]{:S(2)}, u32[]{:S(2)}) collective-permute-start(bf16[128,256]{1,0:T(8,128)(2,1)S(1)} %get-tuple-element.63), channel_id=1, source_target_pairs={{0,64},{8,72},{16,80},{24,88},{32,96},{40,104},{48,112},{56,120},{... | collective-permute-start | bytes 196616 | tf_op jit(solution)/shard_map/ppermute | solution.py:53
  58.4 11.8 %collective-permute-start.15 = (bf16[128,256]{1,0:T(8,128)(2,1)S(1)}, bf16[128,256]{1,0:T(8,128)(2,1)S(1)}, u32[]{:S(2)}, u32[]{:S(2)}) collective-permute-start(bf16[128,256]{1,0:T(8,128)(2,1)S(1)} %get-tuple-element.64), channel_id=1, source_target_pairs={{0,128},{8,136},{16,144},{24,152},{32,160},{40,168},{48,176},{56,1... | collective-permute-start | bytes 196616 | tf_op jit(solution)/shard_map/ppermute | solution.py:53
  62.3 7.9 %collective-permute-start.16 = (bf16[128,256]{1,0:T(8,128)(2,1)S(1)}, bf16[128,256]{1,0:T(8,128)(2,1)S(1)}, u32[]{:S(2)}, u32[]{:S(2)}) collective-permute-start(bf16[128,256]{1,0:T(8,128)(2,1)S(1)} %get-tuple-element.65), channel_id=1, source_target_pairs={{0,192},{8,200},{16,208},{24,216},{32,224},{40,232},{48,240},{56,2... | collective-permute-start | bytes 196616 | tf_op jit(solution)/shard_map/ppermute | solution.py:53
  65.0 9.2 %collective-permute-start.9 = (bf16[128,256]{1,0:T(8,128)(2,1)S(1)}, bf16[128,256]{1,0:T(8,128)(2,1)S(1)}, u32[]{:S(2)}, u32[]{:S(2)}) collective-permute-start(bf16[128,256]{1,0:T(8,128)(2,1)S(1)} %get-tuple-element.54.refs_7_.refs_0_), channel_id=1, source_target_pairs={{0,24},{8,32},{16,40},{24,48},{32,56},{40,0},{48,8},{56,16},{64,88... | collective-permute-start | bytes 196616 | tf_op jit(solution)/shard_map/ppermute | solution.py:53
  67.9 6.8 %collective-permute-start.8 = (bf16[128,256]{1,0:T(8,128)(2,1)S(1)}, bf16[128,256]{1,0:T(8,128)(2,1)S(1)}, u32[]{:S(2)}, u32[]{:S(2)}) collective-permute-start(bf16[128,256]{1,0:T(8,128)(2,1)S(1)} %get-tuple-element.54.refs_7_.refs_0_), channel_id=1, source_target_pairs={{0,40},{8,48},{16,56},{24,0},{32,8},{40,16},{48,24},{56,32},{64,10... | collective-permute-start | bytes 196616 | tf_op jit(solution)/shard_map/ppermute | solution.py:53
  70.5 7.4 %collective-permute-start.21 = (bf16[128,256]{1,0:T(8,128)(2,1)S(1)}, bf16[128,256]{1,0:T(8,128)(2,1)S(1)}, u32[]{:S(2)}, u32[]{:S(2)}) collective-permute-start(bf16[128,256]{1,0:T(8,128)(2,1)S(1)} %get-tuple-element.67.refs_3_.refs_0_), channel_id=1, source_target_pairs={{0,192},{8,200},{16,208},{24,216},{32,224},{40,232},{48,240},{56,2... | collective-permute-start | bytes 196616 | tf_op jit(solution)/shard_map/ppermute | solution.py:53
  73.2 5.9 %collective-permute-start.20 = (bf16[128,256]{1,0:T(8,128)(2,1)S(1)}, bf16[128,256]{1,0:T(8,128)(2,1)S(1)}, u32[]{:S(2)}, u32[]{:S(2)}) collective-permute-start(bf16[128,256]{1,0:T(8,128)(2,1)S(1)} %get-tuple-element.67.refs_3_.refs_0_), channel_id=1, source_target_pairs={{0,128},{8,136},{16,144},{24,152},{32,160},{40,168},{48,176},{56,1... | collective-permute-start | bytes 196616 | tf_op jit(solution)/shard_map/ppermute | solution.py:53
  73.2 6.2 %collective-permute-start.19 = (bf16[128,256]{1,0:T(8,128)(2,1)S(1)}, bf16[128,256]{1,0:T(8,128)(2,1)S(1)}, u32[]{:S(2)}, u32[]{:S(2)}) collective-permute-start(bf16[128,256]{1,0:T(8,128)(2,1)S(1)} %get-tuple-element.67.refs_3_.refs_0_), channel_id=1, source_target_pairs={{0,64},{8,72},{16,80},{24,88},{32,96},{40,104},{48,112},{56,120},{... | collective-permute-start | bytes 196616 | tf_op jit(solution)/shard_map/ppermute | solution.py:53
  74.8 9.8 %collective-permute-start.18 = (bf16[128,640]{1,0:T(8,128)(2,1)S(1)}, bf16[128,640]{1,0:T(8,128)(2,1)S(1)}, u32[]{:S(2)}, u32[]{:S(2)}) collective-permute-start(bf16[128,640]{1,0:T(8,128)(2,1)S(1)} %get-tuple-element.69), channel_id=1, source_target_pairs={{0,56},{8,0},{16,8},{24,16},{32,24},{40,32},{48,40},{56,48},{64,12... | collective-permute-start | bytes 491528 | tf_op jit(solution)/shard_map/ppermute | solution.py:53
  77.9 11.0 %collective-permute-start.17 = (bf16[128,640]{1,0:T(8,128)(2,1)S(1)}, bf16[128,640]{1,0:T(8,128)(2,1)S(1)}, u32[]{:S(2)}, u32[]{:S(2)}) collective-permute-start(bf16[128,640]{1,0:T(8,128)(2,1)S(1)} %get-tuple-element.68.refs_4_), channel_id=1, source_target_pairs={{0,8},{8,16},{16,24},{24,32},{32,40},{40,48},{48,56},{56,0},{64,72... | collective-permute-start | bytes 491528 | tf_op jit(solution)/shard_map/ppermute | solution.py:53
  79.4 18.8 %collective-permute-start.25 = (bf16[128,1024]{1,0:T(8,128)(2,1)S(1)}, bf16[128,1024]{1,0:T(8,128)(2,1)S(1)}, u32[]{:S(2)}, u32[]{:S(2)}) collective-permute-start(bf16[128,1024]{1,0:T(8,128)(2,1)S(1)} %join_b.1.refs_5_.refs_0_.refs_3_), channel_id=1, source_target_pairs={{0,24},{8,32},{16,40},{24,48},{32,56},{40,0},{48,8},{56,16},{64,88... | collective-permute-start | bytes 786440 | tf_op jit(solution)/shard_map/ppermute | solution.py:53
  83.5 16.9 %collective-permute-start.24 = (bf16[128,1024]{1,0:T(8,128)(2,1)S(1)}, bf16[128,1024]{1,0:T(8,128)(2,1)S(1)}, u32[]{:S(2)}, u32[]{:S(2)}) collective-permute-start(bf16[128,1024]{1,0:T(8,128)(2,1)S(1)} %join_b.1.refs_5_.refs_0_.refs_3_), channel_id=1, source_target_pairs={{0,40},{8,48},{16,56},{24,0},{32,8},{40,16},{48,24},{56,32},{64,10... | collective-permute-start | bytes 786440 | tf_op jit(solution)/shard_map/ppermute | solution.py:53
  88.9 14.6 %collective-permute-start.23 = (bf16[128,2048]{1,0:T(8,128)(2,1)S(1)}, bf16[128,2048]{1,0:T(8,128)(2,1)S(1)}, u32[]{:S(2)}, u32[]{:S(2)}) collective-permute-start(bf16[128,2048]{1,0:T(8,128)(2,1)S(1)} %join_row_a.1.refs_3_.refs_0_), channel_id=1, source_target_pairs={{0,192},{8,200},{16,208},{24,216},{32,224},{40,232},{48,240},{56,2... | collective-permute-start | bytes 1572872 | tf_op jit(solution)/shard_map/ppermute | solution.py:53
  89.9 13.6 %collective-permute-start.22 = (bf16[128,2048]{1,0:T(8,128)(2,1)S(1)}, bf16[128,2048]{1,0:T(8,128)(2,1)S(1)}, u32[]{:S(2)}, u32[]{:S(2)}) collective-permute-start(bf16[128,2048]{1,0:T(8,128)(2,1)S(1)} %join_row_a.1.refs_3_.refs_0_), channel_id=1, source_target_pairs={{0,64},{8,72},{16,80},{24,88},{32,96},{40,104},{48,112},{56,120},{... | collective-permute-start | bytes 1572872 | tf_op jit(solution)/shard_map/ppermute | solution.py:53
  100.5 12.7 %collective-permute-start.29 = (bf16[128,2560]{1,0:T(8,128)(2,1)S(1)}, bf16[128,2560]{1,0:T(8,128)(2,1)S(1)}, u32[]{:S(2)}, u32[]{:S(2)}) collective-permute-start(bf16[128,2560]{1,0:T(8,128)(2,1)S(1)} %get-tuple-element.73), channel_id=1, source_target_pairs={{0,56},{8,0},{16,8},{24,16},{32,24},{40,32},{48,40},{56,48},{64,12... | collective-permute-start | bytes 1966088 | tf_op jit(solution)/shard_map/ppermute | solution.py:53
  100.5 14.2 %collective-permute-start.28 = (bf16[128,2560]{1,0:T(8,128)(2,1)S(1)}, bf16[128,2560]{1,0:T(8,128)(2,1)S(1)}, u32[]{:S(2)}, u32[]{:S(2)}) collective-permute-start(bf16[128,2560]{1,0:T(8,128)(2,1)S(1)} %get-tuple-element.70.refs_2_), channel_id=1, source_target_pairs={{0,8},{8,16},{16,24},{24,32},{32,40},{40,48},{48,56},{56,0},{64,72... | collective-permute-start | bytes 1966088 | tf_op jit(solution)/shard_map/ppermute | solution.py:53
  103.6 11.1 %collective-permute-start.26 = (bf16[128,1024]{1,0:T(8,128)(2,1)S(1)}, bf16[128,1024]{1,0:T(8,128)(2,1)S(1)}, u32[]{:S(2)}, u32[]{:S(2)}) collective-permute-start(bf16[128,1024]{1,0:T(8,128)(2,1)S(1)} %get-tuple-element.71), channel_id=1, source_target_pairs={{0,64},{8,72},{16,80},{24,88},{32,96},{40,104},{48,112},{56,120},{... | collective-permute-start | bytes 786440 | tf_op jit(solution)/shard_map/ppermute | solution.py:53
  103.7 11.0 %collective-permute-start.27 = (bf16[128,1024]{1,0:T(8,128)(2,1)S(1)}, bf16[128,1024]{1,0:T(8,128)(2,1)S(1)}, u32[]{:S(2)}, u32[]{:S(2)}) collective-permute-start(bf16[128,1024]{1,0:T(8,128)(2,1)S(1)} %get-tuple-element.72), channel_id=1, source_target_pairs={{0,192},{8,200},{16,208},{24,216},{32,224},{40,232},{48,240},{56,2... | collective-permute-start | bytes 786440 | tf_op jit(solution)/shard_map/ppermute | solution.py:53

commit v4 on v3

--- a/solution.py
+++ b/solution.py
@@ -374,7 +374,7 @@
     )
     from_minus_b, from_plus_b = shift(plus_b, 0, 1), shift(minus_b, 0, -1)
     low, high = join(
-        (((0, 0, 1024),), ((1, 1024, 1024),)), m1, p1, after=(plus_b,), name="relay_row_a"
+        (((0, 0, 1024),), ((1, 1024, 1024),)), m1, p1, name="relay_row_a"
     )
     low, high = shift(low, 1, 0), shift(high, -1, 0)
     new_momentum = jnp.concatenate([momentum_a, momentum_b], axis=0)

time: 119 us -> 118 us (level)
  no operation moved by 1% of the time
where the time goes in v4:
time: 118 us; the launch traced here: 116 us
  starting transfers between devices  56.4 us (48%)
  waiting for transfers between devices  42.7 us (36%)
  Pallas kernels  15.6 us (13%)
    ppermute x30, starting transfers between devices, shift(): return lax.ppermute(value, 'replica', pairs)  56.4 us
    ppermute x30, waiting for transfers between devices, shift(): return lax.ppermute(value, 'replica', pairs)  42.7 us
    pallas_call x4, Pallas kernels, contribute(): pl.pallas_call(functools.partial(contribute_kernel, jobs, len(after)), ou...  10.1 us
    pallas_call x2, Pallas kernels, assemble(): pl.pallas_call(functools.partial(assemble_kernel, plan), out_shape=jax.Sh...  3.99 us
  transfers between devices with their start and end apart: 30, of which 12 were waited for; matrix products, arithmetic and copies ran while one was open for 1% of the time, Pallas kernels for 10%

profile of v4, /device:TPU:16, one launch (start us, length us, event | category | flops | bytes accessed | tf_op | source)
XLA Modules:
  0.0 116.5 jit_solution(9107042787681643756)
XLA Ops:
  0.6 1.9 %contribute.6 = (bf16[128,1024]{1,0:T(8,128)(2,1)S(1)}, bf16[128,1024]{1,0:T(8,128)(2,1)S(1)}) custom-call(bf16[1,256,8192]{2,1,0:T(8,128)(2,1)} %local.7, bf16[256,8192]{1,0:T(8,128)(2,1)} %base.7), custom_call_target="tpu_custom_call" | custom-call | flops 268435456 | bytes 1572864 | tf_op jit(solution)/shard_map/contribute/pallas_call | solution.py:129
  2.5 2.8 %collective-permute-start.1 = (bf16[128,1024]{1,0:T(8,128)(2,1)S(1)}, bf16[128,1024]{1,0:T(8,128)(2,1)S(1)}, u32[]{:S(2)}, u32[]{:S(2)}) collective-permute-start(bf16[128,1024]{1,0:T(8,128)(2,1)S(1)} %get-tuple-element.43), channel_id=1, source_target_pairs={{0,192},{8,200},{16,208},{24,216},{32,224},{40,232},{48,240},{56,2... | collective-permute-start | bytes 786440 | tf_op jit(solution)/shard_map/ppermute | solution.py:53
  5.3 2.9 %contribute.7 = (bf16[128,2560]{1,0:T(8,128)(2,1)S(1)}, bf16[128,2560]{1,0:T(8,128)(2,1)S(1)}) custom-call(bf16[1,256,8192]{2,1,0:T(8,128)(2,1)} %local.7, bf16[256,8192]{1,0:T(8,128)(2,1)} %base.7, bf16[128,1024]{1,0:T(8,128)(2,1)S(1)} %get-tuple-element.42.rest_0_), custom_call_target="tpu_custom_call" | custom-call | flops 671088640 | bytes 3932160 | tf_op jit(solution)/shard_map/contribute/pallas_call | solution.py:129
  8.2 2.0 %collective-permute-start.10 = (bf16[128,2560]{1,0:T(8,128)(2,1)S(1)}, bf16[128,2560]{1,0:T(8,128)(2,1)S(1)}, u32[]{:S(2)}, u32[]{:S(2)}) collective-permute-start(bf16[128,2560]{1,0:T(8,128)(2,1)S(1)} %get-tuple-element.56), channel_id=1, source_target_pairs={{0,8},{8,16},{16,24},{24,32},{32,40},{40,48},{48,56},{56,0},{64,72... | collective-permute-start | bytes 1966088 | tf_op jit(solution)/shard_map/ppermute | solution.py:53
  10.2 4.0 %collective-permute-start.11 = (bf16[128,2560]{1,0:T(8,128)(2,1)S(1)}, bf16[128,2560]{1,0:T(8,128)(2,1)S(1)}, u32[]{:S(2)}, u32[]{:S(2)}) collective-permute-start(bf16[128,2560]{1,0:T(8,128)(2,1)S(1)} %get-tuple-element.57), channel_id=1, source_target_pairs={{0,56},{8,0},{16,8},{24,16},{32,24},{40,32},{48,40},{56,48},{64,12... | collective-permute-start | bytes 1966088 | tf_op jit(solution)/shard_map/ppermute | solution.py:53
  14.2 2.5 %contribute.5 = (bf16[128,2048]{1,0:T(8,128)(2,1)S(1)}, bf16[128,2048]{1,0:T(8,128)(2,1)S(1)}) custom-call(bf16[1,256,8192]{2,1,0:T(8,128)(2,1)} %local.7, bf16[256,8192]{1,0:T(8,128)(2,1)} %base.7), custom_call_target="tpu_custom_call" | custom-call | flops 536870912 | bytes 3145728 | tf_op jit(solution)/shard_map/contribute/pallas_call | solution.py:129
  16.9 0.8 collective-permute-start.2
  17.7 2.6 %collective-permute-start.3 = (bf16[128,2048]{1,0:T(8,128)(2,1)S(1)}, bf16[128,2048]{1,0:T(8,128)(2,1)S(1)}, u32[]{:S(2)}, u32[]{:S(2)}) collective-permute-start(bf16[128,2048]{1,0:T(8,128)(2,1)S(1)} %get-tuple-element.45), channel_id=1, source_target_pairs={{0,192},{8,200},{16,208},{24,216},{32,224},{40,232},{48,240},{56,2... | collective-permute-start | bytes 1572872 | tf_op jit(solution)/shard_map/ppermute | solution.py:53
  20.3 2.9 %contribute.4 = (bf16[128,2048]{1,0:T(8,128)(2,1)S(1)}, bf16[128,256]{1,0:T(8,128)(2,1)S(1)}, bf16[128,1024]{1,0:T(8,128)(2,1)S(1)}, bf16[128,1024]{1,0:T(8,128)...) custom-call(bf16[1,256,8192]{2,1,0:T(8,128)(2,1)} %local.7, bf16[256,8192]{1,0:T(8,128)(2,1)} %base.7), custom_call_target="tpu_custom_call" | custom-call | flops 671088640 | bytes 3932160 | tf_op jit(solution)/shard_map/contribute/pallas_call | solution.py:129
  23.2 5.4 %collective-permute-done.10.refs_2_.refs_1_ = bf16[128,2560]{1,0:T(8,128)(2,1)S(1)} collective-permute-done((bf16[128,2560]{1,0:T(8,128)(2,1)S(1)}, bf16[128,2560]{1,0:T(8,128)(2,1)S(1)}, u32[]{:S(2)}, u32[]{:S(2)}) %collective-permute-start.10) | collective-permute-done | bytes 655392 | tf_op jit(solution)/shard_map/ppermute | solution.py:53
  28.8 4.6 %collective-permute-start.12 = (bf16[128,1024]{1,0:T(8,128)(2,1)S(1)}, bf16[128,1024]{1,0:T(8,128)(2,1)S(1)}, u32[]{:S(2)}, u32[]{:S(2)}) collective-permute-start(bf16[128,1024]{1,0:T(8,128)(2,1)S(1)} %get-tuple-element.60), channel_id=1, source_target_pairs={{0,24},{8,32},{16,40},{24,48},{32,56},{40,0},{48,8},{56,16},{64,88... | collective-permute-start | bytes 786440 | tf_op jit(solution)/shard_map/ppermute | solution.py:53
  33.4 0.5 collective-permute-start.13
  33.9 0.2 sum_a.1
  34.2 3.2 %collective-permute-start.5 = (bf16[128,640]{1,0:T(8,128)(2,1)S(1)}, bf16[128,640]{1,0:T(8,128)(2,1)S(1)}, u32[]{:S(2)}, u32[]{:S(2)}) collective-permute-start(bf16[128,640]{1,0:T(8,128)(2,1)S(1)} %get-tuple-element.48), channel_id=1, source_target_pairs={{0,56},{8,0},{16,8},{24,16},{32,24},{40,32},{48,40},{56,48},{64,12... | collective-permute-start | bytes 491528 | tf_op jit(solution)/shard_map/ppermute | solution.py:53
  37.4 14.1 %collective-permute-done.4.refs_2_.refs_1_ = bf16[128,640]{1,0:T(8,128)(2,1)S(1)} collective-permute-done((bf16[128,640]{1,0:T(8,128)(2,1)S(1)}, bf16[128,640]{1,0:T(8,128)(2,1)S(1)}, u32[]{:S(2)}, u32[]{:S(2)}) %collective-permute-start.4) | collective-permute-done | bytes 163872 | tf_op jit(solution)/shard_map/ppermute | solution.py:53
  51.5 0.8 collective-permute-done.5.refs_3_.refs_2_
  52.3 5.1 %collective-permute-start.7 = (bf16[128,256]{1,0:T(8,128)(2,1)S(1)}, bf16[128,256]{1,0:T(8,128)(2,1)S(1)}, u32[]{:S(2)}, u32[]{:S(2)}) collective-permute-start(bf16[128,256]{1,0:T(8,128)(2,1)S(1)} %get-tuple-element.52), channel_id=1, source_target_pairs={{0,40},{8,48},{16,56},{24,0},{32,8},{40,16},{48,24},{56,32},{64,10... | collective-permute-start | bytes 196616 | tf_op jit(solution)/shard_map/ppermute | solution.py:53
  57.4 0.5 collective-permute-start.6
  57.9 0.2 sum_b.1
  58.1 0.3 collective-permute-start.14
  58.4 4.0 %collective-permute-start.15 = (bf16[128,256]{1,0:T(8,128)(2,1)S(1)}, bf16[128,256]{1,0:T(8,128)(2,1)S(1)}, u32[]{:S(2)}, u32[]{:S(2)}) collective-permute-start(bf16[128,256]{1,0:T(8,128)(2,1)S(1)} %get-tuple-element.64), channel_id=1, source_target_pairs={{0,128},{8,136},{16,144},{24,152},{32,160},{40,168},{48,176},{56,1... | collective-permute-start | bytes 196616 | tf_op jit(solution)/shard_map/ppermute | solution.py:53
  62.3 0.2 collective-permute-start.16
  62.6 2.2 %collective-permute-done.6.refs_3_ = bf16[128,256]{1,0:T(8,128)(2,1)S(1)} collective-permute-done((bf16[128,256]{1,0:T(8,128)(2,1)S(1)}, bf16[128,256]{1,0:T(8,128)(2,1)S(1)}, u32[]{:S(2)}, u32[]{:S(2)}) %collective-permute-start.6) | collective-permute-done | bytes 65568 | tf_op jit(solution)/shard_map/ppermute | solution.py:53
  64.7 0.3 update.2
  65.0 2.9 %collective-permute-start.9 = (bf16[128,256]{1,0:T(8,128)(2,1)S(1)}, bf16[128,256]{1,0:T(8,128)(2,1)S(1)}, u32[]{:S(2)}, u32[]{:S(2)}) collective-permute-start(bf16[128,256]{1,0:T(8,128)(2,1)S(1)} %get-tuple-element.54.refs_7_.refs_0_), channel_id=1, source_target_pairs={{0,24},{8,32},{16,40},{24,48},{32,56},{40,0},{48,8},{56,16},{64,88... | collective-permute-start | bytes 196616 | tf_op jit(solution)/shard_map/ppermute | solution.py:53
  67.9 2.2 %collective-permute-start.8 = (bf16[128,256]{1,0:T(8,128)(2,1)S(1)}, bf16[128,256]{1,0:T(8,128)(2,1)S(1)}, u32[]{:S(2)}, u32[]{:S(2)}) collective-permute-start(bf16[128,256]{1,0:T(8,128)(2,1)S(1)} %get-tuple-element.54.refs_7_.refs_0_), channel_id=1, source_target_pairs={{0,40},{8,48},{16,56},{24,0},{32,8},{40,16},{48,24},{56,32},{64,10... | collective-permute-start | bytes 196616 | tf_op jit(solution)/shard_map/ppermute | solution.py:53
  70.2 0.3 update.3
  70.5 2.8 %collective-permute-start.21 = (bf16[128,256]{1,0:T(8,128)(2,1)S(1)}, bf16[128,256]{1,0:T(8,128)(2,1)S(1)}, u32[]{:S(2)}, u32[]{:S(2)}) collective-permute-start(bf16[128,256]{1,0:T(8,128)(2,1)S(1)} %get-tuple-element.67.refs_3_.refs_0_), channel_id=1, source_target_pairs={{0,192},{8,200},{16,208},{24,216},{32,224},{40,232},{48,240},{56,2... | collective-permute-start | bytes 196616 | tf_op jit(solution)/shard_map/ppermute | solution.py:53
  73.2 1.0 collective-permute-start.19
  74.2 0.6 collective-permute-done.8.refs_1_
  74.8 3.1 %collective-permute-start.18 = (bf16[128,640]{1,0:T(8,128)(2,1)S(1)}, bf16[128,640]{1,0:T(8,128)(2,1)S(1)}, u32[]{:S(2)}, u32[]{:S(2)}) collective-permute-start(bf16[128,640]{1,0:T(8,128)(2,1)S(1)} %get-tuple-element.69), channel_id=1, source_target_pairs={{0,56},{8,0},{16,8},{24,16},{32,24},{40,32},{48,40},{56,48},{64,12... | collective-permute-start | bytes 491528 | tf_op jit(solution)/shard_map/ppermute | solution.py:53
  77.9 1.2 %collective-permute-done.20.refs_2_ = bf16[128,256]{1,0:T(8,128)(2,1)S(1)} collective-permute-done((bf16[128,256]{1,0:T(8,128)(2,1)S(1)}, bf16[128,256]{1,0:T(8,128)(2,1)S(1)}, u32[]{:S(2)}, u32[]{:S(2)}) %collective-permute-start.20) | collective-permute-done | bytes 65568 | tf_op jit(solution)/shard_map/ppermute | solution.py:53
  79.1 0.3 collective-permute-done.19.refs_1_
  79.4 4.0 %collective-permute-start.27 = (bf16[128,1024]{1,0:T(8,128)(2,1)S(1)}, bf16[128,1024]{1,0:T(8,128)(2,1)S(1)}, u32[]{:S(2)}, u32[]{:S(2)}) collective-permute-start(bf16[128,1024]{1,0:T(8,128)(2,1)S(1)} %join_b.1.refs_5_.refs_0_.refs_3_), channel_id=1, source_target_pairs={{0,24},{8,32},{16,40},{24,48},{32,56},{40,0},{48,8},{56,16},{64,88... | collective-permute-start | bytes 786440 | tf_op jit(solution)/shard_map/ppermute | solution.py:53
  83.5 1.1 collective-permute-start.26
  84.6 4.3 %collective-permute-done.17.refs_3_ = bf16[128,640]{1,0:T(8,128)(2,1)S(1)} collective-permute-done((bf16[128,640]{1,0:T(8,128)(2,1)S(1)}, bf16[128,640]{1,0:T(8,128)(2,1)S(1)}, u32[]{:S(2)}, u32[]{:S(2)}) %collective-permute-start.17) | collective-permute-done | bytes 163872 | tf_op jit(solution)/shard_map/ppermute | solution.py:53
  88.9 1.0 collective-permute-start.23
  89.9 1.1 collective-permute-start.22
  91.1 7.1 %collective-permute-done.27.refs_2_.refs_5_ = bf16[128,1024]{1,0:T(8,128)(2,1)S(1)} collective-permute-done((bf16[128,1024]{1,0:T(8,128)(2,1)S(1)}, bf16[128,1024]{1,0:T(8,128)(2,1)S(1)}, u32[]{:S(2)}, u32[]{:S(2)}) %collective-permute-start.27) | collective-permute-done | bytes 262176 | tf_op jit(solution)/shard_map/ppermute | solution.py:53
  98.2 2.4 %collective-permute-done.26.refs_1_.refs_4_ = bf16[128,1024]{1,0:T(8,128)(2,1)S(1)} collective-permute-done((bf16[128,1024]{1,0:T(8,128)(2,1)S(1)}, bf16[128,1024]{1,0:T(8,128)(2,1)S(1)}, u32[]{:S(2)}, u32[]{:S(2)}) %collective-permute-start.26) | collective-permute-done | bytes 262176 | tf_op jit(solution)/shard_map/ppermute | solution.py:53
  100.7 0.3 collective-permute-start.28
  101.0 3.0 %collective-permute-start.29 = (bf16[128,2560]{1,0:T(8,128)(2,1)S(1)}, bf16[128,2560]{1,0:T(8,128)(2,1)S(1)}, u32[]{:S(2)}, u32[]{:S(2)}) collective-permute-start(bf16[128,2560]{1,0:T(8,128)(2,1)S(1)} %get-tuple-element.73), channel_id=1, source_target_pairs={{0,56},{8,0},{16,8},{24,16},{32,24},{40,32},{48,40},{56,48},{64,12... | collective-permute-start | bytes 1966088 | tf_op jit(solution)/shard_map/ppermute | solution.py:53
  104.2 3.2 %collective-permute-start.25 = (bf16[128,1024]{1,0:T(8,128)(2,1)S(1)}, bf16[128,1024]{1,0:T(8,128)(2,1)S(1)}, u32[]{:S(2)}, u32[]{:S(2)}) collective-permute-start(bf16[128,1024]{1,0:T(8,128)(2,1)S(1)} %get-tuple-element.71), channel_id=1, source_target_pairs={{0,192},{8,200},{16,208},{24,216},{32,224},{40,232},{48,240},{56,2... | collective-permute-start | bytes 786440 | tf_op jit(solution)/shard_map/ppermute | solution.py:53
  107.4 0.7 pad_maximum_fusion
  108.1 2.1 %assemble.2.refs_4_ = bf16[256,8192]{1,0:T(8,128)(2,1)} custom-call(bf16[128,2048]{1,0:T(8,128)(2,1)S(1)} %join_row_a.1.refs_3_.refs_0_, bf16[128,2048]{1,0:T(8,128)(2,1)S(1)} %collective-permute-done.22.refs_0_.refs_1_, bf16[128,2048]{1,0:T(8,128)(2,1)S(1)} %collective-permute-done.23.refs_1_.refs_2_, bf16[128,1024]{1,0:T(8,128)(2,1)S(1)} %join_b.1.refs_5_.refs_0_.refs_3_, ...), custom_call_target="tpu_custom_call" | custom-call | bytes 4194304 | tf_op jit(solution)/shard_map/assemble/pallas_call | solution.py:284
  110.2 2.9 %collective-permute-done.28.refs_2_ = bf16[128,2560]{1,0:T(8,128)(2,1)S(1)} collective-permute-done((bf16[128,2560]{1,0:T(8,128)(2,1)S(1)}, bf16[128,2560]{1,0:T(8,128)(2,1)S(1)}, u32[]{:S(2)}, u32[]{:S(2)}) %collective-permute-start.28) | collective-permute-done | bytes 655392 | tf_op jit(solution)/shard_map/ppermute | solution.py:53
  113.1 1.3 %collective-permute-done.29.refs_3_ = bf16[128,2560]{1,0:T(8,128)(2,1)S(1)} collective-permute-done((bf16[128,2560]{1,0:T(8,128)(2,1)S(1)}, bf16[128,2560]{1,0:T(8,128)(2,1)S(1)}, u32[]{:S(2)}, u32[]{:S(2)}) %collective-permute-start.29) | collective-permute-done | bytes 655392 | tf_op jit(solution)/shard_map/ppermute | solution.py:53
  114.4 1.9 %assemble.3 = bf16[256,8192]{1,0:T(8,128)(2,1)} custom-call(bf16[128,1024]{1,0:T(8,128)(2,1)S(1)} %collective-permute-done.24.refs_0_, bf16[128,1024]{1,0:T(8,128)(2,1)S(1)} %collective-permute-done.25.refs_1_, bf16[128,2560]{1,0:T(8,128)(2,1)S(1)} %collective-permute-done.28.refs_2_, ...), custom_call_target="tpu_custom_call", output_to_operand_aliasing={{}: (4, {})} | custom-call | bytes 4194304 | tf_op jit(solution)/shard_map/assemble/pallas_call | solution.py:284
  (36 shorter events, 0.8 us)
Async XLA Ops:
  2.5 14.2 %collective-permute-start.1 = (bf16[128,1024]{1,0:T(8,128)(2,1)S(1)}, bf16[128,1024]{1,0:T(8,128)(2,1)S(1)}, u32[]{:S(2)}, u32[]{:S(2)}) collective-permute-start(bf16[128,1024]{1,0:T(8,128)(2,1)S(1)} %get-tuple-element.43), channel_id=1, source_target_pairs={{0,192},{8,200},{16,208},{24,216},{32,224},{40,232},{48,240},{56,2... | collective-permute-start | bytes 786440 | tf_op jit(solution)/shard_map/ppermute | solution.py:53
  5.3 11.4 %collective-permute-start = (bf16[128,1024]{1,0:T(8,128)(2,1)S(1)}, bf16[128,1024]{1,0:T(8,128)(2,1)S(1)}, u32[]{:S(2)}, u32[]{:S(2)}) collective-permute-start(bf16[128,1024]{1,0:T(8,128)(2,1)S(1)} %get-tuple-element.42.rest_0_), channel_id=1, source_target_pairs={{0,64},{8,72},{16,80},{24,88},{32,96},{40,104},{48,112},{56,120},{... | collective-permute-start | bytes 786440 | tf_op jit(solution)/shard_map/ppermute | solution.py:53
  8.2 20.4 %collective-permute-start.10 = (bf16[128,2560]{1,0:T(8,128)(2,1)S(1)}, bf16[128,2560]{1,0:T(8,128)(2,1)S(1)}, u32[]{:S(2)}, u32[]{:S(2)}) collective-permute-start(bf16[128,2560]{1,0:T(8,128)(2,1)S(1)} %get-tuple-element.56), channel_id=1, source_target_pairs={{0,8},{8,16},{16,24},{24,32},{32,40},{40,48},{48,56},{56,0},{64,72... | collective-permute-start | bytes 1966088 | tf_op jit(solution)/shard_map/ppermute | solution.py:53
  10.2 18.4 %collective-permute-start.11 = (bf16[128,2560]{1,0:T(8,128)(2,1)S(1)}, bf16[128,2560]{1,0:T(8,128)(2,1)S(1)}, u32[]{:S(2)}, u32[]{:S(2)}) collective-permute-start(bf16[128,2560]{1,0:T(8,128)(2,1)S(1)} %get-tuple-element.57), channel_id=1, source_target_pairs={{0,56},{8,0},{16,8},{24,16},{32,24},{40,32},{48,40},{56,48},{64,12... | collective-permute-start | bytes 1966088 | tf_op jit(solution)/shard_map/ppermute | solution.py:53
  16.9 17.0 %collective-permute-start.2 = (bf16[128,2048]{1,0:T(8,128)(2,1)S(1)}, bf16[128,2048]{1,0:T(8,128)(2,1)S(1)}, u32[]{:S(2)}, u32[]{:S(2)}) collective-permute-start(bf16[128,2048]{1,0:T(8,128)(2,1)S(1)} %get-tuple-element.44), channel_id=1, source_target_pairs={{0,64},{8,72},{16,80},{24,88},{32,96},{40,104},{48,112},{56,120},{... | collective-permute-start | bytes 1572872 | tf_op jit(solution)/shard_map/ppermute | solution.py:53
  17.7 16.2 %collective-permute-start.3 = (bf16[128,2048]{1,0:T(8,128)(2,1)S(1)}, bf16[128,2048]{1,0:T(8,128)(2,1)S(1)}, u32[]{:S(2)}, u32[]{:S(2)}) collective-permute-start(bf16[128,2048]{1,0:T(8,128)(2,1)S(1)} %get-tuple-element.45), channel_id=1, source_target_pairs={{0,192},{8,200},{16,208},{24,216},{32,224},{40,232},{48,240},{56,2... | collective-permute-start | bytes 1572872 | tf_op jit(solution)/shard_map/ppermute | solution.py:53
  23.2 39.3 %copy-start.1 = (f32[256,256]{1,0:T(8,128)S(1)}, f32[256,256]{1,0:T(8,128)}, u32[]{:S(2)}) copy-start(f32[256,256]{1,0:T(8,128)} %param.7) | copy-start | bytes 786436
  23.2 41.5 %copy-start = (f32[128,128]{1,0:T(8,128)S(1)}, f32[128,128]{1,0:T(8,128)}, u32[]{:S(2)}) copy-start(f32[128,128]{1,0:T(8,128)} %constant.2.clone.refs_7_.refs_6_) | copy-start | bytes 196612
  28.8 29.2 %collective-permute-start.12 = (bf16[128,1024]{1,0:T(8,128)(2,1)S(1)}, bf16[128,1024]{1,0:T(8,128)(2,1)S(1)}, u32[]{:S(2)}, u32[]{:S(2)}) collective-permute-start(bf16[128,1024]{1,0:T(8,128)(2,1)S(1)} %get-tuple-element.60), channel_id=1, source_target_pairs={{0,24},{8,32},{16,40},{24,48},{32,56},{40,0},{48,8},{56,16},{64,88... | collective-permute-start | bytes 786440 | tf_op jit(solution)/shard_map/ppermute | solution.py:53
  33.4 24.5 %collective-permute-start.13 = (bf16[128,1024]{1,0:T(8,128)(2,1)S(1)}, bf16[128,1024]{1,0:T(8,128)(2,1)S(1)}, u32[]{:S(2)}, u32[]{:S(2)}) collective-permute-start(bf16[128,1024]{1,0:T(8,128)(2,1)S(1)} %get-tuple-element.61), channel_id=1, source_target_pairs={{0,40},{8,48},{16,56},{24,0},{32,8},{40,16},{48,24},{56,32},{64,10... | collective-permute-start | bytes 786440 | tf_op jit(solution)/shard_map/ppermute | solution.py:53
  34.1 17.4 %collective-permute-start.4 = (bf16[128,640]{1,0:T(8,128)(2,1)S(1)}, bf16[128,640]{1,0:T(8,128)(2,1)S(1)}, u32[]{:S(2)}, u32[]{:S(2)}) collective-permute-start(bf16[128,640]{1,0:T(8,128)(2,1)S(1)} %get-tuple-element.47), channel_id=1, source_target_pairs={{0,8},{8,16},{16,24},{24,32},{32,40},{40,48},{48,56},{56,0},{64,72... | collective-permute-start | bytes 491528 | tf_op jit(solution)/shard_map/ppermute | solution.py:53
  34.2 18.1 %collective-permute-start.5 = (bf16[128,640]{1,0:T(8,128)(2,1)S(1)}, bf16[128,640]{1,0:T(8,128)(2,1)S(1)}, u32[]{:S(2)}, u32[]{:S(2)}) collective-permute-start(bf16[128,640]{1,0:T(8,128)(2,1)S(1)} %get-tuple-element.48), channel_id=1, source_target_pairs={{0,56},{8,0},{16,8},{24,16},{32,24},{40,32},{48,40},{56,48},{64,12... | collective-permute-start | bytes 491528 | tf_op jit(solution)/shard_map/ppermute | solution.py:53
  52.3 10.2 %collective-permute-start.7 = (bf16[128,256]{1,0:T(8,128)(2,1)S(1)}, bf16[128,256]{1,0:T(8,128)(2,1)S(1)}, u32[]{:S(2)}, u32[]{:S(2)}) collective-permute-start(bf16[128,256]{1,0:T(8,128)(2,1)S(1)} %get-tuple-element.52), channel_id=1, source_target_pairs={{0,40},{8,48},{16,56},{24,0},{32,8},{40,16},{48,24},{56,32},{64,10... | collective-permute-start | bytes 196616 | tf_op jit(solution)/shard_map/ppermute | solution.py:53
  57.4 7.3 %collective-permute-start.6 = (bf16[128,256]{1,0:T(8,128)(2,1)S(1)}, bf16[128,256]{1,0:T(8,128)(2,1)S(1)}, u32[]{:S(2)}, u32[]{:S(2)}) collective-permute-start(bf16[128,256]{1,0:T(8,128)(2,1)S(1)} %get-tuple-element.51.refs_5_), channel_id=1, source_target_pairs={{0,24},{8,32},{16,40},{24,48},{32,56},{40,0},{48,8},{56,16},{64,88... | collective-permute-start | bytes 196616 | tf_op jit(solution)/shard_map/ppermute | solution.py:53
  58.1 12.1 %collective-permute-start.14 = (bf16[128,256]{1,0:T(8,128)(2,1)S(1)}, bf16[128,256]{1,0:T(8,128)(2,1)S(1)}, u32[]{:S(2)}, u32[]{:S(2)}) collective-permute-start(bf16[128,256]{1,0:T(8,128)(2,1)S(1)} %get-tuple-element.63), channel_id=1, source_target_pairs={{0,64},{8,72},{16,80},{24,88},{32,96},{40,104},{48,112},{56,120},{... | collective-permute-start | bytes 196616 | tf_op jit(solution)/shard_map/ppermute | solution.py:53
  58.4 11.8 %collective-permute-start.15 = (bf16[128,256]{1,0:T(8,128)(2,1)S(1)}, bf16[128,256]{1,0:T(8,128)(2,1)S(1)}, u32[]{:S(2)}, u32[]{:S(2)}) collective-permute-start(bf16[128,256]{1,0:T(8,128)(2,1)S(1)} %get-tuple-element.64), channel_id=1, source_target_pairs={{0,128},{8,136},{16,144},{24,152},{32,160},{40,168},{48,176},{56,1... | collective-permute-start | bytes 196616 | tf_op jit(solution)/shard_map/ppermute | solution.py:53
  62.3 7.9 %collective-permute-start.16 = (bf16[128,256]{1,0:T(8,128)(2,1)S(1)}, bf16[128,256]{1,0:T(8,128)(2,1)S(1)}, u32[]{:S(2)}, u32[]{:S(2)}) collective-permute-start(bf16[128,256]{1,0:T(8,128)(2,1)S(1)} %get-tuple-element.65), channel_id=1, source_target_pairs={{0,192},{8,200},{16,208},{24,216},{32,224},{40,232},{48,240},{56,2... | collective-permute-start | bytes 196616 | tf_op jit(solution)/shard_map/ppermute | solution.py:53
  65.0 9.2 %collective-permute-start.9 = (bf16[128,256]{1,0:T(8,128)(2,1)S(1)}, bf16[128,256]{1,0:T(8,128)(2,1)S(1)}, u32[]{:S(2)}, u32[]{:S(2)}) collective-permute-start(bf16[128,256]{1,0:T(8,128)(2,1)S(1)} %get-tuple-element.54.refs_7_.refs_0_), channel_id=1, source_target_pairs={{0,24},{8,32},{16,40},{24,48},{32,56},{40,0},{48,8},{56,16},{64,88... | collective-permute-start | bytes 196616 | tf_op jit(solution)/shard_map/ppermute | solution.py:53
  67.9 6.8 %collective-permute-start.8 = (bf16[128,256]{1,0:T(8,128)(2,1)S(1)}, bf16[128,256]{1,0:T(8,128)(2,1)S(1)}, u32[]{:S(2)}, u32[]{:S(2)}) collective-permute-start(bf16[128,256]{1,0:T(8,128)(2,1)S(1)} %get-tuple-element.54.refs_7_.refs_0_), channel_id=1, source_target_pairs={{0,40},{8,48},{16,56},{24,0},{32,8},{40,16},{48,24},{56,32},{64,10... | collective-permute-start | bytes 196616 | tf_op jit(solution)/shard_map/ppermute | solution.py:53
  70.5 7.4 %collective-permute-start.21 = (bf16[128,256]{1,0:T(8,128)(2,1)S(1)}, bf16[128,256]{1,0:T(8,128)(2,1)S(1)}, u32[]{:S(2)}, u32[]{:S(2)}) collective-permute-start(bf16[128,256]{1,0:T(8,128)(2,1)S(1)} %get-tuple-element.67.refs_3_.refs_0_), channel_id=1, source_target_pairs={{0,192},{8,200},{16,208},{24,216},{32,224},{40,232},{48,240},{56,2... | collective-permute-start | bytes 196616 | tf_op jit(solution)/shard_map/ppermute | solution.py:53
  73.2 5.9 %collective-permute-start.20 = (bf16[128,256]{1,0:T(8,128)(2,1)S(1)}, bf16[128,256]{1,0:T(8,128)(2,1)S(1)}, u32[]{:S(2)}, u32[]{:S(2)}) collective-permute-start(bf16[128,256]{1,0:T(8,128)(2,1)S(1)} %get-tuple-element.67.refs_3_.refs_0_), channel_id=1, source_target_pairs={{0,128},{8,136},{16,144},{24,152},{32,160},{40,168},{48,176},{56,1... | collective-permute-start | bytes 196616 | tf_op jit(solution)/shard_map/ppermute | solution.py:53
  73.2 6.2 %collective-permute-start.19 = (bf16[128,256]{1,0:T(8,128)(2,1)S(1)}, bf16[128,256]{1,0:T(8,128)(2,1)S(1)}, u32[]{:S(2)}, u32[]{:S(2)}) collective-permute-start(bf16[128,256]{1,0:T(8,128)(2,1)S(1)} %get-tuple-element.67.refs_3_.refs_0_), channel_id=1, source_target_pairs={{0,64},{8,72},{16,80},{24,88},{32,96},{40,104},{48,112},{56,120},{... | collective-permute-start | bytes 196616 | tf_op jit(solution)/shard_map/ppermute | solution.py:53
  74.8 9.8 %collective-permute-start.18 = (bf16[128,640]{1,0:T(8,128)(2,1)S(1)}, bf16[128,640]{1,0:T(8,128)(2,1)S(1)}, u32[]{:S(2)}, u32[]{:S(2)}) collective-permute-start(bf16[128,640]{1,0:T(8,128)(2,1)S(1)} %get-tuple-element.69), channel_id=1, source_target_pairs={{0,56},{8,0},{16,8},{24,16},{32,24},{40,32},{48,40},{56,48},{64,12... | collective-permute-start | bytes 491528 | tf_op jit(solution)/shard_map/ppermute | solution.py:53
  77.9 11.0 %collective-permute-start.17 = (bf16[128,640]{1,0:T(8,128)(2,1)S(1)}, bf16[128,640]{1,0:T(8,128)(2,1)S(1)}, u32[]{:S(2)}, u32[]{:S(2)}) collective-permute-start(bf16[128,640]{1,0:T(8,128)(2,1)S(1)} %get-tuple-element.68.refs_4_), channel_id=1, source_target_pairs={{0,8},{8,16},{16,24},{24,32},{32,40},{40,48},{48,56},{56,0},{64,72... | collective-permute-start | bytes 491528 | tf_op jit(solution)/shard_map/ppermute | solution.py:53
  79.4 18.8 %collective-permute-start.27 = (bf16[128,1024]{1,0:T(8,128)(2,1)S(1)}, bf16[128,1024]{1,0:T(8,128)(2,1)S(1)}, u32[]{:S(2)}, u32[]{:S(2)}) collective-permute-start(bf16[128,1024]{1,0:T(8,128)(2,1)S(1)} %join_b.1.refs_5_.refs_0_.refs_3_), channel_id=1, source_target_pairs={{0,24},{8,32},{16,40},{24,48},{32,56},{40,0},{48,8},{56,16},{64,88... | collective-permute-start | bytes 786440 | tf_op jit(solution)/shard_map/ppermute | solution.py:53
  83.5 17.2 %collective-permute-start.26 = (bf16[128,1024]{1,0:T(8,128)(2,1)S(1)}, bf16[128,1024]{1,0:T(8,128)(2,1)S(1)}, u32[]{:S(2)}, u32[]{:S(2)}) collective-permute-start(bf16[128,1024]{1,0:T(8,128)(2,1)S(1)} %join_b.1.refs_5_.refs_0_.refs_3_), channel_id=1, source_target_pairs={{0,40},{8,48},{16,56},{24,0},{32,8},{40,16},{48,24},{56,32},{64,10... | collective-permute-start | bytes 786440 | tf_op jit(solution)/shard_map/ppermute | solution.py:53
  88.9 15.1 %collective-permute-start.23 = (bf16[128,2048]{1,0:T(8,128)(2,1)S(1)}, bf16[128,2048]{1,0:T(8,128)(2,1)S(1)}, u32[]{:S(2)}, u32[]{:S(2)}) collective-permute-start(bf16[128,2048]{1,0:T(8,128)(2,1)S(1)} %join_row_a.1.refs_3_.refs_0_), channel_id=1, source_target_pairs={{0,192},{8,200},{16,208},{24,216},{32,224},{40,232},{48,240},{56,2... | collective-permute-start | bytes 1572872 | tf_op jit(solution)/shard_map/ppermute | solution.py:53
  89.9 14.1 %collective-permute-start.22 = (bf16[128,2048]{1,0:T(8,128)(2,1)S(1)}, bf16[128,2048]{1,0:T(8,128)(2,1)S(1)}, u32[]{:S(2)}, u32[]{:S(2)}) collective-permute-start(bf16[128,2048]{1,0:T(8,128)(2,1)S(1)} %join_row_a.1.refs_3_.refs_0_), channel_id=1, source_target_pairs={{0,64},{8,72},{16,80},{24,88},{32,96},{40,104},{48,112},{56,120},{... | collective-permute-start | bytes 1572872 | tf_op jit(solution)/shard_map/ppermute | solution.py:53
  100.7 12.4 %collective-permute-start.28 = (bf16[128,2560]{1,0:T(8,128)(2,1)S(1)}, bf16[128,2560]{1,0:T(8,128)(2,1)S(1)}, u32[]{:S(2)}, u32[]{:S(2)}) collective-permute-start(bf16[128,2560]{1,0:T(8,128)(2,1)S(1)} %get-tuple-element.72), channel_id=1, source_target_pairs={{0,8},{8,16},{16,24},{24,32},{32,40},{40,48},{48,56},{56,0},{64,72... | collective-permute-start | bytes 1966088 | tf_op jit(solution)/shard_map/ppermute | solution.py:53
  101.0 13.4 %collective-permute-start.29 = (bf16[128,2560]{1,0:T(8,128)(2,1)S(1)}, bf16[128,2560]{1,0:T(8,128)(2,1)S(1)}, u32[]{:S(2)}, u32[]{:S(2)}) collective-permute-start(bf16[128,2560]{1,0:T(8,128)(2,1)S(1)} %get-tuple-element.73), channel_id=1, source_target_pairs={{0,56},{8,0},{16,8},{24,16},{32,24},{40,32},{48,40},{56,48},{64,12... | collective-permute-start | bytes 1966088 | tf_op jit(solution)/shard_map/ppermute | solution.py:53
  104.1 10.3 %collective-permute-start.24 = (bf16[128,1024]{1,0:T(8,128)(2,1)S(1)}, bf16[128,1024]{1,0:T(8,128)(2,1)S(1)}, u32[]{:S(2)}, u32[]{:S(2)}) collective-permute-start(bf16[128,1024]{1,0:T(8,128)(2,1)S(1)} %get-tuple-element.70), channel_id=1, source_target_pairs={{0,64},{8,72},{16,80},{24,88},{32,96},{40,104},{48,112},{56,120},{... | collective-permute-start | bytes 786440 | tf_op jit(solution)/shard_map/ppermute | solution.py:53
  104.2 10.2 %collective-permute-start.25 = (bf16[128,1024]{1,0:T(8,128)(2,1)S(1)}, bf16[128,1024]{1,0:T(8,128)(2,1)S(1)}, u32[]{:S(2)}, u32[]{:S(2)}) collective-permute-start(bf16[128,1024]{1,0:T(8,128)(2,1)S(1)} %get-tuple-element.71), channel_id=1, source_target_pairs={{0,192},{8,200},{16,208},{24,216},{32,224},{40,232},{48,240},{56,2... | collective-permute-start | bytes 786440 | tf_op jit(solution)/shard_map/ppermute | solution.py:53

commit v5 on v4

--- a/solution.py
+++ b/solution.py
@@ -341,7 +341,7 @@
     strip = (ROWS_B, W)
     own, s1, s2, s3 = call(
         sum_z_kernel, [(strip, F32), (strip, BF), (strip, BF), (strip, BF)],
-        keep0_b, from_minus_b, from_plus_b, r3p_b, r3m_b, after=(to3p,), name="sum_b",
+        keep0_b, from_minus_b, from_plus_b, r3p_b, r3m_b, after=(plus_a,), name="sum_b",
     )
     b1, b2, b3 = shift(s1, 1, 0), shift(s2, 2, 0), shift(s3, 3, 0)
 
@@ -350,7 +350,7 @@
     )
     p3, m3 = shift(own_a, 0, -3), shift(own_a, 0, 3)
     momentum_b, own_b = update(
-        update_b_kernel, base_b, momentum[ROWS_A:], own, b1, b2, b3, after=(own_a,)
+        update_b_kernel, base_b, momentum[ROWS_A:], own, b1, b2, b3
     )
     b1, b2, b3 = [shift(own_b, e, 0) for e in (1, 2, 3)]
     plus_a, minus_a = join(
@@ -370,7 +370,7 @@
     m1, p1 = shift(row_a, 1, 0), shift(row_a, -1, 0)
     plus_b, minus_b = join(
         (((0, 0, 1024), (1, 0, 1024), (2, 0, 512)), ((0, 0, 1024), (2, 0, 1024), (1, 512, 512))),
-        row_b, p3_b, m3_b, after=(row_a,), name="join_row_b",
+        row_b, p3_b, m3_b, name="join_row_b",
     )
     from_minus_b, from_plus_b = shift(plus_b, 0, 1), shift(minus_b, 0, -1)
     low, high = join(

time: 118 us -> 118 us (level); the launches traced: 116 us -> 118 us
  waiting for transfers between devices: 42.7 us -> 44.4 us
    ppermute x30, waiting for transfers between devices: 42.7 us -> 44.4 us  [shift(): return lax.ppermute(value, 'replica', pairs)]
  transfers between devices with their start and end apart: 30 -> 30, of which waited for: 12 -> 11; matrix products, arithmetic and copies ran while one was open for 1% -> 1% of each run, Pallas kernels for 10% -> 10%
where the time goes in v5:
time: 118 us
  starting transfers between devices  55.9 us (47%)
  waiting for transfers between devices  44.4 us (38%)
  Pallas kernels  15.6 us (13%)
    ppermute x30, starting transfers between devices, shift(): return lax.ppermute(value, 'replica', pairs)  55.9 us
    ppermute x30, waiting for transfers between devices, shift(): return lax.ppermute(value, 'replica', pairs)  44.4 us
    pallas_call x4, Pallas kernels, contribute(): pl.pallas_call(functools.partial(contribute_kernel, jobs, len(after)), ou...  10.1 us
    pallas_call x2, Pallas kernels, assemble(): pl.pallas_call(functools.partial(assemble_kernel, plan), out_shape=jax.Sh...  4.02 us
  transfers between devices with their start and end apart: 30, of which 11 were waited for; matrix products, arithmetic and copies ran while one was open for 1% of the time, Pallas kernels for 10%

profile of v5, /device:TPU:16, one launch (start us, length us, event | category | flops | bytes accessed | tf_op | source)
XLA Modules:
  0.0 117.7 jit_solution(12747269132243563948)
XLA Ops:
  0.6 1.9 %contribute.6 = (bf16[128,1024]{1,0:T(8,128)(2,1)S(1)}, bf16[128,1024]{1,0:T(8,128)(2,1)S(1)}) custom-call(bf16[1,256,8192]{2,1,0:T(8,128)(2,1)} %local.7, bf16[256,8192]{1,0:T(8,128)(2,1)} %base.7), custom_call_target="tpu_custom_call" | custom-call | flops 268435456 | bytes 1572864 | tf_op jit(solution)/shard_map/contribute/pallas_call | solution.py:129
  2.5 2.8 %collective-permute-start.1 = (bf16[128,1024]{1,0:T(8,128)(2,1)S(1)}, bf16[128,1024]{1,0:T(8,128)(2,1)S(1)}, u32[]{:S(2)}, u32[]{:S(2)}) collective-permute-start(bf16[128,1024]{1,0:T(8,128)(2,1)S(1)} %get-tuple-element.43), channel_id=1, source_target_pairs={{0,192},{8,200},{16,208},{24,216},{32,224},{40,232},{48,240},{56,2... | collective-permute-start | bytes 786440 | tf_op jit(solution)/shard_map/ppermute | solution.py:53
  5.3 2.9 %contribute.7 = (bf16[128,2560]{1,0:T(8,128)(2,1)S(1)}, bf16[128,2560]{1,0:T(8,128)(2,1)S(1)}) custom-call(bf16[1,256,8192]{2,1,0:T(8,128)(2,1)} %local.7, bf16[256,8192]{1,0:T(8,128)(2,1)} %base.7, bf16[128,1024]{1,0:T(8,128)(2,1)S(1)} %get-tuple-element.42.rest_0_), custom_call_target="tpu_custom_call" | custom-call | flops 671088640 | bytes 3932160 | tf_op jit(solution)/shard_map/contribute/pallas_call | solution.py:129
  8.2 2.0 %collective-permute-start.10 = (bf16[128,2560]{1,0:T(8,128)(2,1)S(1)}, bf16[128,2560]{1,0:T(8,128)(2,1)S(1)}, u32[]{:S(2)}, u32[]{:S(2)}) collective-permute-start(bf16[128,2560]{1,0:T(8,128)(2,1)S(1)} %get-tuple-element.56), channel_id=1, source_target_pairs={{0,8},{8,16},{16,24},{24,32},{32,40},{40,48},{48,56},{56,0},{64,72... | collective-permute-start | bytes 1966088 | tf_op jit(solution)/shard_map/ppermute | solution.py:53
  10.2 4.0 %collective-permute-start.11 = (bf16[128,2560]{1,0:T(8,128)(2,1)S(1)}, bf16[128,2560]{1,0:T(8,128)(2,1)S(1)}, u32[]{:S(2)}, u32[]{:S(2)}) collective-permute-start(bf16[128,2560]{1,0:T(8,128)(2,1)S(1)} %get-tuple-element.57), channel_id=1, source_target_pairs={{0,56},{8,0},{16,8},{24,16},{32,24},{40,32},{48,40},{56,48},{64,12... | collective-permute-start | bytes 1966088 | tf_op jit(solution)/shard_map/ppermute | solution.py:53
  14.2 2.5 %contribute.5 = (bf16[128,2048]{1,0:T(8,128)(2,1)S(1)}, bf16[128,2048]{1,0:T(8,128)(2,1)S(1)}) custom-call(bf16[1,256,8192]{2,1,0:T(8,128)(2,1)} %local.7, bf16[256,8192]{1,0:T(8,128)(2,1)} %base.7), custom_call_target="tpu_custom_call" | custom-call | flops 536870912 | bytes 3145728 | tf_op jit(solution)/shard_map/contribute/pallas_call | solution.py:129
  16.9 0.8 collective-permute-start.2
  17.7 2.6 %collective-permute-start.3 = (bf16[128,2048]{1,0:T(8,128)(2,1)S(1)}, bf16[128,2048]{1,0:T(8,128)(2,1)S(1)}, u32[]{:S(2)}, u32[]{:S(2)}) collective-permute-start(bf16[128,2048]{1,0:T(8,128)(2,1)S(1)} %get-tuple-element.45), channel_id=1, source_target_pairs={{0,192},{8,200},{16,208},{24,216},{32,224},{40,232},{48,240},{56,2... | collective-permute-start | bytes 1572872 | tf_op jit(solution)/shard_map/ppermute | solution.py:53
  20.3 2.9 %contribute.4 = (bf16[128,2048]{1,0:T(8,128)(2,1)S(1)}, bf16[128,256]{1,0:T(8,128)(2,1)S(1)}, bf16[128,1024]{1,0:T(8,128)(2,1)S(1)}, bf16[128,1024]{1,0:T(8,128)...) custom-call(bf16[1,256,8192]{2,1,0:T(8,128)(2,1)} %local.7, bf16[256,8192]{1,0:T(8,128)(2,1)} %base.7), custom_call_target="tpu_custom_call" | custom-call | flops 671088640 | bytes 3932160 | tf_op jit(solution)/shard_map/contribute/pallas_call | solution.py:129
  23.2 5.4 %collective-permute-done.10.refs_2_.refs_1_ = bf16[128,2560]{1,0:T(8,128)(2,1)S(1)} collective-permute-done((bf16[128,2560]{1,0:T(8,128)(2,1)S(1)}, bf16[128,2560]{1,0:T(8,128)(2,1)S(1)}, u32[]{:S(2)}, u32[]{:S(2)}) %collective-permute-start.10) | collective-permute-done | bytes 655392 | tf_op jit(solution)/shard_map/ppermute | solution.py:53
  28.6 0.2 relay_b.1
  28.8 4.6 %collective-permute-start.12 = (bf16[128,1024]{1,0:T(8,128)(2,1)S(1)}, bf16[128,1024]{1,0:T(8,128)(2,1)S(1)}, u32[]{:S(2)}, u32[]{:S(2)}) collective-permute-start(bf16[128,1024]{1,0:T(8,128)(2,1)S(1)} %get-tuple-element.60), channel_id=1, source_target_pairs={{0,24},{8,32},{16,40},{24,48},{32,56},{40,0},{48,8},{56,16},{64,88... | collective-permute-start | bytes 786440 | tf_op jit(solution)/shard_map/ppermute | solution.py:53
  33.4 0.5 collective-permute-start.13
  33.9 0.2 sum_a.1
  34.1 1.9 %collective-permute-start.5 = (bf16[128,640]{1,0:T(8,128)(2,1)S(1)}, bf16[128,640]{1,0:T(8,128)(2,1)S(1)}, u32[]{:S(2)}, u32[]{:S(2)}) collective-permute-start(bf16[128,640]{1,0:T(8,128)(2,1)S(1)} %get-tuple-element.48), channel_id=1, source_target_pairs={{0,56},{8,0},{16,8},{24,16},{32,24},{40,32},{48,40},{56,48},{64,12... | collective-permute-start | bytes 491528 | tf_op jit(solution)/shard_map/ppermute | solution.py:53
  36.0 0.2 collective-permute-start.4
  36.2 14.9 %collective-permute-done.12.refs_3_ = bf16[128,1024]{1,0:T(8,128)(2,1)S(1)} collective-permute-done((bf16[128,1024]{1,0:T(8,128)(2,1)S(1)}, bf16[128,1024]{1,0:T(8,128)(2,1)S(1)}, u32[]{:S(2)}, u32[]{:S(2)}) %collective-permute-start.12) | collective-permute-done | bytes 262176 | tf_op jit(solution)/shard_map/ppermute | solution.py:53
  51.0 3.5 %collective-permute-done.13.refs_4_ = bf16[128,1024]{1,0:T(8,128)(2,1)S(1)} collective-permute-done((bf16[128,1024]{1,0:T(8,128)(2,1)S(1)}, bf16[128,1024]{1,0:T(8,128)(2,1)S(1)}, u32[]{:S(2)}, u32[]{:S(2)}) %collective-permute-start.13) | collective-permute-done | bytes 262176 | tf_op jit(solution)/shard_map/ppermute | solution.py:53
  54.5 0.2 sum_b.1
  54.7 0.3 collective-permute-start.14
  55.0 3.9 %collective-permute-start.15 = (bf16[128,256]{1,0:T(8,128)(2,1)S(1)}, bf16[128,256]{1,0:T(8,128)(2,1)S(1)}, u32[]{:S(2)}, u32[]{:S(2)}) collective-permute-start(bf16[128,256]{1,0:T(8,128)(2,1)S(1)} %get-tuple-element.64), channel_id=1, source_target_pairs={{0,128},{8,136},{16,144},{24,152},{32,160},{40,168},{48,176},{56,1... | collective-permute-start | bytes 196616 | tf_op jit(solution)/shard_map/ppermute | solution.py:53
  59.0 0.2 collective-permute-start.16
  59.2 2.1 %collective-permute-start.6 = (bf16[128,256]{1,0:T(8,128)(2,1)S(1)}, bf16[128,256]{1,0:T(8,128)(2,1)S(1)}, u32[]{:S(2)}, u32[]{:S(2)}) collective-permute-start(bf16[128,256]{1,0:T(8,128)(2,1)S(1)} %get-tuple-element.51), channel_id=1, source_target_pairs={{0,24},{8,32},{16,40},{24,48},{32,56},{40,0},{48,8},{56,16},{64,88... | collective-permute-start | bytes 196616 | tf_op jit(solution)/shard_map/ppermute | solution.py:53
  61.2 3.1 %collective-permute-start.7 = (bf16[128,256]{1,0:T(8,128)(2,1)S(1)}, bf16[128,256]{1,0:T(8,128)(2,1)S(1)}, u32[]{:S(2)}, u32[]{:S(2)}) collective-permute-start(bf16[128,256]{1,0:T(8,128)(2,1)S(1)} %get-tuple-element.52), channel_id=1, source_target_pairs={{0,40},{8,48},{16,56},{24,0},{32,8},{40,16},{48,24},{56,32},{64,10... | collective-permute-start | bytes 196616 | tf_op jit(solution)/shard_map/ppermute | solution.py:53
  64.3 2.3 %collective-permute-done.6.refs_3_ = bf16[128,256]{1,0:T(8,128)(2,1)S(1)} collective-permute-done((bf16[128,256]{1,0:T(8,128)(2,1)S(1)}, bf16[128,256]{1,0:T(8,128)(2,1)S(1)}, u32[]{:S(2)}, u32[]{:S(2)}) %collective-permute-start.6) | collective-permute-done | bytes 65568 | tf_op jit(solution)/shard_map/ppermute | solution.py:53
  66.7 2.0 %collective-permute-done.7.refs_4_ = bf16[128,256]{1,0:T(8,128)(2,1)S(1)} collective-permute-done((bf16[128,256]{1,0:T(8,128)(2,1)S(1)}, bf16[128,256]{1,0:T(8,128)(2,1)S(1)}, u32[]{:S(2)}, u32[]{:S(2)}) %collective-permute-start.7) | collective-permute-done | bytes 65568 | tf_op jit(solution)/shard_map/ppermute | solution.py:53
  68.7 0.3 update.2
  69.0 0.8 collective-permute-start.9
  69.8 4.3 %collective-permute-start.8 = (bf16[128,256]{1,0:T(8,128)(2,1)S(1)}, bf16[128,256]{1,0:T(8,128)(2,1)S(1)}, u32[]{:S(2)}, u32[]{:S(2)}) collective-permute-start(bf16[128,256]{1,0:T(8,128)(2,1)S(1)} %get-tuple-element.54.refs_0_), channel_id=1, source_target_pairs={{0,40},{8,48},{16,56},{24,0},{32,8},{40,16},{48,24},{56,32},{64,10... | collective-permute-start | bytes 196616 | tf_op jit(solution)/shard_map/ppermute | solution.py:53
  74.1 0.3 update.3
  74.5 3.7 %collective-permute-start.20 = (bf16[128,256]{1,0:T(8,128)(2,1)S(1)}, bf16[128,256]{1,0:T(8,128)(2,1)S(1)}, u32[]{:S(2)}, u32[]{:S(2)}) collective-permute-start(bf16[128,256]{1,0:T(8,128)(2,1)S(1)} %get-tuple-element.67.refs_3_.refs_0_), channel_id=1, source_target_pairs={{0,128},{8,136},{16,144},{24,152},{32,160},{40,168},{48,176},{56,1... | collective-permute-start | bytes 196616 | tf_op jit(solution)/shard_map/ppermute | solution.py:53
  78.3 2.7 %collective-permute-start.18 = (bf16[128,640]{1,0:T(8,128)(2,1)S(1)}, bf16[128,640]{1,0:T(8,128)(2,1)S(1)}, u32[]{:S(2)}, u32[]{:S(2)}) collective-permute-start(bf16[128,640]{1,0:T(8,128)(2,1)S(1)} %get-tuple-element.69), channel_id=1, source_target_pairs={{0,56},{8,0},{16,8},{24,16},{32,24},{40,32},{48,40},{56,48},{64,12... | collective-permute-start | bytes 491528 | tf_op jit(solution)/shard_map/ppermute | solution.py:53
  81.0 2.7 %collective-permute-done.19.refs_1_ = bf16[128,256]{1,0:T(8,128)(2,1)S(1)} collective-permute-done((bf16[128,256]{1,0:T(8,128)(2,1)S(1)}, bf16[128,256]{1,0:T(8,128)(2,1)S(1)}, u32[]{:S(2)}, u32[]{:S(2)}) %collective-permute-start.19) | collective-permute-done | bytes 65568 | tf_op jit(solution)/shard_map/ppermute | solution.py:53
  83.8 5.0 %collective-permute-start.26 = (bf16[128,1024]{1,0:T(8,128)(2,1)S(1)}, bf16[128,1024]{1,0:T(8,128)(2,1)S(1)}, u32[]{:S(2)}, u32[]{:S(2)}) collective-permute-start(bf16[128,1024]{1,0:T(8,128)(2,1)S(1)} %join_b.1.refs_5_.refs_0_.refs_3_), channel_id=1, source_target_pairs={{0,40},{8,48},{16,56},{24,0},{32,8},{40,16},{48,24},{56,32},{64,10... | collective-permute-start | bytes 786440 | tf_op jit(solution)/shard_map/ppermute | solution.py:53
  88.9 1.1 collective-permute-done.18.refs_4_
  89.9 1.0 collective-permute-done.17.refs_3_
  90.9 0.9 collective-permute-start.23
  91.8 1.4 %collective-permute-start.22 = (bf16[128,2048]{1,0:T(8,128)(2,1)S(1)}, bf16[128,2048]{1,0:T(8,128)(2,1)S(1)}, u32[]{:S(2)}, u32[]{:S(2)}) collective-permute-start(bf16[128,2048]{1,0:T(8,128)(2,1)S(1)} %join_row_a.1.refs_0_), channel_id=1, source_target_pairs={{0,64},{8,72},{16,80},{24,88},{32,96},{40,104},{48,112},{56,120},{... | collective-permute-start | bytes 1572872 | tf_op jit(solution)/shard_map/ppermute | solution.py:53
  93.3 6.0 %collective-permute-done.27.refs_2_.refs_5_ = bf16[128,1024]{1,0:T(8,128)(2,1)S(1)} collective-permute-done((bf16[128,1024]{1,0:T(8,128)(2,1)S(1)}, bf16[128,1024]{1,0:T(8,128)(2,1)S(1)}, u32[]{:S(2)}, u32[]{:S(2)}) %collective-permute-start.27) | collective-permute-done | bytes 262176 | tf_op jit(solution)/shard_map/ppermute | solution.py:53
  99.3 0.3 collective-permute-done.26.refs_1_.refs_4_
  99.7 1.9 %collective-permute-start.28 = (bf16[128,2560]{1,0:T(8,128)(2,1)S(1)}, bf16[128,2560]{1,0:T(8,128)(2,1)S(1)}, u32[]{:S(2)}, u32[]{:S(2)}) collective-permute-start(bf16[128,2560]{1,0:T(8,128)(2,1)S(1)} %get-tuple-element.72), channel_id=1, source_target_pairs={{0,8},{8,16},{16,24},{24,32},{32,40},{40,48},{48,56},{56,0},{64,72... | collective-permute-start | bytes 1966088 | tf_op jit(solution)/shard_map/ppermute | solution.py:53
  101.5 2.6 %collective-permute-start.29 = (bf16[128,2560]{1,0:T(8,128)(2,1)S(1)}, bf16[128,2560]{1,0:T(8,128)(2,1)S(1)}, u32[]{:S(2)}, u32[]{:S(2)}) collective-permute-start(bf16[128,2560]{1,0:T(8,128)(2,1)S(1)} %get-tuple-element.73), channel_id=1, source_target_pairs={{0,56},{8,0},{16,8},{24,16},{32,24},{40,32},{48,40},{56,48},{64,12... | collective-permute-start | bytes 1966088 | tf_op jit(solution)/shard_map/ppermute | solution.py:53
  104.2 2.3 %collective-permute-start.24 = (bf16[128,1024]{1,0:T(8,128)(2,1)S(1)}, bf16[128,1024]{1,0:T(8,128)(2,1)S(1)}, u32[]{:S(2)}, u32[]{:S(2)}) collective-permute-start(bf16[128,1024]{1,0:T(8,128)(2,1)S(1)} %get-tuple-element.70), channel_id=1, source_target_pairs={{0,64},{8,72},{16,80},{24,88},{32,96},{40,104},{48,112},{56,120},{... | collective-permute-start | bytes 786440 | tf_op jit(solution)/shard_map/ppermute | solution.py:53
  106.5 1.0 collective-permute-start.25
  107.5 0.7 pad_maximum_fusion
  108.2 2.1 %assemble.2.refs_4_ = bf16[256,8192]{1,0:T(8,128)(2,1)} custom-call(bf16[128,2048]{1,0:T(8,128)(2,1)S(1)} %join_row_a.1.refs_0_, bf16[128,2048]{1,0:T(8,128)(2,1)S(1)} %collective-permute-done.22.refs_0_.refs_1_, bf16[128,2048]{1,0:T(8,128)(2,1)S(1)} %collective-permute-done.23.refs_1_.refs_2_, bf16[128,1024]{1,0:T(8,128)(2,1)S(1)} %join_b.1.refs_5_.refs_0_.refs_3_, ...), custom_call_target="tpu_custom_call" | custom-call | bytes 4194304 | tf_op jit(solution)/shard_map/assemble/pallas_call | solution.py:284
  110.3 5.3 %collective-permute-done.28.refs_2_ = bf16[128,2560]{1,0:T(8,128)(2,1)S(1)} collective-permute-done((bf16[128,2560]{1,0:T(8,128)(2,1)S(1)}, bf16[128,2560]{1,0:T(8,128)(2,1)S(1)}, u32[]{:S(2)}, u32[]{:S(2)}) %collective-permute-start.28) | collective-permute-done | bytes 655392 | tf_op jit(solution)/shard_map/ppermute | solution.py:53
  115.6 1.9 %assemble.3 = bf16[256,8192]{1,0:T(8,128)(2,1)} custom-call(bf16[128,1024]{1,0:T(8,128)(2,1)S(1)} %collective-permute-done.24.refs_0_, bf16[128,1024]{1,0:T(8,128)(2,1)S(1)} %collective-permute-done.25.refs_1_, bf16[128,2560]{1,0:T(8,128)(2,1)S(1)} %collective-permute-done.28.refs_2_, ...), custom_call_target="tpu_custom_call", output_to_operand_aliasing={{}: (4, {})} | custom-call | bytes 4194304 | tf_op jit(solution)/shard_map/assemble/pallas_call | solution.py:284
  (36 shorter events, 0.6 us)
Async XLA Ops:
  2.5 14.2 %collective-permute-start.1 = (bf16[128,1024]{1,0:T(8,128)(2,1)S(1)}, bf16[128,1024]{1,0:T(8,128)(2,1)S(1)}, u32[]{:S(2)}, u32[]{:S(2)}) collective-permute-start(bf16[128,1024]{1,0:T(8,128)(2,1)S(1)} %get-tuple-element.43), channel_id=1, source_target_pairs={{0,192},{8,200},{16,208},{24,216},{32,224},{40,232},{48,240},{56,2... | collective-permute-start | bytes 786440 | tf_op jit(solution)/shard_map/ppermute | solution.py:53
  5.3 11.4 %collective-permute-start = (bf16[128,1024]{1,0:T(8,128)(2,1)S(1)}, bf16[128,1024]{1,0:T(8,128)(2,1)S(1)}, u32[]{:S(2)}, u32[]{:S(2)}) collective-permute-start(bf16[128,1024]{1,0:T(8,128)(2,1)S(1)} %get-tuple-element.42.rest_0_), channel_id=1, source_target_pairs={{0,64},{8,72},{16,80},{24,88},{32,96},{40,104},{48,112},{56,120},{... | collective-permute-start | bytes 786440 | tf_op jit(solution)/shard_map/ppermute | solution.py:53
  8.2 20.4 %collective-permute-start.10 = (bf16[128,2560]{1,0:T(8,128)(2,1)S(1)}, bf16[128,2560]{1,0:T(8,128)(2,1)S(1)}, u32[]{:S(2)}, u32[]{:S(2)}) collective-permute-start(bf16[128,2560]{1,0:T(8,128)(2,1)S(1)} %get-tuple-element.56), channel_id=1, source_target_pairs={{0,8},{8,16},{16,24},{24,32},{32,40},{40,48},{48,56},{56,0},{64,72... | collective-permute-start | bytes 1966088 | tf_op jit(solution)/shard_map/ppermute | solution.py:53
  10.2 18.4 %collective-permute-start.11 = (bf16[128,2560]{1,0:T(8,128)(2,1)S(1)}, bf16[128,2560]{1,0:T(8,128)(2,1)S(1)}, u32[]{:S(2)}, u32[]{:S(2)}) collective-permute-start(bf16[128,2560]{1,0:T(8,128)(2,1)S(1)} %get-tuple-element.57), channel_id=1, source_target_pairs={{0,56},{8,0},{16,8},{24,16},{32,24},{40,32},{48,40},{56,48},{64,12... | collective-permute-start | bytes 1966088 | tf_op jit(solution)/shard_map/ppermute | solution.py:53
  16.9 17.0 %collective-permute-start.2 = (bf16[128,2048]{1,0:T(8,128)(2,1)S(1)}, bf16[128,2048]{1,0:T(8,128)(2,1)S(1)}, u32[]{:S(2)}, u32[]{:S(2)}) collective-permute-start(bf16[128,2048]{1,0:T(8,128)(2,1)S(1)} %get-tuple-element.44), channel_id=1, source_target_pairs={{0,64},{8,72},{16,80},{24,88},{32,96},{40,104},{48,112},{56,120},{... | collective-permute-start | bytes 1572872 | tf_op jit(solution)/shard_map/ppermute | solution.py:53
  17.7 16.2 %collective-permute-start.3 = (bf16[128,2048]{1,0:T(8,128)(2,1)S(1)}, bf16[128,2048]{1,0:T(8,128)(2,1)S(1)}, u32[]{:S(2)}, u32[]{:S(2)}) collective-permute-start(bf16[128,2048]{1,0:T(8,128)(2,1)S(1)} %get-tuple-element.45), channel_id=1, source_target_pairs={{0,192},{8,200},{16,208},{24,216},{32,224},{40,232},{48,240},{56,2... | collective-permute-start | bytes 1572872 | tf_op jit(solution)/shard_map/ppermute | solution.py:53
  23.2 41.1 %copy-start.1 = (f32[256,256]{1,0:T(8,128)S(1)}, f32[256,256]{1,0:T(8,128)}, u32[]{:S(2)}) copy-start(f32[256,256]{1,0:T(8,128)} %param.7) | copy-start | bytes 786436
  23.2 45.5 %copy-start = (f32[128,128]{1,0:T(8,128)S(1)}, f32[128,128]{1,0:T(8,128)}, u32[]{:S(2)}) copy-start(f32[128,128]{1,0:T(8,128)} %constant.2.clone.refs_7_.refs_6_) | copy-start | bytes 196612
  28.8 22.3 %collective-permute-start.12 = (bf16[128,1024]{1,0:T(8,128)(2,1)S(1)}, bf16[128,1024]{1,0:T(8,128)(2,1)S(1)}, u32[]{:S(2)}, u32[]{:S(2)}) collective-permute-start(bf16[128,1024]{1,0:T(8,128)(2,1)S(1)} %get-tuple-element.60), channel_id=1, source_target_pairs={{0,24},{8,32},{16,40},{24,48},{32,56},{40,0},{48,8},{56,16},{64,88... | collective-permute-start | bytes 786440 | tf_op jit(solution)/shard_map/ppermute | solution.py:53
  33.4 21.1 %collective-permute-start.13 = (bf16[128,1024]{1,0:T(8,128)(2,1)S(1)}, bf16[128,1024]{1,0:T(8,128)(2,1)S(1)}, u32[]{:S(2)}, u32[]{:S(2)}) collective-permute-start(bf16[128,1024]{1,0:T(8,128)(2,1)S(1)} %get-tuple-element.61), channel_id=1, source_target_pairs={{0,40},{8,48},{16,56},{24,0},{32,8},{40,16},{48,24},{56,32},{64,10... | collective-permute-start | bytes 786440 | tf_op jit(solution)/shard_map/ppermute | solution.py:53
  34.1 25.1 %collective-permute-start.5 = (bf16[128,640]{1,0:T(8,128)(2,1)S(1)}, bf16[128,640]{1,0:T(8,128)(2,1)S(1)}, u32[]{:S(2)}, u32[]{:S(2)}) collective-permute-start(bf16[128,640]{1,0:T(8,128)(2,1)S(1)} %get-tuple-element.48), channel_id=1, source_target_pairs={{0,56},{8,0},{16,8},{24,16},{32,24},{40,32},{48,40},{56,48},{64,12... | collective-permute-start | bytes 491528 | tf_op jit(solution)/shard_map/ppermute | solution.py:53
  36.0 23.2 %collective-permute-start.4 = (bf16[128,640]{1,0:T(8,128)(2,1)S(1)}, bf16[128,640]{1,0:T(8,128)(2,1)S(1)}, u32[]{:S(2)}, u32[]{:S(2)}) collective-permute-start(bf16[128,640]{1,0:T(8,128)(2,1)S(1)} %get-tuple-element.47.refs_5_), channel_id=1, source_target_pairs={{0,8},{8,16},{16,24},{24,32},{32,40},{40,48},{48,56},{56,0},{64,72... | collective-permute-start | bytes 491528 | tf_op jit(solution)/shard_map/ppermute | solution.py:53
  54.7 19.4 %collective-permute-start.14 = (bf16[128,256]{1,0:T(8,128)(2,1)S(1)}, bf16[128,256]{1,0:T(8,128)(2,1)S(1)}, u32[]{:S(2)}, u32[]{:S(2)}) collective-permute-start(bf16[128,256]{1,0:T(8,128)(2,1)S(1)} %get-tuple-element.63), channel_id=1, source_target_pairs={{0,64},{8,72},{16,80},{24,88},{32,96},{40,104},{48,112},{56,120},{... | collective-permute-start | bytes 196616 | tf_op jit(solution)/shard_map/ppermute | solution.py:53
  55.0 19.1 %collective-permute-start.15 = (bf16[128,256]{1,0:T(8,128)(2,1)S(1)}, bf16[128,256]{1,0:T(8,128)(2,1)S(1)}, u32[]{:S(2)}, u32[]{:S(2)}) collective-permute-start(bf16[128,256]{1,0:T(8,128)(2,1)S(1)} %get-tuple-element.64), channel_id=1, source_target_pairs={{0,128},{8,136},{16,144},{24,152},{32,160},{40,168},{48,176},{56,1... | collective-permute-start | bytes 196616 | tf_op jit(solution)/shard_map/ppermute | solution.py:53
  59.0 15.2 %collective-permute-start.16 = (bf16[128,256]{1,0:T(8,128)(2,1)S(1)}, bf16[128,256]{1,0:T(8,128)(2,1)S(1)}, u32[]{:S(2)}, u32[]{:S(2)}) collective-permute-start(bf16[128,256]{1,0:T(8,128)(2,1)S(1)} %get-tuple-element.65), channel_id=1, source_target_pairs={{0,192},{8,200},{16,208},{24,216},{32,224},{40,232},{48,240},{56,2... | collective-permute-start | bytes 196616 | tf_op jit(solution)/shard_map/ppermute | solution.py:53
  59.2 7.5 %collective-permute-start.6 = (bf16[128,256]{1,0:T(8,128)(2,1)S(1)}, bf16[128,256]{1,0:T(8,128)(2,1)S(1)}, u32[]{:S(2)}, u32[]{:S(2)}) collective-permute-start(bf16[128,256]{1,0:T(8,128)(2,1)S(1)} %get-tuple-element.51), channel_id=1, source_target_pairs={{0,24},{8,32},{16,40},{24,48},{32,56},{40,0},{48,8},{56,16},{64,88... | collective-permute-start | bytes 196616 | tf_op jit(solution)/shard_map/ppermute | solution.py:53
  61.2 7.4 %collective-permute-start.7 = (bf16[128,256]{1,0:T(8,128)(2,1)S(1)}, bf16[128,256]{1,0:T(8,128)(2,1)S(1)}, u32[]{:S(2)}, u32[]{:S(2)}) collective-permute-start(bf16[128,256]{1,0:T(8,128)(2,1)S(1)} %get-tuple-element.52), channel_id=1, source_target_pairs={{0,40},{8,48},{16,56},{24,0},{32,8},{40,16},{48,24},{56,32},{64,10... | collective-permute-start | bytes 196616 | tf_op jit(solution)/shard_map/ppermute | solution.py:53
  69.0 9.2 %collective-permute-start.9 = (bf16[128,256]{1,0:T(8,128)(2,1)S(1)}, bf16[128,256]{1,0:T(8,128)(2,1)S(1)}, u32[]{:S(2)}, u32[]{:S(2)}) collective-permute-start(bf16[128,256]{1,0:T(8,128)(2,1)S(1)} %get-tuple-element.54.refs_0_), channel_id=1, source_target_pairs={{0,24},{8,32},{16,40},{24,48},{32,56},{40,0},{48,8},{56,16},{64,88... | collective-permute-start | bytes 196616 | tf_op jit(solution)/shard_map/ppermute | solution.py:53
  69.8 8.5 %collective-permute-start.8 = (bf16[128,256]{1,0:T(8,128)(2,1)S(1)}, bf16[128,256]{1,0:T(8,128)(2,1)S(1)}, u32[]{:S(2)}, u32[]{:S(2)}) collective-permute-start(bf16[128,256]{1,0:T(8,128)(2,1)S(1)} %get-tuple-element.54.refs_0_), channel_id=1, source_target_pairs={{0,40},{8,48},{16,56},{24,0},{32,8},{40,16},{48,24},{56,32},{64,10... | collective-permute-start | bytes 196616 | tf_op jit(solution)/shard_map/ppermute | solution.py:53
  74.4 6.6 %collective-permute-start.21 = (bf16[128,256]{1,0:T(8,128)(2,1)S(1)}, bf16[128,256]{1,0:T(8,128)(2,1)S(1)}, u32[]{:S(2)}, u32[]{:S(2)}) collective-permute-start(bf16[128,256]{1,0:T(8,128)(2,1)S(1)} %get-tuple-element.67.refs_3_.refs_0_), channel_id=1, source_target_pairs={{0,192},{8,200},{16,208},{24,216},{32,224},{40,232},{48,240},{56,2... | collective-permute-start | bytes 196616 | tf_op jit(solution)/shard_map/ppermute | solution.py:53
  74.5 6.5 %collective-permute-start.20 = (bf16[128,256]{1,0:T(8,128)(2,1)S(1)}, bf16[128,256]{1,0:T(8,128)(2,1)S(1)}, u32[]{:S(2)}, u32[]{:S(2)}) collective-permute-start(bf16[128,256]{1,0:T(8,128)(2,1)S(1)} %get-tuple-element.67.refs_3_.refs_0_), channel_id=1, source_target_pairs={{0,128},{8,136},{16,144},{24,152},{32,160},{40,168},{48,176},{56,1... | collective-permute-start | bytes 196616 | tf_op jit(solution)/shard_map/ppermute | solution.py:53
  78.2 5.5 %collective-permute-start.19 = (bf16[128,256]{1,0:T(8,128)(2,1)S(1)}, bf16[128,256]{1,0:T(8,128)(2,1)S(1)}, u32[]{:S(2)}, u32[]{:S(2)}) collective-permute-start(bf16[128,256]{1,0:T(8,128)(2,1)S(1)} %get-tuple-element.67.refs_3_.refs_0_), channel_id=1, source_target_pairs={{0,64},{8,72},{16,80},{24,88},{32,96},{40,104},{48,112},{56,120},{... | collective-permute-start | bytes 196616 | tf_op jit(solution)/shard_map/ppermute | solution.py:53
  78.3 11.6 %collective-permute-start.18 = (bf16[128,640]{1,0:T(8,128)(2,1)S(1)}, bf16[128,640]{1,0:T(8,128)(2,1)S(1)}, u32[]{:S(2)}, u32[]{:S(2)}) collective-permute-start(bf16[128,640]{1,0:T(8,128)(2,1)S(1)} %get-tuple-element.69), channel_id=1, source_target_pairs={{0,56},{8,0},{16,8},{24,16},{32,24},{40,32},{48,40},{56,48},{64,12... | collective-permute-start | bytes 491528 | tf_op jit(solution)/shard_map/ppermute | solution.py:53
  81.0 9.8 %collective-permute-start.17 = (bf16[128,640]{1,0:T(8,128)(2,1)S(1)}, bf16[128,640]{1,0:T(8,128)(2,1)S(1)}, u32[]{:S(2)}, u32[]{:S(2)}) collective-permute-start(bf16[128,640]{1,0:T(8,128)(2,1)S(1)} %get-tuple-element.68.refs_4_), channel_id=1, source_target_pairs={{0,8},{8,16},{16,24},{24,32},{32,40},{40,48},{48,56},{56,0},{64,72... | collective-permute-start | bytes 491528 | tf_op jit(solution)/shard_map/ppermute | solution.py:53
  83.7 15.5 %collective-permute-start.27 = (bf16[128,1024]{1,0:T(8,128)(2,1)S(1)}, bf16[128,1024]{1,0:T(8,128)(2,1)S(1)}, u32[]{:S(2)}, u32[]{:S(2)}) collective-permute-start(bf16[128,1024]{1,0:T(8,128)(2,1)S(1)} %join_b.1.refs_5_.refs_0_.refs_3_), channel_id=1, source_target_pairs={{0,24},{8,32},{16,40},{24,48},{32,56},{40,0},{48,8},{56,16},{64,88... | collective-permute-start | bytes 786440 | tf_op jit(solution)/shard_map/ppermute | solution.py:53
  83.8 15.7 %collective-permute-start.26 = (bf16[128,1024]{1,0:T(8,128)(2,1)S(1)}, bf16[128,1024]{1,0:T(8,128)(2,1)S(1)}, u32[]{:S(2)}, u32[]{:S(2)}) collective-permute-start(bf16[128,1024]{1,0:T(8,128)(2,1)S(1)} %join_b.1.refs_5_.refs_0_.refs_3_), channel_id=1, source_target_pairs={{0,40},{8,48},{16,56},{24,0},{32,8},{40,16},{48,24},{56,32},{64,10... | collective-permute-start | bytes 786440 | tf_op jit(solution)/shard_map/ppermute | solution.py:53
  90.9 13.2 %collective-permute-start.23 = (bf16[128,2048]{1,0:T(8,128)(2,1)S(1)}, bf16[128,2048]{1,0:T(8,128)(2,1)S(1)}, u32[]{:S(2)}, u32[]{:S(2)}) collective-permute-start(bf16[128,2048]{1,0:T(8,128)(2,1)S(1)} %join_row_a.1.refs_0_), channel_id=1, source_target_pairs={{0,192},{8,200},{16,208},{24,216},{32,224},{40,232},{48,240},{56,2... | collective-permute-start | bytes 1572872 | tf_op jit(solution)/shard_map/ppermute | solution.py:53
  91.8 12.3 %collective-permute-start.22 = (bf16[128,2048]{1,0:T(8,128)(2,1)S(1)}, bf16[128,2048]{1,0:T(8,128)(2,1)S(1)}, u32[]{:S(2)}, u32[]{:S(2)}) collective-permute-start(bf16[128,2048]{1,0:T(8,128)(2,1)S(1)} %join_row_a.1.refs_0_), channel_id=1, source_target_pairs={{0,64},{8,72},{16,80},{24,88},{32,96},{40,104},{48,112},{56,120},{... | collective-permute-start | bytes 1572872 | tf_op jit(solution)/shard_map/ppermute | solution.py:53
  99.7 15.9 %collective-permute-start.28 = (bf16[128,2560]{1,0:T(8,128)(2,1)S(1)}, bf16[128,2560]{1,0:T(8,128)(2,1)S(1)}, u32[]{:S(2)}, u32[]{:S(2)}) collective-permute-start(bf16[128,2560]{1,0:T(8,128)(2,1)S(1)} %get-tuple-element.72), channel_id=1, source_target_pairs={{0,8},{8,16},{16,24},{24,32},{32,40},{40,48},{48,56},{56,0},{64,72... | collective-permute-start | bytes 1966088 | tf_op jit(solution)/shard_map/ppermute | solution.py:53
  101.5 14.1 %collective-permute-start.29 = (bf16[128,2560]{1,0:T(8,128)(2,1)S(1)}, bf16[128,2560]{1,0:T(8,128)(2,1)S(1)}, u32[]{:S(2)}, u32[]{:S(2)}) collective-permute-start(bf16[128,2560]{1,0:T(8,128)(2,1)S(1)} %get-tuple-element.73), channel_id=1, source_target_pairs={{0,56},{8,0},{16,8},{24,16},{32,24},{40,32},{48,40},{56,48},{64,12... | collective-permute-start | bytes 1966088 | tf_op jit(solution)/shard_map/ppermute | solution.py:53
  104.2 11.4 %collective-permute-start.24 = (bf16[128,1024]{1,0:T(8,128)(2,1)S(1)}, bf16[128,1024]{1,0:T(8,128)(2,1)S(1)}, u32[]{:S(2)}, u32[]{:S(2)}) collective-permute-start(bf16[128,1024]{1,0:T(8,128)(2,1)S(1)} %get-tuple-element.70), channel_id=1, source_target_pairs={{0,64},{8,72},{16,80},{24,88},{32,96},{40,104},{48,112},{56,120},{... | collective-permute-start | bytes 786440 | tf_op jit(solution)/shard_map/ppermute | solution.py:53
  106.5 9.1 %collective-permute-start.25 = (bf16[128,1024]{1,0:T(8,128)(2,1)S(1)}, bf16[128,1024]{1,0:T(8,128)(2,1)S(1)}, u32[]{:S(2)}, u32[]{:S(2)}) collective-permute-start(bf16[128,1024]{1,0:T(8,128)(2,1)S(1)} %get-tuple-element.71), channel_id=1, source_target_pairs={{0,192},{8,200},{16,208},{24,216},{32,224},{40,232},{48,240},{56,2... | collective-permute-start | bytes 786440 | tf_op jit(solution)/shard_map/ppermute | solution.py:53
